TPU v7x, 32 devices: a whole 2x2x4 slice. The times are simulated.
32 devices in a mesh: groups: 2 (over y), ctx: 4 (over z), head: 2 (over x), sub: 2 (over core).
Axes of the slice: x: 2, y: 2, z: 4, core: 2. Of those that a mesh axis runs over, the one named last changes fastest.
Arguments:
- query_nope: bfloat16 [4, 4, 128, 128], P(('groups', 'sub'), None, 'head'), parts along dimension 0, may hold values from -6 to 6
- query_rope: bfloat16 [4, 4, 128, 64], P(('groups', 'sub'), None, 'head'), parts along dimension 0, may hold values from -8 to 8
- latent_cache: bfloat16 [4, 16384, 576], P(('groups', 'sub'), 'ctx'), parts along dimension 0, may hold values from -12 to 12
- lengths: int32 [4], P(('groups', 'sub')), parts along dimension 0, may hold values from 2052 to 16384, as said below
- block_ids: int32 [4, 4, 32], P(('groups', 'sub')), parts along dimension 0, may hold values from 0 to 255, as said below
- key_absorb: bfloat16 [128, 128, 512], P('head', None, 'ctx'), may hold values from -0.5 to 0.5
- value_absorb: bfloat16 [128, 512, 128], P('head', 'ctx'), may hold values from -0.25 to 0.25
- output_weight: bfloat16 [16384, 7168], P('head', 'ctx'), may hold values from -0.375 to 0.375
Outputs:
- attended: bfloat16 [4, 4, 7168], P(('groups', 'sub'), None, ('ctx', 'head')), parts along dimension 0
There are 2 independent parts, one for each index of `groups`. A program takes and returns all parts, laid end to end along the dimension named above; an argument that names none is the same for every part. Nothing has to cross between parts.
Inputs may be any that keep to these rules, and one draw needn't show every extreme that they name: `lengths`: every request with the greatest length 16384 exists in each draw. `block_ids`: the 32 ids of one query token are distinct, and each block holds a position p <= lengths[r] - 4; the block of position lengths[r] - 4 is always among them.
All inputs are finite; a program needn't handle non-finite values.
Results may differ from a plain program's by a relative error of at most 0.03.
Values may be sent and summed in bfloat16 or wider, within the bound.
No kernel may reach another device: no remote copies, remote signals or barrier semaphores. Data moves between devices by JAX's collectives and lax.ppermute only.
A program may use at most 128 MiB of HBM per device.

v0:
```python
import jax
import jax.numpy as jnp
from jax import lax
from jax.sharding import PartitionSpec as P

BLK = 64


def joined(shard, axis, combine):
    everything = jax.tree.map(
        lambda part, kind: lax.all_gather(part.astype(kind), axis),
        shard,
        (jnp.bfloat16, jnp.bfloat16, jnp.bfloat16),
    )

    def take(k):
        return jax.tree.map(lambda part, own: part[k].astype(own.dtype), everything, shard)

    return lax.fori_loop(
        1, lax.axis_size(axis), lambda k, so_far: combine(so_far, take(k)), take(0)
    )


def combine_parts(former, latter):
    joined_max = jnp.maximum(former[0], latter[0])
    former_factor = jnp.exp(former[0] - joined_max)
    latter_factor = jnp.exp(latter[0] - joined_max)
    joined_total = former[1] * former_factor + latter[1] * latter_factor
    joined_sums = former[2] * former_factor[..., None] + latter[2] * latter_factor[..., None]
    return (joined_max, joined_total, joined_sums)


def local(
    query_nope,
    query_rope,
    latent_cache,
    lengths,
    block_ids,
    key_absorb,
    value_absorb,
    output_weight,
):
    request_count, draft_count, head_count, _ = query_nope.shape
    ctx_tokens = latent_cache.shape[1]
    value_width = value_absorb.shape[2]
    softmax_scale = (query_nope.shape[3] + query_rope.shape[3]) ** (-0.5)
    query_piece = jnp.einsum(
        "rtho,hoc->rthc", query_nope, key_absorb, preferred_element_type=jnp.float32
    ).astype(jnp.bfloat16)
    q_latent = lax.all_gather(query_piece, "ctx", axis=3, tiled=True)
    latent_width = q_latent.shape[3]
    query_rows = jnp.concatenate([q_latent, query_rope], axis=3).reshape(
        request_count, draft_count * head_count, -1
    )
    scores = (
        jnp.einsum("rqc,rjc->rqj", query_rows, latent_cache, preferred_element_type=jnp.float32)
        * softmax_scale
    )
    first_token = lax.axis_index("ctx") * ctx_tokens
    position = first_token + jnp.arange(ctx_tokens, dtype=jnp.int32)
    local_blocks = first_token // BLK + jnp.arange(ctx_tokens // BLK, dtype=jnp.int32)
    chosen_blocks = jnp.any(block_ids[:, :, :, None] == local_blocks[None, None, None, :], axis=2)
    chosen_tokens = jnp.repeat(chosen_blocks, BLK, axis=2)
    limit = lengths[:, None] - draft_count + jnp.arange(draft_count, dtype=jnp.int32)[None, :]
    visible = chosen_tokens & (position[None, None, :] <= limit[:, :, None])
    visible_mask = jnp.broadcast_to(
        visible[:, :, None, :], (request_count, draft_count, head_count, ctx_tokens)
    ).reshape(request_count, draft_count * head_count, ctx_tokens)
    scores = jnp.where(visible_mask, scores, -1e30)
    value_rows = latent_cache[:, :, :latent_width]
    local_max = jnp.max(scores, axis=2)
    weights = jnp.where(visible_mask, jnp.exp(scores - local_max[..., None]), 0.0)
    local_total = jnp.sum(weights, axis=2)
    weighted = jnp.einsum(
        "rqj,rjc->rqc", weights.astype(jnp.bfloat16), value_rows, preferred_element_type=jnp.float32
    )
    joined_max, denominator, weighted = joined(
        (local_max, local_total, weighted), "ctx", combine_parts
    )
    o_latent = (
        (weighted / denominator[..., None])
        .astype(jnp.bfloat16)
        .reshape(request_count, draft_count, head_count, latent_width)
    )
    head_values = jnp.einsum(
        "rthc,hcv->rthv",
        o_latent,
        lax.all_gather(value_absorb, "ctx", axis=1, tiled=True),
        preferred_element_type=jnp.float32,
    )
    flat_heads = head_values.astype(jnp.bfloat16).reshape(
        request_count * draft_count, head_count * value_width
    )
    partial_output = jnp.dot(flat_heads, output_weight, preferred_element_type=jnp.float32)
    summed = lax.psum_scatter(partial_output, "head", scatter_dimension=1, tiled=True)
    return summed.astype(jnp.bfloat16).reshape(request_count, draft_count, -1)


def solution(mesh):
    placed = (
        P(("groups", "sub"), None, "head", None),
        P(("groups", "sub"), None, "head", None),
        P(("groups", "sub"), "ctx", None),
        P(("groups", "sub")),
        P(("groups", "sub"), None, None),
        P("head", None, "ctx"),
        P("head", "ctx", None),
        P("head", "ctx"),
    )
    return jax.shard_map(
        local,
        mesh=mesh,
        in_specs=placed,
        out_specs=P(("groups", "sub"), None, ("ctx", "head")),
        check_vma=False,
    )
```

profile of v0, /device:TPU:0, one launch (start us, length us, event | category | flops | bytes accessed | tf_op | source)
XLA Modules:
  0.0 254.8 jit_solution(17346021313962555228)
XLA Ops:
  6.5 0.0 copy-start
  6.5 0.0 all-gather.10.cloned.1.call-start
  6.6 0.9 compare_reduce_fusion
  7.5 0.1 broadcast_in_dim.34
  7.6 0.1 broadcast_in_dim.35
  8.4 0.0 copy-done
  8.4 1.5 fusion.13
  9.9 15.8 %all_gather.20 = bf16[1,4,64,512]{3,1,2,0:T(4,128)(2,1)S(1)} all-gather(bf16[1,4,64,128]{3,1,2,0:T(4,128)(2,1)S(1)} %fusion.13), channel_id=1, replica_groups=mesh['groups'=2,'ctx'=4,'head'=2,'sub'=2] {'ctx'}, dimensions={3}, use_global_device_ids=true | all-gather | bytes 327680 | tf_op jit(solution)/shard_map/all_gather | solution.py:50
  25.7 0.9 copy.24
  26.6 0.2 pad_maximum_fusion
  26.8 0.1 compare_and_fusion
  26.9 0.0 slice-start
  26.9 0.0 slice-start.1
  26.9 4.6 %fusion.21 = (f32[256]{0:T(256)S(1)}, f32[256,4096]{1,0:T(8,128)S(1)}) fusion(bf16[256,576]{1,0:T(8,128)(2,1)S(1)} %bitcast.92, bf16[1,4096,576]{1,2,0:T(8,128)(2,1)} %param.12, pred[4,4096]{1,0:T(4,128)(4,1)S(1)} %compare_and_fusion), kind=kOutput, calls=%fused_computation.40 | convolution fusion | flops 1211105024 | bytes 9225216 | tf_op jit(solution)/shard_map/rqc,rjc->rqj/dot_general | solution.py:56
  31.5 1.0 fusion.7
  32.6 0.0 slice-done
  32.6 0.0 slice-done.1
  32.6 2.0 fusion.9
  34.6 0.0 all-gather.10.cloned.1.call-update
  34.6 0.0 all-gather.8.cloned.1.call-start
  34.6 0.7 all-gather.8.cloned.1.call-update
  35.3 0.0 reduce-scatter.4.cloned.1.call-start
  35.4 7.6 %all-gather.4 = bf16[4,1,256]{2,1,0:T(2,128)(2,1)S(1)} all-gather(bf16[1,1,256]{2,1,0:T(2,128)(2,1)S(1)} %reshape.325), channel_id=3, replica_groups=mesh['groups'=2,'ctx'=4,'head'=2,'sub'=2] {'ctx'}, dimensions={0}, use_global_device_ids=true | all-gather | bytes 2560 | tf_op jit(solution)/shard_map/all_gather | solution.py:11
  43.0 9.7 %all-gather.3 = bf16[4,1,256]{2,1,0:T(2,128)(2,1)S(1)} all-gather(bf16[1,1,256]{2,1,0:T(2,128)(2,1)S(1)} %reshape.323), channel_id=2, replica_groups=mesh['groups'=2,'ctx'=4,'head'=2,'sub'=2] {'ctx'}, dimensions={0}, use_global_device_ids=true | all-gather | bytes 2560 | tf_op jit(solution)/shard_map/all_gather | solution.py:11
  52.7 8.2 %all-gather.10.cloned.1.call-done = bf16[1024,512]{1,0:T(8,128)(2,1)} async-done(((bf16[256,512]{1,0:T(8,128)(2,1)}), bf16[1024,512]{1,0:T(8,128)(2,1)}) %all-gather.10.cloned.1.call-update) | async-done | bytes 1048592 | tf_op jit(solution)/shard_map/all_gather | solution.py:11
  60.9 1.0 fusion.14
  61.9 3.5 %while.19 = (s32[]{:T(128)}, f32[1,256]{1,0:T(1,128)S(1)}, f32[1,256]{1,0:T(1,128)S(1)}, f32[1,256,512]{2,1,0:T(8,128)S(1)}, bf16[4,1,256]{2,1,0:T(2,128)(2,1)S(...) while((s32[]{:T(128)}, f32[1,256]{1,0:T(1,128)S(1)}, ...), condition=%wide.region_4.5_spmd, body=%wide.region_3.4_spmd.sunk | while | flops 526341 | bytes 1320087 | solution.py:19
  62.0 1.1 fusion.30
  63.2 1.1 fusion.30
  64.3 1.1 fusion.30
  65.5 0.1 divide_convert_fusion
  65.6 146.1 %all-gather.8.cloned.1.call-done = bf16[64,512,128]{2,1,0:T(8,128)(2,1)} async-done(((bf16[64,128,128]{2,1,0:T(8,128)(2,1)}), bf16[64,512,128]{2,1,0:T(8,128)(2,1)}) %all-gather.8.cloned.1.call-update) | async-done | bytes 8388624 | tf_op jit(solution)/shard_map/all_gather | solution.py:88
  211.7 17.6 %convolution_bitcast_fusion = f32[1792,4]{1,0:T(8,128)} fusion(bf16[8192,1792]{1,0:T(8,128)(2,1)} %param.17, bf16[64,512,128]{2,1,0:T(8,128)(2,1)} %all-gather.8.cloned.1.call-done, bf16[4,64,512]{2,1,0:T(8,128)(2,1)S(1)} %bitcast.91), kind=kOutput, calls=%fused_computation.18 | convolution fusion | flops 151027712 | bytes 38039552
  229.2 0.0 reduce-scatter.4.cloned.1.call-update
  229.2 17.2 %reduce-scatter.4.cloned.1.call-done = f32[896,4]{1,0:T(8,128)} async-done(((f32[1792,4]{1,0:T(8,128)}), f32[896,4]{1,0:T(8,128)}) %reduce-scatter.4.cloned.1.call-update) | async-done | bytes 14352
  246.5 1.8 copy.29
  (13 shorter events, 0.2 us)
Async XLA Ops:
  6.5 1.9 copy-start
  6.5 54.4 %all-gather.10.cloned.1.call-start = ((), (), s32[]{:S(2)}) async-start(), calls=%async_computation.2 | async-start | bytes 1310720 | tf_op jit(solution)/shard_map/all_gather | solution.py:11
  26.9 5.7 %slice-start = ((s8[4718592]{0:T(1024)(128)(4,1)}), s8[4194304]{0:T(1024)(128)(4,1)S(1)}, s32[]{:S(2)}) async-start(s8[4718592]{0:T(1024)(128)(4,1)} %bitcast.88), calls=%async_computation.4 | async-start | bytes 8388608
  26.9 5.7 %slice-start.1 = ((s8[4718592]{0:T(1024)(128)(4,1)}), s8[524288]{0:T(1024)(128)(4,1)S(1)}, s32[]{:S(2)}) async-start(s8[4718592]{0:T(1024)(128)(4,1)} %bitcast.88), calls=%async_computation.5 | async-start | bytes 1048576
  34.6 177.1 %all-gather.8.cloned.1.call-start = ((), (), s32[]{:S(2)}) async-start(), calls=%async_computation.1 | async-start | bytes 10485760 | tf_op jit(solution)/shard_map/all_gather | solution.py:88
  35.3 211.1 %reduce-scatter.4.cloned.1.call-start = ((), (), s32[]{:S(2)}) async-start(), calls=%async_computation.3 | async-start | bytes 1376256
Sparse Core Ops, SparseCore 0:
  34.7 26.1 all-gather.9
  62.5 149.1 all-gather.7
  229.4 17.0 reduce-scatter.3
where the time goes:
time: 255 us
  waiting for transfers between devices  172 us (67%)
  blocking collectives  33 us (13%)
  matrix products  25.6 us (10%)
  between operations  13.9 us (5%)
  other arithmetic  6.81 us (3%)
  local copies, waits for them, and re-layouts  2.98 us (1%)
    all_gather x1, waiting for transfers between devices, local(): lax.all_gather(value_absorb, 'ctx', axis=1, tiled=True)  146 us
    unnamed x4, waiting for transfers between devices  17.9 us
    unnamed x1, matrix products  17.6 us
    all_gather x2, blocking collectives, joined(): lax.all_gather(part.astype(kind), axis)  17.3 us
    all_gather x1, blocking collectives, local(): q_latent = lax.all_gather(query_piece, 'ctx', axis=3, tiled=True)  15.8 us
    all_gather x1, waiting for transfers between devices, joined(): lax.all_gather(part.astype(kind), axis)  8.25 us
  transfers between devices with their start and end apart: 3, of which 3 were waited for; matrix products, arithmetic and copies ran while one was open for 2% of the time, Pallas kernels for 0%

commit v1 on v0

v1 whole, which is shorter than its diff:
```python
import jax
import jax.numpy as jnp
from jax import lax
from jax.sharding import PartitionSpec as P

BLK = 64
FEW = 4


def swap(value, axis, step):
    count = lax.axis_size(axis)
    return lax.ppermute(value, axis, [(i, i ^ step) for i in range(count)])


def everyone(value, axis):
    me, count = lax.axis_index(axis), lax.axis_size(axis)
    held = jnp.stack([value] + [swap(value, axis, step) for step in range(1, count)])
    return [held[me ^ i] for i in range(count)]


def halves(value):
    high = lax.reduce_precision(value, 8, 7)
    return high.astype(jnp.bfloat16), (value - high).astype(jnp.bfloat16)


def combine_few(local_max, total, weighted):
    me, count = lax.axis_index("ctx"), lax.axis_size("ctx")
    rows, width = weighted.shape
    part = width // count
    stats = jnp.stack([*halves(local_max), *halves(total)]).reshape(-1, part)

    def chunk(step):
        mine = lax.dynamic_slice(weighted, (0, (me ^ step) * part), (rows, part))
        return jnp.concatenate([mine.astype(jnp.bfloat16), stats], axis=0)

    held = [chunk(0)] + [swap(chunk(step), "ctx", step) for step in range(1, count)]
    maxima, totals, sums = [], [], []
    for packed in held:
        numbers = packed[rows:].astype(jnp.float32).reshape(4, rows)
        maxima.append(numbers[0] + numbers[1])
        totals.append(numbers[2] + numbers[3])
        sums.append(packed[:rows].astype(jnp.float32))
    joint = maxima[0]
    for other in maxima[1:]:
        joint = jnp.maximum(joint, other)
    factors = [jnp.exp(other - joint) for other in maxima]
    total = sum(a * b for a, b in zip(totals, factors))
    return sum(a * b[:, None] for a, b in zip(sums, factors)) / total[:, None]


def combine_many(local_max, total, weighted):
    joint = lax.pmax(local_max, "ctx")
    factor = jnp.exp(local_max - joint)
    total = lax.psum(total * factor, "ctx")
    summed = lax.psum_scatter(weighted * factor[:, None], "ctx", scatter_dimension=1, tiled=True)
    return summed / total[:, None]


def local(
    query_nope,
    query_rope,
    latent_cache,
    lengths,
    block_ids,
    key_absorb,
    value_absorb,
    output_weight,
):
    _, drafts, heads, nope = query_nope.shape
    rope = query_rope.shape[3]
    tokens = latent_cache.shape[1]
    scale = (nope + rope) ** (-0.5)
    rows = drafts * heads
    few = lax.axis_size("ctx") <= FEW

    q_piece = jnp.einsum(
        "tho,hoc->thc", query_nope[0], key_absorb, preferred_element_type=jnp.float32
    ).astype(jnp.bfloat16)
    if few:
        pieces = everyone(q_piece, "ctx")
    else:
        pieces = [lax.all_gather(q_piece, "ctx", axis=2, tiled=True)]
    queries = jnp.concatenate(pieces + [query_rope[0]], axis=2).reshape(rows, -1)
    latent = queries.shape[1] - rope

    cache = latent_cache[0]
    scores = jnp.einsum("qc,jc->qj", queries, cache, preferred_element_type=jnp.float32) * scale
    first = lax.axis_index("ctx") * tokens
    position = first + jnp.arange(tokens, dtype=jnp.int32)
    blocks = first // BLK + jnp.arange(tokens // BLK, dtype=jnp.int32)
    chosen = jnp.any(block_ids[0][:, :, None] == blocks[None, None, :], axis=1)
    limit = lengths[0] - drafts + jnp.arange(drafts, dtype=jnp.int32)
    visible = jnp.repeat(chosen, BLK, axis=1) & (position[None, :] <= limit[:, None])
    visible = jnp.broadcast_to(visible[:, None, :], (drafts, heads, tokens)).reshape(rows, tokens)
    scores = jnp.where(visible, scores, -1e30)
    local_max = jnp.max(scores, axis=1)
    weights = jnp.where(visible, jnp.exp(scores - local_max[:, None]), 0.0)
    total = jnp.sum(weights, axis=1)
    weighted = jnp.einsum(
        "qj,jc->qc",
        weights.astype(jnp.bfloat16),
        cache[:, :latent],
        preferred_element_type=jnp.float32,
    )

    combine = combine_few if few else combine_many
    o_latent = combine(local_max, total, weighted).astype(jnp.bfloat16)
    head_values = jnp.einsum(
        "thc,hcv->thv",
        o_latent.reshape(drafts, heads, -1),
        value_absorb,
        preferred_element_type=jnp.float32,
    )
    if few:
        piece = head_values.astype(jnp.bfloat16)
        head_values = piece.astype(jnp.float32)
        for step in range(1, lax.axis_size("ctx")):
            head_values += swap(piece, "ctx", step).astype(jnp.float32)
    else:
        head_values = lax.psum(head_values, "ctx")
    flat = head_values.astype(jnp.bfloat16).reshape(drafts, -1)
    partial = jnp.dot(flat, output_weight, preferred_element_type=jnp.float32)
    if lax.axis_size("head") == 2:
        me, half = lax.axis_index("head"), partial.shape[1] // 2
        mine = lax.dynamic_slice(partial, (0, me * half), (drafts, half))
        theirs = lax.dynamic_slice(partial, (0, (1 - me) * half), (drafts, half))
        summed = mine + swap(theirs, "head", 1)
    else:
        summed = lax.psum_scatter(partial, "head", scatter_dimension=1, tiled=True)
    return summed.astype(jnp.bfloat16)[None]


def solution(mesh):
    placed = (
        P(("groups", "sub"), None, "head", None),
        P(("groups", "sub"), None, "head", None),
        P(("groups", "sub"), "ctx", None),
        P(("groups", "sub")),
        P(("groups", "sub"), None, None),
        P("head", None, "ctx"),
        P("head", "ctx", None),
        P("head", "ctx"),
    )
    return jax.shard_map(
        local,
        mesh=mesh,
        in_specs=placed,
        out_specs=P(("groups", "sub"), None, ("ctx", "head")),
        check_vma=False,
    )
```

time: 255 us -> 61.1 us (0.24)
  waiting for transfers between devices: 172 us -> 13.8 us
  blocking collectives: 33 us -> 0 us
  starting transfers between devices: 0.08 us -> 16 us
  between operations: 13.9 us -> 0.87 us
    all_gather x2 -> x0, waiting for transfers between devices: 154 us -> none  [the longest x1 146 us: local(): lax.all_gather(value_absorb, 'ctx', axis=1, tiled=True)]
    all_gather x3 -> x0, blocking collectives: 33 us -> none  [the longest x2 17.3 us: joined(): lax.all_gather(part.astype(kind), axis)]
    unnamed x4 -> x0, waiting for transfers between devices: 17.9 us -> none
    unnamed x1 -> x0, matrix products: 17.6 us -> none
    ppermute x0 -> x10, starting transfers between devices: none -> 16 us  [swap(): return lax.ppermute(value, axis, [(i, i ^ step) for i in range(count)])]
    dot_general x3 -> x5, matrix products: 8.06 us -> 23.6 us  [the longest x1 11.4 us: local(): partial = jnp.dot(flat, output_weight, preferred_element_type=jnp.float32)]
    ppermute x0 -> x10, waiting for transfers between devices: none -> 13.8 us  [swap(): return lax.ppermute(value, axis, [(i, i ^ step) for i in range(count)])]
    add x9 -> x4, other arithmetic: 3.47 us -> 0.03 us  [the longest x1 0.02 us: combine_few(): total = sum((a * b for a, b in zip(totals, factors)))]
  transfers between devices with their start and end apart: 3 -> 10, of which waited for: 3 -> 8; matrix products, arithmetic and copies ran while one was open for 2% -> 2% of each run, Pallas kernels for 0% -> 0%
where the time goes in v1:
time: 61.1 us; the launch traced here: 60.8 us
  matrix products  23.6 us (39%)
  starting transfers between devices  16 us (26%)
  waiting for transfers between devices  13.8 us (23%)
  other arithmetic  4.33 us (7%)
  local copies, waits for them, and re-layouts  2.11 us (3%)
  between operations  0.87 us (1%)
    ppermute x10, starting transfers between devices, swap(): return lax.ppermute(value, axis, [(i, i ^ step) for i in range(count)])  16 us
    ppermute x10, waiting for transfers between devices, swap(): return lax.ppermute(value, axis, [(i, i ^ step) for i in range(count)])  13.8 us
    dot_general x1, matrix products, local(): partial = jnp.dot(flat, output_weight, preferred_element_type=jnp.float32)  11.4 us
    dot_general x1, matrix products, local(): jnp.einsum('qc,jc->qj', queries, cache, preferred_element_type=jnp.float32)  4.44 us
    dot_general x1, matrix products, local(): jnp.einsum('qj,jc->qc', weights.astype(jnp.bfloat16), cache[:, :latent],...  4.11 us
    reduce_sum x1, other arithmetic, local(): total = jnp.sum(weights, axis=1)  2.29 us
    dot_general x1, matrix products, local(): jnp.einsum('thc,hcv->thv', o_latent.reshape(drafts, heads, -1), value_abs...  2.24 us
    unnamed x8, local copies, waits for them, and re-layouts  1.66 us
  transfers between devices with their start and end apart: 10, of which 8 were waited for; matrix products, arithmetic and copies ran while one was open for 2% of the time, Pallas kernels for 0%

profile of v1, /device:TPU:0, one launch (start us, length us, event | category | flops | bytes accessed | tf_op | source)
XLA Modules:
  0.0 60.8 jit_solution(4992635196966263915)
XLA Ops:
  0.0 0.0 copy-start
  0.0 0.0 copy-start.1
  0.0 1.6 %copy-done = bf16[64,128,128]{2,1,0:T(8,128)(2,1)S(1)} copy-done((bf16[64,128,128]{2,1,0:T(8,128)(2,1)S(1)}, bf16[64,128,128]{2,1,0:T(8,128)(2,1)}, u32[]{:S(2)}) %copy-start) | copy-done | bytes 2097176
  1.6 1.5 %convolution_convert_fusion.1 = bf16[64,128,4]{1,2,0:T(4,128)(2,1)S(1)} fusion(bf16[64,128,128]{2,1,0:T(8,128)(2,1)S(1)} %copy-done, bf16[4,64,128]{2,1,0:T(8,128)(2,1)} %bitcast.99), kind=kOutput, calls=%fused_computation.8 | convolution fusion | flops 8421376 | bytes 2228224 | tf_op jit(solution)/shard_map/tho,hoc->thc/dot_general | solution.py:76
  3.1 3.0 %collective-permute-start = (bf16[4,64,128]{2,0,1:T(4,128)(2,1)S(1)}, bf16[4,64,128]{2,0,1:T(4,128)(2,1)S(1)}, u32[]{:S(2)}, u32[]{:S(2)}) collective-permute-start(bf16[4,64,128]{2,0,1:T(4,128)(2,1)S(1)} %bitcast.95), channel_id=1, source_target_pairs={{0,4},{4,0},{8,12},{12,8},{1,5},{5,1},{9,13},{13,9},{2,6},{6,2},{1... | collective-permute-start | bytes 196616 | tf_op jit(solution)/shard_map/ppermute | solution.py:12
  6.1 2.6 %collective-permute-start.1 = (bf16[4,64,128]{2,0,1:T(4,128)(2,1)S(1)}, bf16[4,64,128]{2,0,1:T(4,128)(2,1)S(1)}, u32[]{:S(2)}, u32[]{:S(2)}) collective-permute-start(bf16[4,64,128]{2,0,1:T(4,128)(2,1)S(1)} %bitcast.96), channel_id=1, source_target_pairs={{0,8},{4,12},{8,0},{12,4},{1,9},{5,13},{9,1},{13,5},{2,10},{6,14},... | collective-permute-start | bytes 196616 | tf_op jit(solution)/shard_map/ppermute | solution.py:12
  8.7 0.0 collective-permute-start.2
  8.7 0.8 %compare_reduce_fusion = pred[4,64]{1,0:T(4,128)(4,1)S(1)} fusion(s32[64]{0:T(128)S(1)} %iota_add_fusion.2, s32[4,32]{1,0:T(4,128)} %bitcast.106), kind=kLoop, calls=%fused_computation.25 | loop fusion | flops 16128 | bytes 1024 | tf_op jit(solution)/shard_map/reduce_or | solution.py:91
  9.5 0.1 broadcast_in_dim.13
  9.6 0.1 reshape.340
  10.4 0.1 compare_and_fusion
  10.5 0.0 collective-permute-done
  10.5 2.8 %collective-permute-done.1 = bf16[4,64,128]{2,0,1:T(4,128)(2,1)S(1)} collective-permute-done((bf16[4,64,128]{2,0,1:T(4,128)(2,1)S(1)}, bf16[4,64,128]{2,0,1:T(4,128)(2,1)S(1)}, u32[]{:S(2)}, u32[]{:S(2)}) %collective-permute-start.1) | collective-permute-done | bytes 65568 | tf_op jit(solution)/shard_map/ppermute | solution.py:12
  13.4 1.4 %collective-permute-done.2 = bf16[4,64,128]{2,0,1:T(4,128)(2,1)S(1)} collective-permute-done((bf16[4,64,128]{2,0,1:T(4,128)(2,1)S(1)}, bf16[4,64,128]{2,0,1:T(4,128)(2,1)S(1)}, u32[]{:S(2)}, u32[]{:S(2)}) %collective-permute-start.2) | collective-permute-done | bytes 65568 | tf_op jit(solution)/shard_map/ppermute | solution.py:12
  14.8 0.2 pad_maximum_fusion
  15.0 0.1 constant_dynamic-slice_fusion.1
  15.3 0.0 copy-done.1
  15.3 4.4 %fusion.25 = (f32[256]{0:T(256)S(1)}, f32[256,4096]{1,0:T(8,128)S(1)}) fusion(bf16[256,576]{1,0:T(8,128)(2,1)S(1)} %constant_dynamic-update-slice_fusion, bf16[1,4096,576]{1,2,0:T(8,128)(2,1)} %param.10, pred[4,4096]{1,0:T(4,128)(4,1)S(1)} %compare_and_fusion), kind=kOutput, calls=%fused_computation.74 | convolution fusion | flops 1211105024 | bytes 9225216 | tf_op jit(solution)/shard_map/qc,jc->qj/dot_general | solution.py:87
  19.8 2.3 %fusion.2 = (f32[256]{0:T(256)S(1)}, bf16[256,4096]{1,0:T(8,128)(2,1)}) fusion(f32[256,4096]{1,0:T(8,128)S(1)} %get-tuple-element.27, f32[256]{0:T(256)S(1)} %get-tuple-element.26, pred[4,4096]{1,0:T(4,128)(4,1)S(1)} %compare_and_fusion), kind=kLoop, calls=%fused_computation.5 | loop fusion | flops 4194048 | bytes 6309888 | tf_op jit(solution)/shard_map/reduce_sum | solution.py:98
  22.1 4.1 %fusion = bf16[256,512]{1,0:T(8,128)(2,1)S(1)} fusion(bf16[256,4096]{1,0:T(8,128)(2,1)} %get-tuple-element.11, bf16[4096,576]{0,1:T(8,128)(2,1)} %bitcast.89), kind=kOutput, calls=%fused_computation.3 | convolution fusion | flops 1073741824 | bytes 6553600 | tf_op jit(solution)/shard_map/qj,jc->qc/dot_general | solution.py:99
  26.3 1.8 %collective-permute-start.5 = (bf16[264,128]{1,0:T(8,128)(2,1)S(1)}, bf16[264,128]{1,0:T(8,128)(2,1)S(1)}, u32[]{:S(2)}, u32[]{:S(2)}) collective-permute-start(bf16[264,128]{1,0:T(8,128)(2,1)S(1)} %get-tuple-element.21), channel_id=1, source_target_pairs={{0,12},{4,8},{8,4},{12,0},{1,13},{5,9},{9,5},{13,1},{2,14},{6,10},... | collective-permute-start | bytes 202760 | tf_op jit(solution)/shard_map/ppermute | solution.py:12
  28.2 0.0 collective-permute-start.4
  28.2 2.6 %collective-permute-start.3 = (bf16[264,128]{1,0:T(8,128)(2,1)S(1)}, bf16[264,128]{1,0:T(8,128)(2,1)S(1)}, u32[]{:S(2)}, u32[]{:S(2)}) collective-permute-start(bf16[264,128]{1,0:T(8,128)(2,1)S(1)} %get-tuple-element.19), channel_id=1, source_target_pairs={{0,4},{4,0},{8,12},{12,8},{1,5},{5,1},{9,13},{13,9},{2,6},{6,2},{1... | collective-permute-start | bytes 202760 | tf_op jit(solution)/shard_map/ppermute | solution.py:12
  30.8 1.7 %collective-permute-done.5 = bf16[264,128]{1,0:T(8,128)(2,1)S(1)} collective-permute-done((bf16[264,128]{1,0:T(8,128)(2,1)S(1)}, bf16[264,128]{1,0:T(8,128)(2,1)S(1)}, u32[]{:S(2)}, u32[]{:S(2)}) %collective-permute-start.5) | collective-permute-done | bytes 67616 | tf_op jit(solution)/shard_map/ppermute | solution.py:12
  32.5 1.4 %collective-permute-done.4 = bf16[264,128]{1,0:T(8,128)(2,1)S(1)} collective-permute-done((bf16[264,128]{1,0:T(8,128)(2,1)S(1)}, bf16[264,128]{1,0:T(8,128)(2,1)S(1)}, u32[]{:S(2)}, u32[]{:S(2)}) %collective-permute-start.4) | collective-permute-done | bytes 67616 | tf_op jit(solution)/shard_map/ppermute | solution.py:12
  33.9 0.0 collective-permute-done.3
  33.9 0.2 divide_convert_fusion
  34.2 2.2 %fusion.4 = bf16[4,64,128]{2,0,1:T(4,128)(2,1)S(1)} fusion(bf16[64,128,128]{2,1,0:T(8,128)(2,1)} %param.14, bf16[4,64,128]{2,1,0:T(8,128)(2,1)S(1)} %bitcast.90), kind=kOutput, calls=%fused_computation.9 | convolution fusion | flops 8421376 | bytes 2228224 | tf_op jit(solution)/shard_map/thc,hcv->thv/dot_general | solution.py:108
  36.4 1.1 %collective-permute-start.6 = (bf16[4,64,128]{2,0,1:T(4,128)(2,1)S(1)}, bf16[4,64,128]{2,0,1:T(4,128)(2,1)S(1)}, u32[]{:S(2)}, u32[]{:S(2)}) collective-permute-start(bf16[4,64,128]{2,0,1:T(4,128)(2,1)S(1)} %fusion.4), channel_id=1, source_target_pairs={{0,4},{4,0},{8,12},{12,8},{1,5},{5,1},{9,13},{13,9},{2,6},{6,2},{1... | collective-permute-start | bytes 196616 | tf_op jit(solution)/shard_map/ppermute | solution.py:12
  37.6 1.4 %collective-permute-start.7 = (bf16[4,64,128]{2,0,1:T(4,128)(2,1)S(1)}, bf16[4,64,128]{2,0,1:T(4,128)(2,1)S(1)}, u32[]{:S(2)}, u32[]{:S(2)}) collective-permute-start(bf16[4,64,128]{2,0,1:T(4,128)(2,1)S(1)} %fusion.4), channel_id=1, source_target_pairs={{0,8},{4,12},{8,0},{12,4},{1,9},{5,13},{9,1},{13,5},{2,10},{6,14},... | collective-permute-start | bytes 196616 | tf_op jit(solution)/shard_map/ppermute | solution.py:12
  39.0 1.9 %collective-permute-start.8 = (bf16[4,64,128]{2,0,1:T(4,128)(2,1)S(1)}, bf16[4,64,128]{2,0,1:T(4,128)(2,1)S(1)}, u32[]{:S(2)}, u32[]{:S(2)}) collective-permute-start(bf16[4,64,128]{2,0,1:T(4,128)(2,1)S(1)} %fusion.4), channel_id=1, source_target_pairs={{0,12},{4,8},{8,4},{12,0},{1,13},{5,9},{9,5},{13,1},{2,14},{6,10},... | collective-permute-start | bytes 196616 | tf_op jit(solution)/shard_map/ppermute | solution.py:12
  40.8 0.6 collective-permute-done.6
  41.4 2.0 %collective-permute-done.7 = bf16[4,64,128]{2,0,1:T(4,128)(2,1)S(1)} collective-permute-done((bf16[4,64,128]{2,0,1:T(4,128)(2,1)S(1)}, bf16[4,64,128]{2,0,1:T(4,128)(2,1)S(1)}, u32[]{:S(2)}, u32[]{:S(2)}) %collective-permute-start.7) | collective-permute-done | bytes 65568 | tf_op jit(solution)/shard_map/ppermute | solution.py:12
  43.4 1.6 %collective-permute-done.8 = bf16[4,64,128]{2,0,1:T(4,128)(2,1)S(1)} collective-permute-done((bf16[4,64,128]{2,0,1:T(4,128)(2,1)S(1)}, bf16[4,64,128]{2,0,1:T(4,128)(2,1)S(1)}, u32[]{:S(2)}, u32[]{:S(2)}) %collective-permute-start.8) | collective-permute-done | bytes 65568 | tf_op jit(solution)/shard_map/ppermute | solution.py:12
  45.0 11.4 %fusion.6 = f32[4,1792]{1,0:T(4,128)S(1)} fusion(bf16[8192,1792]{1,0:T(8,128)(2,1)} %param.15, bf16[4,64,128]{2,0,1:T(4,128)(2,1)S(1)} %collective-permute-done.8, bf16[4,64,128]{2,0,1:T(4,128)(2,1)S(1)} %collective-permute-done.7, bf16[4,64,128]{2,0,1:T(4,128)(2,1)S(1)} %collective-permute-done.6, bf16[4,64,128]{2,0,1:T(4,128)(2,1)S(1)} %fusion.4), kind=kOutput, calls=%fused_computation.21 | convolution fusion | flops 117702656 | bytes 29650944 | tf_op jit(solution)/shard_map/dot_general | solution.py:122
  56.4 1.6 %collective-permute-start.9 = (f32[4,896]{1,0:T(4,128)S(1)}, f32[4,896]{1,0:T(4,128)S(1)}, u32[]{:S(2)}, u32[]{:S(2)}) collective-permute-start(f32[4,896]{1,0:T(4,128)S(1)} %constant_dynamic-slice_fusion), channel_id=1, source_target_pairs={{0,2},{2,0},{1,3},{3,1},{4,6},{6,4},{5,7},{7,5},{8,10},{10,8},{9,1... | collective-permute-start | bytes 43016 | tf_op jit(solution)/shard_map/ppermute | solution.py:12
  58.0 2.2 %collective-permute-done.9 = f32[4,896]{1,0:T(4,128)S(1)} collective-permute-done((f32[4,896]{1,0:T(4,128)S(1)}, f32[4,896]{1,0:T(4,128)S(1)}, u32[]{:S(2)}, u32[]{:S(2)}) %collective-permute-start.9) | collective-permute-done | bytes 14368 | tf_op jit(solution)/shard_map/ppermute | solution.py:12
  60.2 0.6 fusion.10
  (23 shorter events, 0.3 us)
Async XLA Ops:
  0.0 1.6 %copy-start = (bf16[64,128,128]{2,1,0:T(8,128)(2,1)S(1)}, bf16[64,128,128]{2,1,0:T(8,128)(2,1)}, u32[]{:S(2)}) copy-start(bf16[64,128,128]{2,1,0:T(8,128)(2,1)} %param.13) | copy-start | bytes 6291460
  0.0 15.3 %copy-start.1 = (bf16[1,4,64,64]{3,2,1,0:T(8,128)(2,1)S(1)}, bf16[1,4,64,64]{3,2,1,0:T(8,128)(2,1)}, u32[]{:S(2)}) copy-start(bf16[1,4,64,64]{3,2,1,0:T(8,128)(2,1)} %param.9) | copy-start | bytes 98308
  3.1 7.4 %collective-permute-start = (bf16[4,64,128]{2,0,1:T(4,128)(2,1)S(1)}, bf16[4,64,128]{2,0,1:T(4,128)(2,1)S(1)}, u32[]{:S(2)}, u32[]{:S(2)}) collective-permute-start(bf16[4,64,128]{2,0,1:T(4,128)(2,1)S(1)} %bitcast.95), channel_id=1, source_target_pairs={{0,4},{4,0},{8,12},{12,8},{1,5},{5,1},{9,13},{13,9},{2,6},{6,2},{1... | collective-permute-start | bytes 196616 | tf_op jit(solution)/shard_map/ppermute | solution.py:12
  6.1 7.3 %collective-permute-start.1 = (bf16[4,64,128]{2,0,1:T(4,128)(2,1)S(1)}, bf16[4,64,128]{2,0,1:T(4,128)(2,1)S(1)}, u32[]{:S(2)}, u32[]{:S(2)}) collective-permute-start(bf16[4,64,128]{2,0,1:T(4,128)(2,1)S(1)} %bitcast.96), channel_id=1, source_target_pairs={{0,8},{4,12},{8,0},{12,4},{1,9},{5,13},{9,1},{13,5},{2,10},{6,14},... | collective-permute-start | bytes 196616 | tf_op jit(solution)/shard_map/ppermute | solution.py:12
  8.7 6.1 %collective-permute-start.2 = (bf16[4,64,128]{2,0,1:T(4,128)(2,1)S(1)}, bf16[4,64,128]{2,0,1:T(4,128)(2,1)S(1)}, u32[]{:S(2)}, u32[]{:S(2)}) collective-permute-start(bf16[4,64,128]{2,0,1:T(4,128)(2,1)S(1)} %bitcast.97), channel_id=1, source_target_pairs={{0,12},{4,8},{8,4},{12,0},{1,13},{5,9},{9,5},{13,1},{2,14},{6,10},... | collective-permute-start | bytes 196616 | tf_op jit(solution)/shard_map/ppermute | solution.py:12
  26.3 6.2 %collective-permute-start.5 = (bf16[264,128]{1,0:T(8,128)(2,1)S(1)}, bf16[264,128]{1,0:T(8,128)(2,1)S(1)}, u32[]{:S(2)}, u32[]{:S(2)}) collective-permute-start(bf16[264,128]{1,0:T(8,128)(2,1)S(1)} %get-tuple-element.21), channel_id=1, source_target_pairs={{0,12},{4,8},{8,4},{12,0},{1,13},{5,9},{9,5},{13,1},{2,14},{6,10},... | collective-permute-start | bytes 202760 | tf_op jit(solution)/shard_map/ppermute | solution.py:12
  28.2 5.7 %collective-permute-start.4 = (bf16[264,128]{1,0:T(8,128)(2,1)S(1)}, bf16[264,128]{1,0:T(8,128)(2,1)S(1)}, u32[]{:S(2)}, u32[]{:S(2)}) collective-permute-start(bf16[264,128]{1,0:T(8,128)(2,1)S(1)} %get-tuple-element.20), channel_id=1, source_target_pairs={{0,8},{4,12},{8,0},{12,4},{1,9},{5,13},{9,1},{13,5},{2,10},{6,14},... | collective-permute-start | bytes 202760 | tf_op jit(solution)/shard_map/ppermute | solution.py:12
  28.2 5.8 %collective-permute-start.3 = (bf16[264,128]{1,0:T(8,128)(2,1)S(1)}, bf16[264,128]{1,0:T(8,128)(2,1)S(1)}, u32[]{:S(2)}, u32[]{:S(2)}) collective-permute-start(bf16[264,128]{1,0:T(8,128)(2,1)S(1)} %get-tuple-element.19), channel_id=1, source_target_pairs={{0,4},{4,0},{8,12},{12,8},{1,5},{5,1},{9,13},{13,9},{2,6},{6,2},{1... | collective-permute-start | bytes 202760 | tf_op jit(solution)/shard_map/ppermute | solution.py:12
  36.4 5.0 %collective-permute-start.6 = (bf16[4,64,128]{2,0,1:T(4,128)(2,1)S(1)}, bf16[4,64,128]{2,0,1:T(4,128)(2,1)S(1)}, u32[]{:S(2)}, u32[]{:S(2)}) collective-permute-start(bf16[4,64,128]{2,0,1:T(4,128)(2,1)S(1)} %fusion.4), channel_id=1, source_target_pairs={{0,4},{4,0},{8,12},{12,8},{1,5},{5,1},{9,13},{13,9},{2,6},{6,2},{1... | collective-permute-start | bytes 196616 | tf_op jit(solution)/shard_map/ppermute | solution.py:12
  37.6 5.9 %collective-permute-start.7 = (bf16[4,64,128]{2,0,1:T(4,128)(2,1)S(1)}, bf16[4,64,128]{2,0,1:T(4,128)(2,1)S(1)}, u32[]{:S(2)}, u32[]{:S(2)}) collective-permute-start(bf16[4,64,128]{2,0,1:T(4,128)(2,1)S(1)} %fusion.4), channel_id=1, source_target_pairs={{0,8},{4,12},{8,0},{12,4},{1,9},{5,13},{9,1},{13,5},{2,10},{6,14},... | collective-permute-start | bytes 196616 | tf_op jit(solution)/shard_map/ppermute | solution.py:12
  39.0 6.1 %collective-permute-start.8 = (bf16[4,64,128]{2,0,1:T(4,128)(2,1)S(1)}, bf16[4,64,128]{2,0,1:T(4,128)(2,1)S(1)}, u32[]{:S(2)}, u32[]{:S(2)}) collective-permute-start(bf16[4,64,128]{2,0,1:T(4,128)(2,1)S(1)} %fusion.4), channel_id=1, source_target_pairs={{0,12},{4,8},{8,4},{12,0},{1,13},{5,9},{9,5},{13,1},{2,14},{6,10},... | collective-permute-start | bytes 196616 | tf_op jit(solution)/shard_map/ppermute | solution.py:12
  56.4 3.8 %collective-permute-start.9 = (f32[4,896]{1,0:T(4,128)S(1)}, f32[4,896]{1,0:T(4,128)S(1)}, u32[]{:S(2)}, u32[]{:S(2)}) collective-permute-start(f32[4,896]{1,0:T(4,128)S(1)} %constant_dynamic-slice_fusion), channel_id=1, source_target_pairs={{0,2},{2,0},{1,3},{3,1},{4,6},{6,4},{5,7},{7,5},{8,10},{10,8},{9,1... | collective-permute-start | bytes 43016 | tf_op jit(solution)/shard_map/ppermute | solution.py:12

commit v2 on v1

v2 whole, which is shorter than its diff:
```python
import functools

import jax
import jax.numpy as jnp
from jax import lax
from jax.experimental import pallas as pl
from jax.experimental.pallas import tpu as pltpu
from jax.sharding import PartitionSpec as P

BLK = 64
FEW = 4
LANES = 128
TAIL = 16
LOG2E = 1.4426950408889634
HIDDEN = -1e30
MIB = 1024 * 1024
VMEM = pl.BlockSpec(memory_space=pltpu.VMEM)


def swap(value, axis, step):
    count = lax.axis_size(axis)
    return lax.ppermute(value, axis, [(i, i ^ step) for i in range(count)])


def thirds(value):
    high = value.astype(jnp.bfloat16)
    rest = value - high.astype(jnp.float32)
    middle = rest.astype(jnp.bfloat16)
    low = (rest - middle.astype(jnp.float32)).astype(jnp.bfloat16)
    return [part.astype(jnp.float32) for part in (high, middle, low)]


def attend_kernel(*refs, count, scale):
    pieces, (rope, cache, bias) = refs[:count], refs[count : count + 3]
    outs, (queries, total_sums) = refs[count + 3 : -2], refs[-2:]
    rows, width = pieces[0].shape
    latent = count * width
    me = lax.axis_index("ctx") if count > 1 else 0
    for step in range(count):
        at = pl.multiple_of((me ^ step) * width, width)
        queries[:, pl.ds(at, width)] = pieces[step][...]
    queries[:, latent:] = rope[...]

    tokens = cache.shape[1]
    scores = jnp.dot(queries[...], cache[...], preferred_element_type=jnp.float32)
    scores = (scores.reshape(rows // 8, 8, tokens) + bias[...][None]).reshape(rows, tokens)
    top = jnp.max(scores, axis=1, keepdims=True)
    weights = jnp.exp2((scores - top) * (scale * LOG2E))
    total = jnp.sum(weights, axis=1, keepdims=True)
    total_sums[...] = lax.dot_general(
        weights.astype(jnp.bfloat16),
        cache[:latent, :],
        (((1,), (1,)), ((), ())),
        preferred_element_type=jnp.float32,
    )

    lines = []
    for value in (top * scale, total):
        line = jnp.broadcast_to(value, (rows, LANES)).T[:1]
        for part in thirds(line):
            lines += [part[:, at : at + LANES] for at in range(0, rows, LANES)]
    lines.append(jnp.zeros((TAIL - len(lines), LANES), jnp.float32))
    tail = jnp.concatenate(lines, axis=0).astype(jnp.bfloat16)
    for step in range(count):
        at = pl.multiple_of((me ^ step) * width, width)
        outs[step][:rows, :] = total_sums[:, pl.ds(at, width)].astype(jnp.bfloat16)
        outs[step][rows:, :LANES] = tail


def attend(pieces, rope, cache, bias, scale):
    count, (rows, width) = len(pieces), pieces[0].shape
    depth = cache.shape[0]
    return pl.pallas_call(
        functools.partial(attend_kernel, count=count, scale=scale),
        out_shape=[jax.ShapeDtypeStruct((rows + TAIL, width), jnp.bfloat16)] * count,
        in_specs=[VMEM] * (count + 3),
        out_specs=[VMEM] * count,
        scratch_shapes=[
            pltpu.VMEM((rows, depth), jnp.bfloat16),
            pltpu.VMEM((rows, count * width), jnp.float32),
        ],
        compiler_params=pltpu.CompilerParams(vmem_limit_bytes=16 * MIB),
        name="attend",
    )(*pieces, rope, cache, bias)


def numbers_of(tail, rows):
    each = rows // LANES
    tail = tail.astype(jnp.float32)
    found = []
    for first in (0, 3 * each):
        parts = [
            jnp.concatenate([tail[at + i : at + i + 1] for i in range(each)], axis=1)
            for at in range(first, first + 3 * each, each)
        ]
        found.append(parts[0] + parts[1] + parts[2])
    return found


def values_kernel(*refs, drafts):
    blocks, value_absorb, out = refs[:-2], refs[-2], refs[-1]
    rows = out.shape[0]
    heads, width, value_width = value_absorb.shape
    numbers = [numbers_of(block[rows:, :], rows) for block in blocks]
    top = functools.reduce(jnp.maximum, [number[0] for number in numbers])
    factors = [jnp.exp(number[0] - top) for number in numbers]
    total = sum(factor * number[1] for factor, number in zip(factors, numbers))
    latent = jnp.zeros((rows, width), jnp.float32)
    for block, factor in zip(blocks, factors):
        column = jnp.broadcast_to(factor / total, (width, rows)).T
        latent += block[:rows, :].astype(jnp.float32) * column
    latent = latent.astype(jnp.bfloat16)
    pair = 2 * drafts
    first = lax.broadcasted_iota(jnp.int32, (pair, value_width), 0) < drafts
    for head in range(0, heads, 2):
        both = jnp.concatenate([value_absorb[head], value_absorb[head + 1]], axis=1)
        at = slice(head * drafts, head * drafts + pair)
        found = jnp.dot(latent[at], both, preferred_element_type=jnp.float32)
        out[at, :] = jnp.where(first, found[:, :value_width], found[:, value_width:]).astype(
            jnp.bfloat16
        )


def values_of(blocks, value_absorb, drafts):
    rows = blocks[0].shape[0] - TAIL
    return pl.pallas_call(
        functools.partial(values_kernel, drafts=drafts),
        out_shape=jax.ShapeDtypeStruct((rows, value_absorb.shape[2]), jnp.bfloat16),
        in_specs=[VMEM] * (len(blocks) + 1),
        out_specs=VMEM,
        compiler_params=pltpu.CompilerParams(vmem_limit_bytes=8 * MIB),
        name="values",
    )(*blocks, value_absorb)


def project_kernel(*refs, drafts):
    partials, weight, mine, theirs, flat, found = refs[:-5], *refs[-5:]
    rows, value_width = partials[0].shape
    summed = sum(partial[...].astype(jnp.float32) for partial in partials)
    for head in range(rows // drafts):
        flat[:, head * value_width : (head + 1) * value_width] = summed[
            head * drafts : (head + 1) * drafts
        ]
    found[...] = jnp.dot(
        flat[...].astype(jnp.bfloat16), weight[...], preferred_element_type=jnp.float32
    )
    half = mine.shape[1]
    me = lax.axis_index("head")
    mine[...] = found[:, pl.ds(pl.multiple_of(me * half, half), half)]
    theirs[...] = found[:, pl.ds(pl.multiple_of((1 - me) * half, half), half)]


def project(partials, weight, drafts):
    depth, width = weight.shape
    return pl.pallas_call(
        functools.partial(project_kernel, drafts=drafts),
        out_shape=[jax.ShapeDtypeStruct((drafts, width // 2), jnp.float32)] * 2,
        in_specs=[VMEM] * (len(partials) + 1),
        out_specs=[VMEM] * 2,
        scratch_shapes=[
            pltpu.VMEM((drafts, depth), jnp.float32),
            pltpu.VMEM((drafts, width), jnp.float32),
        ],
        compiler_params=pltpu.CompilerParams(vmem_limit_bytes=4 * MIB),
        name="project",
    )(*partials, weight)


def visibility(lengths, block_ids, tokens):
    drafts = block_ids.shape[1]
    first = lax.axis_index("ctx") * tokens
    position = first + jnp.arange(tokens, dtype=jnp.int32)
    blocks = first // BLK + jnp.arange(tokens // BLK, dtype=jnp.int32)
    chosen = jnp.any(block_ids[0][:, :, None] == blocks[None, None, :], axis=1)
    limit = lengths[0] - drafts + jnp.arange(drafts, dtype=jnp.int32)
    visible = jnp.repeat(chosen, BLK, axis=1) & (position[None, :] <= limit[:, None])
    bias = jnp.where(visible, 0.0, HIDDEN).astype(jnp.float32)
    return jnp.concatenate([bias] * (8 // drafts), axis=0)


def combine_many(block, rows):
    top, total = (line[0] for line in numbers_of(block[rows:, :LANES], rows))
    joint = lax.pmax(top, "ctx")
    factor = jnp.exp(top - joint)
    total = lax.psum(total * factor, "ctx")
    weighted = block[:rows].astype(jnp.float32) * factor[:, None]
    summed = lax.psum_scatter(weighted, "ctx", scatter_dimension=1, tiled=True)
    return (summed / total[:, None]).astype(jnp.bfloat16)


def local(
    query_nope,
    query_rope,
    latent_cache,
    lengths,
    block_ids,
    key_absorb,
    value_absorb,
    output_weight,
):
    _, drafts, heads, nope = query_nope.shape
    rope = query_rope.shape[3]
    tokens = latent_cache.shape[1]
    scale = (nope + rope) ** (-0.5)
    rows = drafts * heads
    peers = lax.axis_size("ctx")
    few = peers <= FEW and lax.axis_size("head") == 2 and key_absorb.shape[2] == LANES

    q_piece = jnp.einsum(
        "tho,hoc->htc", query_nope[0], key_absorb, preferred_element_type=jnp.float32
    ).astype(jnp.bfloat16)
    q_piece = q_piece.reshape(rows, -1)
    rope_rows = query_rope[0].transpose(1, 0, 2).reshape(rows, rope)
    bias = visibility(lengths, block_ids, tokens)
    cache = latent_cache[0].T
    if few:
        pieces = [q_piece] + [swap(q_piece, "ctx", step) for step in range(1, peers)]
        blocks = attend(pieces, rope_rows, cache, bias, scale)
        blocks = [blocks[0]] + [swap(blocks[step], "ctx", step) for step in range(1, peers)]
        partial = values_of(blocks, value_absorb, drafts)
        partials = [partial] + [swap(partial, "ctx", step) for step in range(1, peers)]
        mine, theirs = project(partials, output_weight, drafts)
        summed = mine + swap(theirs, "head", 1)
    else:
        queries = lax.all_gather(q_piece, "ctx", axis=1, tiled=True)
        block = attend([queries], rope_rows, cache, bias, scale)[0]
        o_latent = combine_many(block, rows)
        head_values = jnp.einsum(
            "htc,hcv->thv",
            o_latent.reshape(heads, drafts, -1),
            value_absorb,
            preferred_element_type=jnp.float32,
        )
        head_values = lax.psum(head_values, "ctx").astype(jnp.bfloat16)
        found = jnp.dot(
            head_values.reshape(drafts, -1), output_weight, preferred_element_type=jnp.float32
        )
        summed = lax.psum_scatter(found, "head", scatter_dimension=1, tiled=True)
    return summed.astype(jnp.bfloat16)[None]


def solution(mesh):
    placed = (
        P(("groups", "sub"), None, "head", None),
        P(("groups", "sub"), None, "head", None),
        P(("groups", "sub"), "ctx", None),
        P(("groups", "sub")),
        P(("groups", "sub"), None, None),
        P("head", None, "ctx"),
        P("head", "ctx", None),
        P("head", "ctx"),
    )
    return jax.shard_map(
        local,
        mesh=mesh,
        in_specs=placed,
        out_specs=P(("groups", "sub"), None, ("ctx", "head")),
        check_vma=False,
    )
```

time: 61.1 us -> 55.2 us (0.903)
  matrix products: 23.6 us -> 1.48 us
  local copies, waits for them, and re-layouts: 2.11 us -> 13.6 us
  Pallas kernels: 0 us -> 8.09 us
  other arithmetic: 4.33 us -> 0.83 us
    dot_general x5 -> x1, matrix products: 23.6 us -> 1.48 us  [local(): jnp.einsum('tho,hoc->htc', query_nope[0], key_absorb, preferred_element_t...]
    unnamed x8 -> x12, local copies, waits for them, and re-layouts: 1.66 us -> 13.3 us
    pallas_call x0 -> x3, Pallas kernels: none -> 8.09 us  [the longest x1 3.9 us: project(): pl.pallas_call(functools.partial(project_kernel, drafts=drafts), out_shap...]
    reduce_sum x1 -> x0, other arithmetic: 2.29 us -> none  [local(): total = jnp.sum(weights, axis=1)]
    reduce_or x1, other arithmetic: 0.78 us -> 0.1 us  [visibility(): chosen = jnp.any(block_ids[0][:, :, None] == blocks[None, None, :], axis=1)]
  transfers between devices with their start and end apart: 10 -> 10, of which waited for: 8 -> 8; matrix products, arithmetic and copies ran while one was open for 2% -> 1% of each run, Pallas kernels for 0% -> 0%
where the time goes in v2:
time: 55.2 us; the launch traced here: 55 us
  starting transfers between devices  16.1 us (29%)
  waiting for transfers between devices  14.2 us (26%)
  local copies, waits for them, and re-layouts  13.6 us (25%)
  Pallas kernels  8.09 us (15%)
  matrix products  1.48 us (3%)
  other arithmetic  0.83 us (2%)
  between operations  0.76 us (1%)
    ppermute x10, starting transfers between devices, swap(): return lax.ppermute(value, axis, [(i, i ^ step) for i in range(count)])  16.1 us
    ppermute x10, waiting for transfers between devices, swap(): return lax.ppermute(value, axis, [(i, i ^ step) for i in range(count)])  14.2 us
    unnamed x12, local copies, waits for them, and re-layouts  13.3 us
    pallas_call x1, Pallas kernels, project(): pl.pallas_call(functools.partial(project_kernel, drafts=drafts), out_shap...  3.9 us
    pallas_call x1, Pallas kernels, attend(): pl.pallas_call(functools.partial(attend_kernel, count=count, scale=scale)...  3.69 us
    dot_general x1, matrix products, local(): jnp.einsum('tho,hoc->htc', query_nope[0], key_absorb, preferred_element_t...  1.48 us
  transfers between devices with their start and end apart: 10, of which 8 were waited for; matrix products, arithmetic and copies ran while one was open for 1% of the time, Pallas kernels for 0%

profile of v2, /device:TPU:0, one launch (start us, length us, event | category | flops | bytes accessed | tf_op | source)
XLA Modules:
  0.0 55.0 jit_solution(6237548332872900834)
XLA Ops:
  0.0 0.0 copy-start
  0.0 0.0 copy-start.5
  0.0 0.0 copy-start.4
  0.0 1.6 %copy-done = bf16[64,128,128]{2,1,0:T(8,128)(2,1)S(1)} copy-done((bf16[64,128,128]{2,1,0:T(8,128)(2,1)S(1)}, bf16[64,128,128]{2,1,0:T(8,128)(2,1)}, u32[]{:S(2)}) %copy-start) | copy-done | bytes 2097176
  1.6 1.5 %convolution_convert_fusion = bf16[64,4,128]{2,1,0:T(4,128)(2,1)S(1)} fusion(bf16[64,128,128]{2,1,0:T(8,128)(2,1)S(1)} %copy-done, bf16[4,64,128]{2,1,0:T(8,128)(2,1)} %bitcast.20), kind=kOutput, calls=%fused_computation | convolution fusion | flops 8421376 | bytes 2228224 | tf_op jit(solution)/shard_map/tho,hoc->htc/dot_general | solution.py:209
  3.1 5.1 %collective-permute-start.2 = (bf16[256,128]{1,0:T(8,128)(2,1)S(1)}, bf16[256,128]{1,0:T(8,128)(2,1)S(1)}, u32[]{:S(2)}, u32[]{:S(2)}) collective-permute-start(bf16[256,128]{1,0:T(8,128)(2,1)S(1)} %bitcast.15), channel_id=1, source_target_pairs={{0,12},{4,8},{8,4},{12,0},{1,13},{5,9},{9,5},{13,1},{2,14},{6,10},... | collective-permute-start | bytes 196616 | tf_op jit(solution)/shard_map/ppermute | solution.py:22
  8.1 0.0 collective-permute-start.1
  8.1 0.6 %collective-permute-start = (bf16[256,128]{1,0:T(8,128)(2,1)S(1)}, bf16[256,128]{1,0:T(8,128)(2,1)S(1)}, u32[]{:S(2)}, u32[]{:S(2)}) collective-permute-start(bf16[256,128]{1,0:T(8,128)(2,1)S(1)} %bitcast.17), channel_id=1, source_target_pairs={{0,4},{4,0},{8,12},{12,8},{1,5},{5,1},{9,13},{13,9},{2,6},{6,2},{1... | collective-permute-start | bytes 196616 | tf_op jit(solution)/shard_map/ppermute | solution.py:22
  9.5 0.0 copy-done.5
  9.5 0.1 compare_reduce_fusion
  9.6 0.1 broadcast_in_dim.17
  9.7 0.1 reshape.26
  9.8 0.1 and_select_fusion
  9.9 0.0 copy-done.4
  10.0 0.1 copy.12
  10.0 0.7 %collective-permute-done.2.refs_3_ = bf16[256,128]{1,0:T(8,128)(2,1)S(1)} collective-permute-done((bf16[256,128]{1,0:T(8,128)(2,1)S(1)}, bf16[256,128]{1,0:T(8,128)(2,1)S(1)}, u32[]{:S(2)}, u32[]{:S(2)}) %collective-permute-start.2) | collective-permute-done | bytes 65568 | tf_op jit(solution)/shard_map/ppermute | solution.py:22
  10.7 3.0 %collective-permute-done.1.refs_2_ = bf16[256,128]{1,0:T(8,128)(2,1)S(1)} collective-permute-done((bf16[256,128]{1,0:T(8,128)(2,1)S(1)}, bf16[256,128]{1,0:T(8,128)(2,1)S(1)}, u32[]{:S(2)}, u32[]{:S(2)}) %collective-permute-start.1) | collective-permute-done | bytes 65568 | tf_op jit(solution)/shard_map/ppermute | solution.py:22
  13.7 0.0 collective-permute-done.refs_1_
  13.7 0.0 copy-start.2
  13.7 2.3 %copy-done.2 = bf16[1,4096,576]{1,2,0:T(8,128)(2,1)S(1)} copy-done((bf16[1,4096,576]{1,2,0:T(8,128)(2,1)S(1)}, bf16[1,4096,576]{1,2,0:T(8,128)(2,1)}, u32[]{:S(2)}) %copy-start.2) | copy-done | bytes 4718616
  16.1 0.0 copy-start.3
  16.1 3.7 %attend.1 = (bf16[272,128]{1,0:T(8,128)(2,1)S(1)}, bf16[272,128]{1,0:T(8,128)(2,1)S(1)}, bf16[272,128]{1,0:T(8,128)(2,1)S(1)}, bf16[272,128]{1,0:T(8,128)(2,1)S(1)}) custom-call(bf16[256,128]{1,0:T(8,128)(2,1)S(1)} %bitcast.18, bf16[256,128]{1,0:T(8,128)(2,1)S(1)} %collective-permute-done.refs_1_, bf16[256,128]{1,0:T(8,128)(2,1)S(1)} %collective-permute-done.1.refs_2_, ...), custom_call_target="tpu_custom_call" | custom-call | tf_op jit(solution)/shard_map/attend/pallas_call | solution.py:73
  19.8 1.2 %collective-permute-start.3 = (bf16[272,128]{1,0:T(8,128)(2,1)S(1)}, bf16[272,128]{1,0:T(8,128)(2,1)S(1)}, u32[]{:S(2)}, u32[]{:S(2)}) collective-permute-start(bf16[272,128]{1,0:T(8,128)(2,1)S(1)} %get-tuple-element.12), channel_id=1, source_target_pairs={{0,4},{4,0},{8,12},{12,8},{1,5},{5,1},{9,13},{13,9},{2,6},{6,2},{1... | collective-permute-start | bytes 208904 | tf_op jit(solution)/shard_map/ppermute | solution.py:22
  20.9 2.2 %collective-permute-start.4 = (bf16[272,128]{1,0:T(8,128)(2,1)S(1)}, bf16[272,128]{1,0:T(8,128)(2,1)S(1)}, u32[]{:S(2)}, u32[]{:S(2)}) collective-permute-start(bf16[272,128]{1,0:T(8,128)(2,1)S(1)} %get-tuple-element.13), channel_id=1, source_target_pairs={{0,8},{4,12},{8,0},{12,4},{1,9},{5,13},{9,1},{13,5},{2,10},{6,14},... | collective-permute-start | bytes 208904 | tf_op jit(solution)/shard_map/ppermute | solution.py:22
  23.1 1.1 %collective-permute-start.5 = (bf16[272,128]{1,0:T(8,128)(2,1)S(1)}, bf16[272,128]{1,0:T(8,128)(2,1)S(1)}, u32[]{:S(2)}, u32[]{:S(2)}) collective-permute-start(bf16[272,128]{1,0:T(8,128)(2,1)S(1)} %get-tuple-element.14), channel_id=1, source_target_pairs={{0,12},{4,8},{8,4},{12,0},{1,13},{5,9},{9,5},{13,1},{2,14},{6,10},... | collective-permute-start | bytes 208904 | tf_op jit(solution)/shard_map/ppermute | solution.py:22
  24.2 0.3 collective-permute-done.3.refs_1_
  24.6 3.1 %collective-permute-done.4.refs_2_ = bf16[272,128]{1,0:T(8,128)(2,1)S(1)} collective-permute-done((bf16[272,128]{1,0:T(8,128)(2,1)S(1)}, bf16[272,128]{1,0:T(8,128)(2,1)S(1)}, u32[]{:S(2)}, u32[]{:S(2)}) %collective-permute-start.4) | collective-permute-done | bytes 69664 | tf_op jit(solution)/shard_map/ppermute | solution.py:22
  27.6 1.7 %collective-permute-done.5.refs_3_ = bf16[272,128]{1,0:T(8,128)(2,1)S(1)} collective-permute-done((bf16[272,128]{1,0:T(8,128)(2,1)S(1)}, bf16[272,128]{1,0:T(8,128)(2,1)S(1)}, u32[]{:S(2)}, u32[]{:S(2)}) %collective-permute-start.5) | collective-permute-done | bytes 69664 | tf_op jit(solution)/shard_map/ppermute | solution.py:22
  29.3 0.0 copy-done.3
  29.4 0.5 values.1.refs_0_
  29.9 1.1 %collective-permute-start.8 = (bf16[256,128]{1,0:T(8,128)(2,1)S(1)}, bf16[256,128]{1,0:T(8,128)(2,1)S(1)}, u32[]{:S(2)}, u32[]{:S(2)}) collective-permute-start(bf16[256,128]{1,0:T(8,128)(2,1)S(1)} %values.1.refs_0_), channel_id=1, source_target_pairs={{0,12},{4,8},{8,4},{12,0},{1,13},{5,9},{9,5},{13,1},{2,14},{6,10},... | collective-permute-start | bytes 196616 | tf_op jit(solution)/shard_map/ppermute | solution.py:22
  30.9 0.5 collective-permute-start.7
  31.4 2.9 %collective-permute-start.6 = (bf16[256,128]{1,0:T(8,128)(2,1)S(1)}, bf16[256,128]{1,0:T(8,128)(2,1)S(1)}, u32[]{:S(2)}, u32[]{:S(2)}) collective-permute-start(bf16[256,128]{1,0:T(8,128)(2,1)S(1)} %values.1.refs_0_), channel_id=1, source_target_pairs={{0,4},{4,0},{8,12},{12,8},{1,5},{5,1},{9,13},{13,9},{2,6},{6,2},{1... | collective-permute-start | bytes 196616 | tf_op jit(solution)/shard_map/ppermute | solution.py:22
  34.3 1.8 %collective-permute-done.8.refs_3_ = bf16[256,128]{1,0:T(8,128)(2,1)S(1)} collective-permute-done((bf16[256,128]{1,0:T(8,128)(2,1)S(1)}, bf16[256,128]{1,0:T(8,128)(2,1)S(1)}, u32[]{:S(2)}, u32[]{:S(2)}) %collective-permute-start.8) | collective-permute-done | bytes 65568 | tf_op jit(solution)/shard_map/ppermute | solution.py:22
  36.0 1.3 %collective-permute-done.7.refs_2_ = bf16[256,128]{1,0:T(8,128)(2,1)S(1)} collective-permute-done((bf16[256,128]{1,0:T(8,128)(2,1)S(1)}, bf16[256,128]{1,0:T(8,128)(2,1)S(1)}, u32[]{:S(2)}, u32[]{:S(2)}) %collective-permute-start.7) | collective-permute-done | bytes 65568 | tf_op jit(solution)/shard_map/ppermute | solution.py:22
  37.4 0.0 collective-permute-done.6.refs_1_
  37.4 0.0 copy-start.1
  37.4 9.4 %copy-done.1 = bf16[8192,1792]{1,0:T(8,128)(2,1)S(1)} copy-done((bf16[8192,1792]{1,0:T(8,128)(2,1)S(1)}, bf16[8192,1792]{1,0:T(8,128)(2,1)}, u32[]{:S(2)}) %copy-start.1) | copy-done | bytes 29360152
  46.7 3.9 %project.1 = (f32[4,896]{1,0:T(4,128)S(1)}, f32[4,896]{1,0:T(4,128)S(1)}) custom-call(bf16[256,128]{1,0:T(8,128)(2,1)S(1)} %values.1.refs_0_, bf16[256,128]{1,0:T(8,128)(2,1)S(1)} %collective-permute-done.6.refs_1_, bf16[256,128]{1,0:T(8,128)(2,1)S(1)} %collective-permute-done.7.refs_2_, bf16[256,128]{1,0:T(8,128)(2,1)S(1)} %collective-permute-done.8.refs_3_, ...), custom_call_target="tpu_custom_call" | custom-call | tf_op jit(solution)/shard_map/project/pallas_call | solution.py:155
  50.6 1.5 %collective-permute-start.9 = (f32[4,896]{1,0:T(4,128)S(1)}, f32[4,896]{1,0:T(4,128)S(1)}, u32[]{:S(2)}, u32[]{:S(2)}) collective-permute-start(f32[4,896]{1,0:T(4,128)S(1)} %get-tuple-element.16), channel_id=1, source_target_pairs={{0,2},{2,0},{1,3},{3,1},{4,6},{6,4},{5,7},{7,5},{8,10},{10,8},{9,1... | collective-permute-start | bytes 43016 | tf_op jit(solution)/shard_map/ppermute | solution.py:22
  52.1 2.2 %collective-permute-done.9 = f32[4,896]{1,0:T(4,128)S(1)} collective-permute-done((f32[4,896]{1,0:T(4,128)S(1)}, f32[4,896]{1,0:T(4,128)S(1)}, u32[]{:S(2)}, u32[]{:S(2)}) %collective-permute-start.9) | collective-permute-done | bytes 14368 | tf_op jit(solution)/shard_map/ppermute | solution.py:22
  54.4 0.6 %fusion.1 = bf16[1,4,896]{2,1,0:T(4,128)(2,1)} fusion(f32[4,896]{1,0:T(4,128)S(1)} %get-tuple-element.15, f32[4,896]{1,0:T(4,128)S(1)} %collective-permute-done.9), kind=kLoop, calls=%fused_computation.7 | loop fusion | flops 7168 | bytes 35840 | tf_op jit(solution)/shard_map/broadcast_in_dim | solution.py:239
  (4 shorter events, 0.0 us)
Async XLA Ops:
  0.0 1.6 %copy-start = (bf16[64,128,128]{2,1,0:T(8,128)(2,1)S(1)}, bf16[64,128,128]{2,1,0:T(8,128)(2,1)}, u32[]{:S(2)}) copy-start(bf16[64,128,128]{2,1,0:T(8,128)(2,1)} %param.13) | copy-start | bytes 6291460
  0.0 9.5 %copy-start.5 = (s32[1,4,32]{2,1,0:T(4,128)S(1)}, s32[1,4,32]{2,1,0:T(4,128)}, u32[]{:S(2)}) copy-start(s32[1,4,32]{2,1,0:T(4,128)} %param.12) | copy-start | bytes 1540
  0.0 9.9 %copy-start.4 = (bf16[1,4,64,64]{3,2,1,0:T(8,128)(2,1)S(1)}, bf16[1,4,64,64]{3,2,1,0:T(8,128)(2,1)}, u32[]{:S(2)}) copy-start(bf16[1,4,64,64]{3,2,1,0:T(8,128)(2,1)} %param.9) | copy-start | bytes 98308
  3.1 7.6 %collective-permute-start.2 = (bf16[256,128]{1,0:T(8,128)(2,1)S(1)}, bf16[256,128]{1,0:T(8,128)(2,1)S(1)}, u32[]{:S(2)}, u32[]{:S(2)}) collective-permute-start(bf16[256,128]{1,0:T(8,128)(2,1)S(1)} %bitcast.15), channel_id=1, source_target_pairs={{0,12},{4,8},{8,4},{12,0},{1,13},{5,9},{9,5},{13,1},{2,14},{6,10},... | collective-permute-start | bytes 196616 | tf_op jit(solution)/shard_map/ppermute | solution.py:22
  8.1 5.6 %collective-permute-start.1 = (bf16[256,128]{1,0:T(8,128)(2,1)S(1)}, bf16[256,128]{1,0:T(8,128)(2,1)S(1)}, u32[]{:S(2)}, u32[]{:S(2)}) collective-permute-start(bf16[256,128]{1,0:T(8,128)(2,1)S(1)} %bitcast.16), channel_id=1, source_target_pairs={{0,8},{4,12},{8,0},{12,4},{1,9},{5,13},{9,1},{13,5},{2,10},{6,14},... | collective-permute-start | bytes 196616 | tf_op jit(solution)/shard_map/ppermute | solution.py:22
  8.1 5.6 %collective-permute-start = (bf16[256,128]{1,0:T(8,128)(2,1)S(1)}, bf16[256,128]{1,0:T(8,128)(2,1)S(1)}, u32[]{:S(2)}, u32[]{:S(2)}) collective-permute-start(bf16[256,128]{1,0:T(8,128)(2,1)S(1)} %bitcast.17), channel_id=1, source_target_pairs={{0,4},{4,0},{8,12},{12,8},{1,5},{5,1},{9,13},{13,9},{2,6},{6,2},{1... | collective-permute-start | bytes 196616 | tf_op jit(solution)/shard_map/ppermute | solution.py:22
  13.7 2.3 %copy-start.2 = (bf16[1,4096,576]{1,2,0:T(8,128)(2,1)S(1)}, bf16[1,4096,576]{1,2,0:T(8,128)(2,1)}, u32[]{:S(2)}) copy-start(bf16[1,4096,576]{1,2,0:T(8,128)(2,1)} %param.10) | copy-start | bytes 14155780
  16.1 13.3 %copy-start.3 = (bf16[64,128,128]{2,1,0:T(8,128)(2,1)S(1)}, bf16[64,128,128]{2,1,0:T(8,128)(2,1)}, u32[]{:S(2)}) copy-start(bf16[64,128,128]{2,1,0:T(8,128)(2,1)} %refs_4_.2) | copy-start | bytes 6291460
  19.8 4.8 %collective-permute-start.3 = (bf16[272,128]{1,0:T(8,128)(2,1)S(1)}, bf16[272,128]{1,0:T(8,128)(2,1)S(1)}, u32[]{:S(2)}, u32[]{:S(2)}) collective-permute-start(bf16[272,128]{1,0:T(8,128)(2,1)S(1)} %get-tuple-element.12), channel_id=1, source_target_pairs={{0,4},{4,0},{8,12},{12,8},{1,5},{5,1},{9,13},{13,9},{2,6},{6,2},{1... | collective-permute-start | bytes 208904 | tf_op jit(solution)/shard_map/ppermute | solution.py:22
  20.9 6.7 %collective-permute-start.4 = (bf16[272,128]{1,0:T(8,128)(2,1)S(1)}, bf16[272,128]{1,0:T(8,128)(2,1)S(1)}, u32[]{:S(2)}, u32[]{:S(2)}) collective-permute-start(bf16[272,128]{1,0:T(8,128)(2,1)S(1)} %get-tuple-element.13), channel_id=1, source_target_pairs={{0,8},{4,12},{8,0},{12,4},{1,9},{5,13},{9,1},{13,5},{2,10},{6,14},... | collective-permute-start | bytes 208904 | tf_op jit(solution)/shard_map/ppermute | solution.py:22
  23.1 6.2 %collective-permute-start.5 = (bf16[272,128]{1,0:T(8,128)(2,1)S(1)}, bf16[272,128]{1,0:T(8,128)(2,1)S(1)}, u32[]{:S(2)}, u32[]{:S(2)}) collective-permute-start(bf16[272,128]{1,0:T(8,128)(2,1)S(1)} %get-tuple-element.14), channel_id=1, source_target_pairs={{0,12},{4,8},{8,4},{12,0},{1,13},{5,9},{9,5},{13,1},{2,14},{6,10},... | collective-permute-start | bytes 208904 | tf_op jit(solution)/shard_map/ppermute | solution.py:22
  29.9 6.2 %collective-permute-start.8 = (bf16[256,128]{1,0:T(8,128)(2,1)S(1)}, bf16[256,128]{1,0:T(8,128)(2,1)S(1)}, u32[]{:S(2)}, u32[]{:S(2)}) collective-permute-start(bf16[256,128]{1,0:T(8,128)(2,1)S(1)} %values.1.refs_0_), channel_id=1, source_target_pairs={{0,12},{4,8},{8,4},{12,0},{1,13},{5,9},{9,5},{13,1},{2,14},{6,10},... | collective-permute-start | bytes 196616 | tf_op jit(solution)/shard_map/ppermute | solution.py:22
  30.9 6.5 %collective-permute-start.7 = (bf16[256,128]{1,0:T(8,128)(2,1)S(1)}, bf16[256,128]{1,0:T(8,128)(2,1)S(1)}, u32[]{:S(2)}, u32[]{:S(2)}) collective-permute-start(bf16[256,128]{1,0:T(8,128)(2,1)S(1)} %values.1.refs_0_), channel_id=1, source_target_pairs={{0,8},{4,12},{8,0},{12,4},{1,9},{5,13},{9,1},{13,5},{2,10},{6,14},... | collective-permute-start | bytes 196616 | tf_op jit(solution)/shard_map/ppermute | solution.py:22
  31.4 6.0 %collective-permute-start.6 = (bf16[256,128]{1,0:T(8,128)(2,1)S(1)}, bf16[256,128]{1,0:T(8,128)(2,1)S(1)}, u32[]{:S(2)}, u32[]{:S(2)}) collective-permute-start(bf16[256,128]{1,0:T(8,128)(2,1)S(1)} %values.1.refs_0_), channel_id=1, source_target_pairs={{0,4},{4,0},{8,12},{12,8},{1,5},{5,1},{9,13},{13,9},{2,6},{6,2},{1... | collective-permute-start | bytes 196616 | tf_op jit(solution)/shard_map/ppermute | solution.py:22
  37.4 9.4 %copy-start.1 = (bf16[8192,1792]{1,0:T(8,128)(2,1)S(1)}, bf16[8192,1792]{1,0:T(8,128)(2,1)}, u32[]{:S(2)}) copy-start(bf16[8192,1792]{1,0:T(8,128)(2,1)} %refs_4_.3) | copy-start | bytes 88080384
  50.6 3.7 %collective-permute-start.9 = (f32[4,896]{1,0:T(4,128)S(1)}, f32[4,896]{1,0:T(4,128)S(1)}, u32[]{:S(2)}, u32[]{:S(2)}) collective-permute-start(f32[4,896]{1,0:T(4,128)S(1)} %get-tuple-element.16), channel_id=1, source_target_pairs={{0,2},{2,0},{1,3},{3,1},{4,6},{6,4},{5,7},{7,5},{8,10},{10,8},{9,1... | collective-permute-start | bytes 43016 | tf_op jit(solution)/shard_map/ppermute | solution.py:22

commit v3 on v2

--- a/solution.py
+++ b/solution.py
@@ -15,6 +15,11 @@
 HIDDEN = -1e30
 MIB = 1024 * 1024
 VMEM = pl.BlockSpec(memory_space=pltpu.VMEM)
+HBM = pl.BlockSpec(memory_space=pltpu.HBM)
+
+
+def spans(microseconds):
+    return pl.CostEstimate(flops=int(microseconds * 1e9), bytes_accessed=0, transcendentals=0)
 
 
 def swap(value, axis, step):
@@ -28,6 +33,105 @@
     middle = rest.astype(jnp.bfloat16)
     low = (rest - middle.astype(jnp.float32)).astype(jnp.bfloat16)
     return [part.astype(jnp.float32) for part in (high, middle, low)]
+
+
+def by_head(value, rows_ref):
+    drafts, heads, _ = value.shape
+    for draft in range(drafts):
+        rows_ref[pl.ds(draft, heads, stride=drafts), :] = value[draft].astype(jnp.float32)
+
+
+def pair_products(left, heads, first, last, drafts, store):
+    pair, width = 2 * drafts, heads.shape[2]
+    upper = lax.broadcasted_iota(jnp.int32, (pair, width), 0) < drafts
+    for head in range(first, last, 2):
+        both = jnp.concatenate([heads[head], heads[head + 1]], axis=1)
+        at = slice(head * drafts, head * drafts + pair)
+        found = jnp.dot(left[at], both, preferred_element_type=jnp.float32)
+        store[at, :] = jnp.where(upper, found[:, :width], found[:, width:]).astype(store.dtype)
+
+
+def queries_kernel(query, key_absorb, out, query_here, held, rows_ref, arrived):
+    drafts, heads, _ = query.shape
+    parts = arrived.shape[0] - 1
+    each = heads // parts
+    copies = [pltpu.make_async_copy(query, query_here, arrived.at[parts])]
+    for i in range(parts):
+        at = pl.ds(i * each, each)
+        copies.append(pltpu.make_async_copy(key_absorb.at[at], held.at[at], arrived.at[i]))
+    for copy in copies:
+        copy.start()
+    copies[0].wait()
+    by_head(query_here[...], rows_ref)
+    left = rows_ref[...].astype(jnp.bfloat16)
+    for i in range(parts):
+        copies[1 + i].wait()
+        pair_products(left, held, i * each, (i + 1) * each, drafts, out)
+
+
+def queries_of(query, key_absorb):
+    drafts, heads, nope = query.shape
+    rows, width = drafts * heads, key_absorb.shape[2]
+    return pl.pallas_call(
+        queries_kernel,
+        out_shape=pltpu.VMEM((rows, width), jnp.bfloat16),
+        in_specs=[HBM] * 2,
+        out_specs=VMEM,
+        scratch_shapes=[
+            pltpu.VMEM(query.shape, query.dtype),
+            pltpu.VMEM(key_absorb.shape, key_absorb.dtype),
+            pltpu.VMEM((rows, nope), jnp.float32),
+            pltpu.SemaphoreType.DMA((min(4, heads // 2) + 1,)),
+        ],
+        compiler_params=pltpu.CompilerParams(vmem_limit_bytes=60 * MIB),
+        name="queries",
+    )(query, key_absorb)
+
+
+def prepare_kernel(
+    lengths, ids_there, rope_there, bias, rope_out, block_ids, query_rope, rows_ref, arrived
+):
+    drafts, chosen = block_ids.shape
+    tokens = bias.shape[1]
+    ids_copy = pltpu.make_async_copy(ids_there, block_ids, arrived.at[0])
+    rope_copy = pltpu.make_async_copy(rope_there, query_rope, arrived.at[1])
+    ids_copy.start()
+    rope_copy.start()
+    ids_copy.wait()
+    ids = jnp.concatenate([block_ids[...]] * (8 // drafts), axis=0)
+    position = lax.axis_index("ctx") * tokens + lax.broadcasted_iota(jnp.int32, (8, tokens), 1)
+    block = position // BLK
+    found = block == ids[:, :1]
+    for i in range(1, chosen):
+        found |= block == ids[:, i : i + 1]
+    draft = lax.broadcasted_iota(jnp.int32, (8, tokens), 0) % drafts
+    visible = found & (position <= lengths[0] - drafts + draft)
+    bias[...] = jnp.where(visible, 0.0, HIDDEN)
+    rope_copy.wait()
+    by_head(query_rope[...], rows_ref)
+    rope_out[...] = rows_ref[...].astype(jnp.bfloat16)
+
+
+def prepare(lengths, block_ids, query_rope, tokens):
+    drafts, heads, rope = query_rope.shape
+    return pl.pallas_call(
+        prepare_kernel,
+        out_shape=[
+            jax.ShapeDtypeStruct((8, tokens), jnp.float32),
+            jax.ShapeDtypeStruct((drafts * heads, rope), jnp.bfloat16),
+        ],
+        in_specs=[pl.BlockSpec(memory_space=pltpu.SMEM), HBM, HBM],
+        out_specs=[VMEM] * 2,
+        scratch_shapes=[
+            pltpu.VMEM(block_ids.shape, block_ids.dtype),
+            pltpu.VMEM(query_rope.shape, query_rope.dtype),
+            pltpu.VMEM((drafts * heads, rope), jnp.float32),
+            pltpu.SemaphoreType.DMA((2,)),
+        ],
+        compiler_params=pltpu.CompilerParams(vmem_limit_bytes=4 * MIB),
+        cost_estimate=spans(12),
+        name="prepare",
+    )(lengths, block_ids, query_rope)
 
 
 def attend_kernel(*refs, count, scale):
@@ -80,6 +184,7 @@
             pltpu.VMEM((rows, count * width), jnp.float32),
         ],
         compiler_params=pltpu.CompilerParams(vmem_limit_bytes=16 * MIB),
+        cost_estimate=spans(40),
         name="attend",
     )(*pieces, rope, cache, bias)
 
@@ -110,15 +215,7 @@
         column = jnp.broadcast_to(factor / total, (width, rows)).T
         latent += block[:rows, :].astype(jnp.float32) * column
     latent = latent.astype(jnp.bfloat16)
-    pair = 2 * drafts
-    first = lax.broadcasted_iota(jnp.int32, (pair, value_width), 0) < drafts
-    for head in range(0, heads, 2):
-        both = jnp.concatenate([value_absorb[head], value_absorb[head + 1]], axis=1)
-        at = slice(head * drafts, head * drafts + pair)
-        found = jnp.dot(latent[at], both, preferred_element_type=jnp.float32)
-        out[at, :] = jnp.where(first, found[:, :value_width], found[:, value_width:]).astype(
-            jnp.bfloat16
-        )
+    pair_products(latent, value_absorb, 0, heads, drafts, out)
 
 
 def values_of(blocks, value_absorb, drafts):
@@ -133,49 +230,55 @@
     )(*blocks, value_absorb)
 
 
-def project_kernel(*refs, drafts):
-    partials, weight, mine, theirs, flat, found = refs[:-5], *refs[-5:]
+def half_of(weight, other):
+    half = weight.shape[1] // 2
+    me = lax.axis_index("head")
+    at = pl.multiple_of((1 - me if other else me) * half, half)
+    return weight[:, pl.ds(at, half)]
+
+
+def theirs_kernel(*refs, drafts):
+    partials, (weight, theirs, flat, rows_ref) = refs[:-4], refs[-4:]
     rows, value_width = partials[0].shape
     summed = sum(partial[...].astype(jnp.float32) for partial in partials)
     for head in range(rows // drafts):
-        flat[:, head * value_width : (head + 1) * value_width] = summed[
+        rows_ref[:, head * value_width : (head + 1) * value_width] = summed[
             head * drafts : (head + 1) * drafts
         ]
-    found[...] = jnp.dot(
-        flat[...].astype(jnp.bfloat16), weight[...], preferred_element_type=jnp.float32
-    )
-    half = mine.shape[1]
-    me = lax.axis_index("head")
-    mine[...] = found[:, pl.ds(pl.multiple_of(me * half, half), half)]
-    theirs[...] = found[:, pl.ds(pl.multiple_of((1 - me) * half, half), half)]
-
-
-def project(partials, weight, drafts):
+    flat[...] = rows_ref[...].astype(jnp.bfloat16)
+    theirs[...] = jnp.dot(flat[...], half_of(weight, True), preferred_element_type=jnp.float32)
+
+
+def theirs_of(partials, weight, drafts):
     depth, width = weight.shape
     return pl.pallas_call(
-        functools.partial(project_kernel, drafts=drafts),
-        out_shape=[jax.ShapeDtypeStruct((drafts, width // 2), jnp.float32)] * 2,
+        functools.partial(theirs_kernel, drafts=drafts),
+        out_shape=[
+            jax.ShapeDtypeStruct((drafts, width // 2), jnp.float32),
+            jax.ShapeDtypeStruct((drafts, depth), jnp.bfloat16),
+        ],
         in_specs=[VMEM] * (len(partials) + 1),
         out_specs=[VMEM] * 2,
-        scratch_shapes=[
-            pltpu.VMEM((drafts, depth), jnp.float32),
-            pltpu.VMEM((drafts, width), jnp.float32),
-        ],
+        scratch_shapes=[pltpu.VMEM((drafts, depth), jnp.float32)],
         compiler_params=pltpu.CompilerParams(vmem_limit_bytes=4 * MIB),
-        name="project",
+        name="theirs",
     )(*partials, weight)
 
 
-def visibility(lengths, block_ids, tokens):
-    drafts = block_ids.shape[1]
-    first = lax.axis_index("ctx") * tokens
-    position = first + jnp.arange(tokens, dtype=jnp.int32)
-    blocks = first // BLK + jnp.arange(tokens // BLK, dtype=jnp.int32)
-    chosen = jnp.any(block_ids[0][:, :, None] == blocks[None, None, :], axis=1)
-    limit = lengths[0] - drafts + jnp.arange(drafts, dtype=jnp.int32)
-    visible = jnp.repeat(chosen, BLK, axis=1) & (position[None, :] <= limit[:, None])
-    bias = jnp.where(visible, 0.0, HIDDEN).astype(jnp.float32)
-    return jnp.concatenate([bias] * (8 // drafts), axis=0)
+def mine_kernel(flat, weight, mine):
+    mine[...] = jnp.dot(flat[...], half_of(weight, False), preferred_element_type=jnp.float32)
+
+
+def mine_of(flat, weight):
+    return pl.pallas_call(
+        mine_kernel,
+        out_shape=jax.ShapeDtypeStruct((flat.shape[0], weight.shape[1] // 2), jnp.float32),
+        in_specs=[VMEM] * 2,
+        out_specs=VMEM,
+        compiler_params=pltpu.CompilerParams(vmem_limit_bytes=4 * MIB),
+        cost_estimate=spans(2),
+        name="mine",
+    )(flat, weight)
 
 
 def combine_many(block, rows):
@@ -206,12 +309,8 @@
     peers = lax.axis_size("ctx")
     few = peers <= FEW and lax.axis_size("head") == 2 and key_absorb.shape[2] == LANES
 
-    q_piece = jnp.einsum(
-        "tho,hoc->htc", query_nope[0], key_absorb, preferred_element_type=jnp.float32
-    ).astype(jnp.bfloat16)
-    q_piece = q_piece.reshape(rows, -1)
-    rope_rows = query_rope[0].transpose(1, 0, 2).reshape(rows, rope)
-    bias = visibility(lengths, block_ids, tokens)
+    q_piece = queries_of(query_nope[0], key_absorb)
+    bias, rope_rows = prepare(lengths, block_ids[0], query_rope[0], tokens)
     cache = latent_cache[0].T
     if few:
         pieces = [q_piece] + [swap(q_piece, "ctx", step) for step in range(1, peers)]
@@ -219,8 +318,8 @@
         blocks = [blocks[0]] + [swap(blocks[step], "ctx", step) for step in range(1, peers)]
         partial = values_of(blocks, value_absorb, drafts)
         partials = [partial] + [swap(partial, "ctx", step) for step in range(1, peers)]
-        mine, theirs = project(partials, output_weight, drafts)
-        summed = mine + swap(theirs, "head", 1)
+        theirs, flat = theirs_of(partials, output_weight, drafts)
+        summed = mine_of(flat, output_weight) + swap(theirs, "head", 1)
     else:
         queries = lax.all_gather(q_piece, "ctx", axis=1, tiled=True)
         block = attend([queries], rope_rows, cache, bias, scale)[0]

time: 55.2 us -> 41.1 us (0.74)
  local copies, waits for them, and re-layouts: 13.6 us -> 1.56 us
  waiting for transfers between devices: 14.2 us -> 10.8 us
  Pallas kernels: 8.09 us -> 10.9 us
  matrix products: 1.48 us -> 0 us
    unnamed x12 -> x22, local copies, waits for them, and re-layouts: 13.3 us -> 1.56 us
    ppermute x10, waiting for transfers between devices: 14.2 us -> 10.8 us  [swap(): return lax.ppermute(value, axis, [(i, i ^ step) for i in range(count)])]
    pallas_call x1 -> x4, Pallas kernels: 3.9 us -> 6.72 us  [the longest x1 2.04 us: theirs_of(): pl.pallas_call(functools.partial(theirs_kernel, drafts=drafts), out_shape...]
    dot_general x1 -> x0, matrix products: 1.48 us -> none  [local(): jnp.einsum('tho,hoc->htc', query_nope[0], key_absorb, preferred_element_t...]
  transfers between devices with their start and end apart: 10 -> 10, of which waited for: 8 -> 7; matrix products, arithmetic and copies ran while one was open for 1% -> 0% of each run, Pallas kernels for 0% -> 7%
where the time goes in v3:
time: 41.1 us; the launch traced here: 40.9 us
  starting transfers between devices  16.2 us (39%)
  Pallas kernels  10.9 us (27%)
  waiting for transfers between devices  10.8 us (26%)
  local copies, waits for them, and re-layouts  1.56 us (4%)
  between operations  0.82 us (2%)
  other arithmetic  0.6 us (1%)
    ppermute x10, starting transfers between devices, swap(): return lax.ppermute(value, axis, [(i, i ^ step) for i in range(count)])  16.2 us
    ppermute x10, waiting for transfers between devices, swap(): return lax.ppermute(value, axis, [(i, i ^ step) for i in range(count)])  10.8 us
    pallas_call x1, Pallas kernels, attend(): pl.pallas_call(functools.partial(attend_kernel, count=count, scale=scale)...  3.69 us
    pallas_call x1, Pallas kernels, theirs_of(): pl.pallas_call(functools.partial(theirs_kernel, drafts=drafts), out_shape...  2.04 us
    pallas_call x1, Pallas kernels, mine_of(): pl.pallas_call(mine_kernel, out_shape=jax.ShapeDtypeStruct((flat.shape[0]...  2 us
    pallas_call x1, Pallas kernels, queries_of(): pl.pallas_call(queries_kernel, out_shape=pltpu.VMEM((rows, width), jnp.bf...  1.86 us
    unnamed x22, local copies, waits for them, and re-layouts  1.56 us
  transfers between devices with their start and end apart: 10, of which 7 were waited for; matrix products, arithmetic and copies ran while one was open for 0% of the time, Pallas kernels for 7%

profile of v3, /device:TPU:0, one launch (start us, length us, event | category | flops | bytes accessed | tf_op | source)
XLA Modules:
  0.0 40.9 jit_solution(15052953340007927282)
XLA Ops:
  0.0 1.9 %queries.1.refs_0_ = bf16[256,128]{1,0:T(8,128)(2,1)S(1)} custom-call(bf16[4,64,128]{2,1,0:T(8,128)(2,1)} %bitcast.13, bf16[64,128,128]{2,1,0:T(8,128)(2,1)} %key_absorb.1), custom_call_target="tpu_custom_call" | custom-call | tf_op jit(solution)/shard_map/queries/pallas_call | solution.py:75
  1.9 5.1 %collective-permute-start.2 = (bf16[256,128]{1,0:T(8,128)(2,1)S(1)}, bf16[256,128]{1,0:T(8,128)(2,1)S(1)}, u32[]{:S(2)}, u32[]{:S(2)}) collective-permute-start(bf16[256,128]{1,0:T(8,128)(2,1)S(1)} %queries.1.refs_0_), channel_id=1, source_target_pairs={{0,12},{4,8},{8,4},{12,0},{1,13},{5,9},{9,5},{13,1},{2,14},{6,10},... | collective-permute-start | bytes 196616 | tf_op jit(solution)/shard_map/ppermute | solution.py:27
  7.0 0.0 collective-permute-start.1
  7.0 0.6 %collective-permute-start = (bf16[256,128]{1,0:T(8,128)(2,1)S(1)}, bf16[256,128]{1,0:T(8,128)(2,1)S(1)}, u32[]{:S(2)}, u32[]{:S(2)}) collective-permute-start(bf16[256,128]{1,0:T(8,128)(2,1)S(1)} %queries.1.refs_0_), channel_id=1, source_target_pairs={{0,4},{4,0},{8,12},{12,8},{1,5},{5,1},{9,13},{13,9},{2,6},{6,2},{1... | collective-permute-start | bytes 196616 | tf_op jit(solution)/shard_map/ppermute | solution.py:27
  8.3 0.0 copy-start.2
  8.3 0.8 %copy-done.2 = bf16[1,4,64,64]{3,2,1,0:T(8,128)(2,1)S(1)} copy-done((bf16[1,4,64,64]{3,2,1,0:T(8,128)(2,1)S(1)}, bf16[1,4,64,64]{3,2,1,0:T(8,128)(2,1)}, u32[]{:S(2)}) %copy-start.2) | copy-done | bytes 32792
  9.1 0.0 copy-start.3
  9.1 0.7 %copy-done.3 = s32[1,4,32]{2,1,0:T(4,128)S(1)} copy-done((s32[1,4,32]{2,1,0:T(4,128)S(1)}, s32[1,4,32]{2,1,0:T(4,128)}, u32[]{:S(2)}) %copy-start.3) | copy-done | bytes 536
  9.8 0.0 copy-start.1
  9.8 0.8 %prepare.1 = (f32[8,4096]{1,0:T(8,128)S(1)}, bf16[256,64]{1,0:T(8,128)(2,1)S(1)}) custom-call(s32[1]{0:T(128)S(6)} %copy.9.lengths, s32[4,32]{1,0:T(4,128)S(1)} %bitcast.12, bf16[4,64,64]{2,1,0:T(8,128)(2,1)S(1)} %bitcast.11), custom_call_target="tpu_custom_call" | custom-call | flops 12000000000 | tf_op jit(solution)/shard_map/prepare/pallas_call | solution.py:117
  10.6 0.0 collective-permute-done.2.refs_3_
  10.6 1.9 %collective-permute-done.1.refs_2_ = bf16[256,128]{1,0:T(8,128)(2,1)S(1)} collective-permute-done((bf16[256,128]{1,0:T(8,128)(2,1)S(1)}, bf16[256,128]{1,0:T(8,128)(2,1)S(1)}, u32[]{:S(2)}, u32[]{:S(2)}) %collective-permute-start.1) | collective-permute-done | bytes 65568 | tf_op jit(solution)/shard_map/ppermute | solution.py:27
  12.6 0.0 collective-permute-done.refs_1_
  12.6 0.0 copy-done.1
  12.6 0.0 copy-start
  12.6 0.0 slice-start.1
  12.6 0.0 slice-start.2
  12.6 0.0 slice-start.3
  12.6 0.0 slice-start.4
  12.7 0.0 slice-start.5
  12.7 0.0 slice-start.6
  12.7 3.7 %attend.1 = (bf16[272,128]{1,0:T(8,128)(2,1)S(1)}, bf16[272,128]{1,0:T(8,128)(2,1)S(1)}, bf16[272,128]{1,0:T(8,128)(2,1)S(1)}, bf16[272,128]{1,0:T(8,128)(2,1)S(1)}) custom-call(bf16[256,128]{1,0:T(8,128)(2,1)S(1)} %queries.1.refs_0_, bf16[256,128]{1,0:T(8,128)(2,1)S(1)} %collective-permute-done.refs_1_, ...), custom_call_target="tpu_custom_call" | custom-call | flops 40000000000 | tf_op jit(solution)/shard_map/attend/pallas_call | solution.py:177
  16.4 1.1 %collective-permute-start.3 = (bf16[272,128]{1,0:T(8,128)(2,1)S(1)}, bf16[272,128]{1,0:T(8,128)(2,1)S(1)}, u32[]{:S(2)}, u32[]{:S(2)}) collective-permute-start(bf16[272,128]{1,0:T(8,128)(2,1)S(1)} %get-tuple-element.16), channel_id=1, source_target_pairs={{0,4},{4,0},{8,12},{12,8},{1,5},{5,1},{9,13},{13,9},{2,6},{6,2},{1... | collective-permute-start | bytes 208904 | tf_op jit(solution)/shard_map/ppermute | solution.py:27
  17.5 2.8 %collective-permute-start.4 = (bf16[272,128]{1,0:T(8,128)(2,1)S(1)}, bf16[272,128]{1,0:T(8,128)(2,1)S(1)}, u32[]{:S(2)}, u32[]{:S(2)}) collective-permute-start(bf16[272,128]{1,0:T(8,128)(2,1)S(1)} %get-tuple-element.17), channel_id=1, source_target_pairs={{0,8},{4,12},{8,0},{12,4},{1,9},{5,13},{9,1},{13,5},{2,10},{6,14},... | collective-permute-start | bytes 208904 | tf_op jit(solution)/shard_map/ppermute | solution.py:27
  20.3 0.5 %collective-permute-start.5 = (bf16[272,128]{1,0:T(8,128)(2,1)S(1)}, bf16[272,128]{1,0:T(8,128)(2,1)S(1)}, u32[]{:S(2)}, u32[]{:S(2)}) collective-permute-start(bf16[272,128]{1,0:T(8,128)(2,1)S(1)} %get-tuple-element.18), channel_id=1, source_target_pairs={{0,12},{4,8},{8,4},{12,0},{1,13},{5,9},{9,5},{13,1},{2,14},{6,10},... | collective-permute-start | bytes 208904 | tf_op jit(solution)/shard_map/ppermute | solution.py:27
  20.8 0.5 %collective-permute-done.3.refs_1_ = bf16[272,128]{1,0:T(8,128)(2,1)S(1)} collective-permute-done((bf16[272,128]{1,0:T(8,128)(2,1)S(1)}, bf16[272,128]{1,0:T(8,128)(2,1)S(1)}, u32[]{:S(2)}, u32[]{:S(2)}) %collective-permute-start.3) | collective-permute-done | bytes 69664 | tf_op jit(solution)/shard_map/ppermute | solution.py:27
  21.3 3.2 %collective-permute-done.4.refs_2_ = bf16[272,128]{1,0:T(8,128)(2,1)S(1)} collective-permute-done((bf16[272,128]{1,0:T(8,128)(2,1)S(1)}, bf16[272,128]{1,0:T(8,128)(2,1)S(1)}, u32[]{:S(2)}, u32[]{:S(2)}) %collective-permute-start.4) | collective-permute-done | bytes 69664 | tf_op jit(solution)/shard_map/ppermute | solution.py:27
  24.5 1.9 %collective-permute-done.5.refs_3_ = bf16[272,128]{1,0:T(8,128)(2,1)S(1)} collective-permute-done((bf16[272,128]{1,0:T(8,128)(2,1)S(1)}, bf16[272,128]{1,0:T(8,128)(2,1)S(1)}, u32[]{:S(2)}, u32[]{:S(2)}) %collective-permute-start.5) | collective-permute-done | bytes 69664 | tf_op jit(solution)/shard_map/ppermute | solution.py:27
  26.4 0.0 copy-done
  26.4 0.5 %values.1.refs_0_ = bf16[256,128]{1,0:T(8,128)(2,1)S(1)} custom-call(bf16[272,128]{1,0:T(8,128)(2,1)S(1)} %get-tuple-element.15.refs_0_, bf16[272,128]{1,0:T(8,128)(2,1)S(1)} %collective-permute-done.3.refs_1_, bf16[272,128]{1,0:T(8,128)(2,1)S(1)} %collective-permute-done.4.refs_2_, bf16[272,128]{1,0:T(8,128)(2,1)S(1)} %collective-permute-done.5.refs_3_, ...), custom_call_target="tpu_custom_call" | custom-call | tf_op jit(solution)/shard_map/values/pallas_call | solution.py:223
  26.9 1.2 %collective-permute-start.8 = (bf16[256,128]{1,0:T(8,128)(2,1)S(1)}, bf16[256,128]{1,0:T(8,128)(2,1)S(1)}, u32[]{:S(2)}, u32[]{:S(2)}) collective-permute-start(bf16[256,128]{1,0:T(8,128)(2,1)S(1)} %values.1.refs_0_), channel_id=1, source_target_pairs={{0,12},{4,8},{8,4},{12,0},{1,13},{5,9},{9,5},{13,1},{2,14},{6,10},... | collective-permute-start | bytes 196616 | tf_op jit(solution)/shard_map/ppermute | solution.py:27
  28.1 0.0 collective-permute-start.7
  28.1 3.3 %collective-permute-start.6 = (bf16[256,128]{1,0:T(8,128)(2,1)S(1)}, bf16[256,128]{1,0:T(8,128)(2,1)S(1)}, u32[]{:S(2)}, u32[]{:S(2)}) collective-permute-start(bf16[256,128]{1,0:T(8,128)(2,1)S(1)} %values.1.refs_0_), channel_id=1, source_target_pairs={{0,4},{4,0},{8,12},{12,8},{1,5},{5,1},{9,13},{13,9},{2,6},{6,2},{1... | collective-permute-start | bytes 196616 | tf_op jit(solution)/shard_map/ppermute | solution.py:27
  31.3 1.7 %collective-permute-done.8.refs_3_ = bf16[256,128]{1,0:T(8,128)(2,1)S(1)} collective-permute-done((bf16[256,128]{1,0:T(8,128)(2,1)S(1)}, bf16[256,128]{1,0:T(8,128)(2,1)S(1)}, u32[]{:S(2)}, u32[]{:S(2)}) %collective-permute-start.8) | collective-permute-done | bytes 65568 | tf_op jit(solution)/shard_map/ppermute | solution.py:27
  33.1 1.3 %collective-permute-done.7.refs_2_ = bf16[256,128]{1,0:T(8,128)(2,1)S(1)} collective-permute-done((bf16[256,128]{1,0:T(8,128)(2,1)S(1)}, bf16[256,128]{1,0:T(8,128)(2,1)S(1)}, u32[]{:S(2)}, u32[]{:S(2)}) %collective-permute-start.7) | collective-permute-done | bytes 65568 | tf_op jit(solution)/shard_map/ppermute | solution.py:27
  34.4 0.0 collective-permute-done.6.refs_1_
  34.4 0.0 slice-done
  34.4 0.0 slice-done.1
  34.4 0.0 slice-done.2
  34.4 0.0 slice-done.3
  34.4 0.0 slice-done.4
  34.5 0.0 slice-done.5
  34.5 0.0 slice-done.6
  34.5 2.0 %theirs.1 = (f32[4,896]{1,0:T(4,128)S(1)}, bf16[4,8192]{1,0:T(4,128)(2,1)S(1)}) custom-call(bf16[256,128]{1,0:T(8,128)(2,1)S(1)} %values.1.refs_0_, bf16[256,128]{1,0:T(8,128)(2,1)S(1)} %collective-permute-done.6.refs_1_, bf16[256,128]{1,0:T(8,128)(2,1)S(1)} %collective-permute-done.7.refs_2_, bf16[256,128]{1,0:T(8,128)(2,1)S(1)} %collective-permute-done.8.refs_3_, ...), custom_call_target="tpu_custom_call" | custom-call | tf_op jit(solution)/shard_map/theirs/pallas_call | solution.py:254
  36.5 1.5 %collective-permute-start.9 = (f32[4,896]{1,0:T(4,128)S(1)}, f32[4,896]{1,0:T(4,128)S(1)}, u32[]{:S(2)}, u32[]{:S(2)}) collective-permute-start(f32[4,896]{1,0:T(4,128)S(1)} %get-tuple-element.20), channel_id=1, source_target_pairs={{0,2},{2,0},{1,3},{3,1},{4,6},{6,4},{5,7},{7,5},{8,10},{10,8},{9,1... | collective-permute-start | bytes 43016 | tf_op jit(solution)/shard_map/ppermute | solution.py:27
  38.0 2.0 %mine.1 = f32[4,896]{1,0:T(4,128)S(1)} custom-call(bf16[4,8192]{1,0:T(4,128)(2,1)S(1)} %get-tuple-element.19.flat, bf16[8192,1792]{1,0:T(8,128)(2,1)S(1)} %bitcast.9), custom_call_target="tpu_custom_call" | custom-call | flops 2000000000 | tf_op jit(solution)/shard_map/mine/pallas_call | solution.py:273
  40.1 0.2 collective-permute-done.9
  40.3 0.6 %fusion = bf16[1,4,896]{2,1,0:T(4,128)(2,1)} fusion(f32[4,896]{1,0:T(4,128)S(1)} %mine.1, f32[4,896]{1,0:T(4,128)S(1)} %collective-permute-done.9), kind=kLoop, calls=%fused_computation.1 | loop fusion | flops 7168 | bytes 35840 | tf_op jit(solution)/shard_map/broadcast_in_dim | solution.py:338
  (2 shorter events, 0.0 us)
Async XLA Ops:
  1.9 8.8 %collective-permute-start.2 = (bf16[256,128]{1,0:T(8,128)(2,1)S(1)}, bf16[256,128]{1,0:T(8,128)(2,1)S(1)}, u32[]{:S(2)}, u32[]{:S(2)}) collective-permute-start(bf16[256,128]{1,0:T(8,128)(2,1)S(1)} %queries.1.refs_0_), channel_id=1, source_target_pairs={{0,12},{4,8},{8,4},{12,0},{1,13},{5,9},{9,5},{13,1},{2,14},{6,10},... | collective-permute-start | bytes 196616 | tf_op jit(solution)/shard_map/ppermute | solution.py:27
  7.0 5.6 %collective-permute-start.1 = (bf16[256,128]{1,0:T(8,128)(2,1)S(1)}, bf16[256,128]{1,0:T(8,128)(2,1)S(1)}, u32[]{:S(2)}, u32[]{:S(2)}) collective-permute-start(bf16[256,128]{1,0:T(8,128)(2,1)S(1)} %queries.1.refs_0_), channel_id=1, source_target_pairs={{0,8},{4,12},{8,0},{12,4},{1,9},{5,13},{9,1},{13,5},{2,10},{6,14},... | collective-permute-start | bytes 196616 | tf_op jit(solution)/shard_map/ppermute | solution.py:27
  7.0 5.6 %collective-permute-start = (bf16[256,128]{1,0:T(8,128)(2,1)S(1)}, bf16[256,128]{1,0:T(8,128)(2,1)S(1)}, u32[]{:S(2)}, u32[]{:S(2)}) collective-permute-start(bf16[256,128]{1,0:T(8,128)(2,1)S(1)} %queries.1.refs_0_), channel_id=1, source_target_pairs={{0,4},{4,0},{8,12},{12,8},{1,5},{5,1},{9,13},{13,9},{2,6},{6,2},{1... | collective-permute-start | bytes 196616 | tf_op jit(solution)/shard_map/ppermute | solution.py:27
  8.3 0.8 %copy-start.2 = (bf16[1,4,64,64]{3,2,1,0:T(8,128)(2,1)S(1)}, bf16[1,4,64,64]{3,2,1,0:T(8,128)(2,1)}, u32[]{:S(2)}) copy-start(bf16[1,4,64,64]{3,2,1,0:T(8,128)(2,1)} %param.9) | copy-start | bytes 98308
  9.1 0.7 %copy-start.3 = (s32[1,4,32]{2,1,0:T(4,128)S(1)}, s32[1,4,32]{2,1,0:T(4,128)}, u32[]{:S(2)}) copy-start(s32[1,4,32]{2,1,0:T(4,128)} %param.12) | copy-start | bytes 1540
  9.8 2.8 %copy-start.1 = (bf16[1,4096,576]{1,2,0:T(8,128)(2,1)S(1)}, bf16[1,4096,576]{1,2,0:T(8,128)(2,1)}, u32[]{:S(2)}) copy-start(bf16[1,4096,576]{1,2,0:T(8,128)(2,1)} %param.10) | copy-start | bytes 14155780
  12.6 21.8 %slice-start = ((s8[29360128]{0:T(1024)(128)(4,1)}), s8[4194304]{0:T(1024)(128)(4,1)S(1)}, s32[]{:S(2)}) async-start(s8[29360128]{0:T(1024)(128)(4,1)} %bitcast.8), calls=%async_computation | async-start | bytes 8388608
  12.6 13.8 %copy-start = (bf16[64,128,128]{2,1,0:T(8,128)(2,1)S(1)}, bf16[64,128,128]{2,1,0:T(8,128)(2,1)}, u32[]{:S(2)}) copy-start(bf16[64,128,128]{2,1,0:T(8,128)(2,1)} %refs_4_.2) | copy-start | bytes 6291460
  12.6 21.8 %slice-start.1 = ((s8[29360128]{0:T(1024)(128)(4,1)}), s8[4194304]{0:T(1024)(128)(4,1)S(1)}, s32[]{:S(2)}) async-start(s8[29360128]{0:T(1024)(128)(4,1)} %bitcast.8), calls=%async_computation.1 | async-start | bytes 8388608
  12.6 21.8 %slice-start.2 = ((s8[29360128]{0:T(1024)(128)(4,1)}), s8[4194304]{0:T(1024)(128)(4,1)S(1)}, s32[]{:S(2)}) async-start(s8[29360128]{0:T(1024)(128)(4,1)} %bitcast.8), calls=%async_computation.2 | async-start | bytes 8388608
  12.6 21.8 %slice-start.3 = ((s8[29360128]{0:T(1024)(128)(4,1)}), s8[4194304]{0:T(1024)(128)(4,1)S(1)}, s32[]{:S(2)}) async-start(s8[29360128]{0:T(1024)(128)(4,1)} %bitcast.8), calls=%async_computation.3 | async-start | bytes 8388608
  12.6 21.8 %slice-start.4 = ((s8[29360128]{0:T(1024)(128)(4,1)}), s8[4194304]{0:T(1024)(128)(4,1)S(1)}, s32[]{:S(2)}) async-start(s8[29360128]{0:T(1024)(128)(4,1)} %bitcast.8), calls=%async_computation.4 | async-start | bytes 8388608
  12.7 21.8 %slice-start.5 = ((s8[29360128]{0:T(1024)(128)(4,1)}), s8[4194304]{0:T(1024)(128)(4,1)S(1)}, s32[]{:S(2)}) async-start(s8[29360128]{0:T(1024)(128)(4,1)} %bitcast.8), calls=%async_computation.5 | async-start | bytes 8388608
  12.7 21.8 %slice-start.6 = ((s8[29360128]{0:T(1024)(128)(4,1)}), s8[4194304]{0:T(1024)(128)(4,1)S(1)}, s32[]{:S(2)}) async-start(s8[29360128]{0:T(1024)(128)(4,1)} %bitcast.8), calls=%async_computation.6 | async-start | bytes 8388608
  16.4 5.0 %collective-permute-start.3 = (bf16[272,128]{1,0:T(8,128)(2,1)S(1)}, bf16[272,128]{1,0:T(8,128)(2,1)S(1)}, u32[]{:S(2)}, u32[]{:S(2)}) collective-permute-start(bf16[272,128]{1,0:T(8,128)(2,1)S(1)} %get-tuple-element.16), channel_id=1, source_target_pairs={{0,4},{4,0},{8,12},{12,8},{1,5},{5,1},{9,13},{13,9},{2,6},{6,2},{1... | collective-permute-start | bytes 208904 | tf_op jit(solution)/shard_map/ppermute | solution.py:27
  17.5 7.0 %collective-permute-start.4 = (bf16[272,128]{1,0:T(8,128)(2,1)S(1)}, bf16[272,128]{1,0:T(8,128)(2,1)S(1)}, u32[]{:S(2)}, u32[]{:S(2)}) collective-permute-start(bf16[272,128]{1,0:T(8,128)(2,1)S(1)} %get-tuple-element.17), channel_id=1, source_target_pairs={{0,8},{4,12},{8,0},{12,4},{1,9},{5,13},{9,1},{13,5},{2,10},{6,14},... | collective-permute-start | bytes 208904 | tf_op jit(solution)/shard_map/ppermute | solution.py:27
  20.3 6.1 %collective-permute-start.5 = (bf16[272,128]{1,0:T(8,128)(2,1)S(1)}, bf16[272,128]{1,0:T(8,128)(2,1)S(1)}, u32[]{:S(2)}, u32[]{:S(2)}) collective-permute-start(bf16[272,128]{1,0:T(8,128)(2,1)S(1)} %get-tuple-element.18), channel_id=1, source_target_pairs={{0,12},{4,8},{8,4},{12,0},{1,13},{5,9},{9,5},{13,1},{2,14},{6,10},... | collective-permute-start | bytes 208904 | tf_op jit(solution)/shard_map/ppermute | solution.py:27
  26.9 6.2 %collective-permute-start.8 = (bf16[256,128]{1,0:T(8,128)(2,1)S(1)}, bf16[256,128]{1,0:T(8,128)(2,1)S(1)}, u32[]{:S(2)}, u32[]{:S(2)}) collective-permute-start(bf16[256,128]{1,0:T(8,128)(2,1)S(1)} %values.1.refs_0_), channel_id=1, source_target_pairs={{0,12},{4,8},{8,4},{12,0},{1,13},{5,9},{9,5},{13,1},{2,14},{6,10},... | collective-permute-start | bytes 196616 | tf_op jit(solution)/shard_map/ppermute | solution.py:27
  28.1 6.4 %collective-permute-start.7 = (bf16[256,128]{1,0:T(8,128)(2,1)S(1)}, bf16[256,128]{1,0:T(8,128)(2,1)S(1)}, u32[]{:S(2)}, u32[]{:S(2)}) collective-permute-start(bf16[256,128]{1,0:T(8,128)(2,1)S(1)} %values.1.refs_0_), channel_id=1, source_target_pairs={{0,8},{4,12},{8,0},{12,4},{1,9},{5,13},{9,1},{13,5},{2,10},{6,14},... | collective-permute-start | bytes 196616 | tf_op jit(solution)/shard_map/ppermute | solution.py:27
  28.1 6.4 %collective-permute-start.6 = (bf16[256,128]{1,0:T(8,128)(2,1)S(1)}, bf16[256,128]{1,0:T(8,128)(2,1)S(1)}, u32[]{:S(2)}, u32[]{:S(2)}) collective-permute-start(bf16[256,128]{1,0:T(8,128)(2,1)S(1)} %values.1.refs_0_), channel_id=1, source_target_pairs={{0,4},{4,0},{8,12},{12,8},{1,5},{5,1},{9,13},{13,9},{2,6},{6,2},{1... | collective-permute-start | bytes 196616 | tf_op jit(solution)/shard_map/ppermute | solution.py:27
  36.5 3.8 %collective-permute-start.9 = (f32[4,896]{1,0:T(4,128)S(1)}, f32[4,896]{1,0:T(4,128)S(1)}, u32[]{:S(2)}, u32[]{:S(2)}) collective-permute-start(f32[4,896]{1,0:T(4,128)S(1)} %get-tuple-element.20), channel_id=1, source_target_pairs={{0,2},{2,0},{1,3},{3,1},{4,6},{6,4},{5,7},{7,5},{8,10},{10,8},{9,1... | collective-permute-start | bytes 43016 | tf_op jit(solution)/shard_map/ppermute | solution.py:27

commit v4 on v3

--- a/solution.py
+++ b/solution.py
@@ -84,20 +84,16 @@
             pltpu.SemaphoreType.DMA((min(4, heads // 2) + 1,)),
         ],
         compiler_params=pltpu.CompilerParams(vmem_limit_bytes=60 * MIB),
+        cost_estimate=spans(5),
         name="queries",
     )(query, key_absorb)
 
 
 def prepare_kernel(
-    lengths, ids_there, rope_there, bias, rope_out, block_ids, query_rope, rows_ref, arrived
+    lengths, block_ids, query_rope, bias, rope_out, rows_ref
 ):
     drafts, chosen = block_ids.shape
     tokens = bias.shape[1]
-    ids_copy = pltpu.make_async_copy(ids_there, block_ids, arrived.at[0])
-    rope_copy = pltpu.make_async_copy(rope_there, query_rope, arrived.at[1])
-    ids_copy.start()
-    rope_copy.start()
-    ids_copy.wait()
     ids = jnp.concatenate([block_ids[...]] * (8 // drafts), axis=0)
     position = lax.axis_index("ctx") * tokens + lax.broadcasted_iota(jnp.int32, (8, tokens), 1)
     block = position // BLK
@@ -107,7 +103,6 @@
     draft = lax.broadcasted_iota(jnp.int32, (8, tokens), 0) % drafts
     visible = found & (position <= lengths[0] - drafts + draft)
     bias[...] = jnp.where(visible, 0.0, HIDDEN)
-    rope_copy.wait()
     by_head(query_rope[...], rows_ref)
     rope_out[...] = rows_ref[...].astype(jnp.bfloat16)
 
@@ -120,34 +115,63 @@
             jax.ShapeDtypeStruct((8, tokens), jnp.float32),
             jax.ShapeDtypeStruct((drafts * heads, rope), jnp.bfloat16),
         ],
-        in_specs=[pl.BlockSpec(memory_space=pltpu.SMEM), HBM, HBM],
+        in_specs=[pl.BlockSpec(memory_space=pltpu.SMEM), VMEM, VMEM],
         out_specs=[VMEM] * 2,
-        scratch_shapes=[
-            pltpu.VMEM(block_ids.shape, block_ids.dtype),
-            pltpu.VMEM(query_rope.shape, query_rope.dtype),
-            pltpu.VMEM((drafts * heads, rope), jnp.float32),
-            pltpu.SemaphoreType.DMA((2,)),
-        ],
+        scratch_shapes=[pltpu.VMEM((drafts * heads, rope), jnp.float32)],
         compiler_params=pltpu.CompilerParams(vmem_limit_bytes=4 * MIB),
         cost_estimate=spans(12),
         name="prepare",
     )(lengths, block_ids, query_rope)
 
 
-def attend_kernel(*refs, count, scale):
-    pieces, (rope, cache, bias) = refs[:count], refs[count : count + 3]
-    outs, (queries, total_sums) = refs[count + 3 : -2], refs[-2:]
+def rows_at(ref, places, width):
+    found = [ref[pl.ds(pl.multiple_of(place * width, width), width), :] for place in places]
+    return found[0] if len(found) == 1 else jnp.concatenate(found, axis=0)
+
+
+def slices_of(steps):
+    return [lax.axis_index("ctx") ^ step for step in steps] if steps else [0]
+
+
+def begin_kernel(*refs, steps):
+    pieces, (rope, cache, bias, scores) = refs[:-4], refs[-4:]
     rows, width = pieces[0].shape
-    latent = count * width
-    me = lax.axis_index("ctx") if count > 1 else 0
-    for step in range(count):
-        at = pl.multiple_of((me ^ step) * width, width)
-        queries[:, pl.ds(at, width)] = pieces[step][...]
-    queries[:, latent:] = rope[...]
-
-    tokens = cache.shape[1]
-    scores = jnp.dot(queries[...], cache[...], preferred_element_type=jnp.float32)
-    scores = (scores.reshape(rows // 8, 8, tokens) + bias[...][None]).reshape(rows, tokens)
+    depth, tokens = cache.shape
+    found = jnp.dot(
+        jnp.concatenate([piece[...] for piece in pieces], axis=1),
+        rows_at(cache, slices_of(steps), width),
+        preferred_element_type=jnp.float32,
+    )
+    found += jnp.dot(
+        rope[...], cache[depth - rope.shape[1] :, :], preferred_element_type=jnp.float32
+    )
+    scores[...] = (found.reshape(rows // 8, 8, tokens) + bias[...][None]).reshape(rows, tokens)
+
+
+def begin(pieces, steps, rope, cache, bias):
+    rows, tokens = pieces[0].shape[0], cache.shape[1]
+    return pl.pallas_call(
+        functools.partial(begin_kernel, steps=steps),
+        out_shape=jax.ShapeDtypeStruct((rows, tokens), jnp.float32),
+        in_specs=[VMEM] * (len(pieces) + 3),
+        out_specs=VMEM,
+        compiler_params=pltpu.CompilerParams(vmem_limit_bytes=6 * MIB),
+        name="begin",
+    )(*pieces, rope, cache, bias)
+
+
+def attend_kernel(*refs, steps, outs_of, scale):
+    pieces, (begun, cache) = refs[: len(steps)], refs[len(steps) : len(steps) + 2]
+    outs, total_sums = refs[len(steps) + 2 : -1], refs[-1]
+    rows, latent = total_sums.shape
+    width = latent // len(outs)
+    scores = begun[...]
+    if steps:
+        scores += jnp.dot(
+            jnp.concatenate([piece[...] for piece in pieces], axis=1),
+            rows_at(cache, slices_of(steps), width),
+            preferred_element_type=jnp.float32,
+        )
     top = jnp.max(scores, axis=1, keepdims=True)
     weights = jnp.exp2((scores - top) * (scale * LOG2E))
     total = jnp.sum(weights, axis=1, keepdims=True)
@@ -165,28 +189,23 @@
             lines += [part[:, at : at + LANES] for at in range(0, rows, LANES)]
     lines.append(jnp.zeros((TAIL - len(lines), LANES), jnp.float32))
     tail = jnp.concatenate(lines, axis=0).astype(jnp.bfloat16)
-    for step in range(count):
-        at = pl.multiple_of((me ^ step) * width, width)
-        outs[step][:rows, :] = total_sums[:, pl.ds(at, width)].astype(jnp.bfloat16)
-        outs[step][rows:, :LANES] = tail
-
-
-def attend(pieces, rope, cache, bias, scale):
-    count, (rows, width) = len(pieces), pieces[0].shape
-    depth = cache.shape[0]
-    return pl.pallas_call(
-        functools.partial(attend_kernel, count=count, scale=scale),
-        out_shape=[jax.ShapeDtypeStruct((rows + TAIL, width), jnp.bfloat16)] * count,
-        in_specs=[VMEM] * (count + 3),
+    for out, place in zip(outs, slices_of(outs_of)):
+        at = pl.multiple_of(place * width, width)
+        out[:rows, :] = total_sums[:, pl.ds(at, width)].astype(jnp.bfloat16)
+        out[rows:, :LANES] = tail
+
+
+def attend(pieces, steps, begun, cache, latent, outs_of, scale):
+    rows, count = begun.shape[0], max(len(outs_of), 1)
+    return pl.pallas_call(
+        functools.partial(attend_kernel, steps=steps, outs_of=outs_of, scale=scale),
+        out_shape=[jax.ShapeDtypeStruct((rows + TAIL, latent // count), jnp.bfloat16)] * count,
+        in_specs=[VMEM] * (len(pieces) + 2),
         out_specs=[VMEM] * count,
-        scratch_shapes=[
-            pltpu.VMEM((rows, depth), jnp.bfloat16),
-            pltpu.VMEM((rows, count * width), jnp.float32),
-        ],
-        compiler_params=pltpu.CompilerParams(vmem_limit_bytes=16 * MIB),
-        cost_estimate=spans(40),
+        scratch_shapes=[pltpu.VMEM((rows, latent), jnp.float32)],
+        compiler_params=pltpu.CompilerParams(vmem_limit_bytes=11 * MIB),
         name="attend",
-    )(*pieces, rope, cache, bias)
+    )(*pieces, begun, cache)
 
 
 def numbers_of(tail, rows):
@@ -200,6 +219,22 @@
         ]
         found.append(parts[0] + parts[1] + parts[2])
     return found
+
+
+def keep_kernel(block, out):
+    out[...] = block[...]
+
+
+def keep(block):
+    return pl.pallas_call(
+        keep_kernel,
+        out_shape=jax.ShapeDtypeStruct(block.shape, block.dtype),
+        in_specs=[VMEM],
+        out_specs=VMEM,
+        compiler_params=pltpu.CompilerParams(vmem_limit_bytes=1 * MIB),
+        cost_estimate=spans(40),
+        name="keep",
+    )(block)
 
 
 def values_kernel(*refs, drafts):
@@ -305,7 +340,7 @@
     rope = query_rope.shape[3]
     tokens = latent_cache.shape[1]
     scale = (nope + rope) ** (-0.5)
-    rows = drafts * heads
+    rows, latent = drafts * heads, latent_cache.shape[2] - rope
     peers = lax.axis_size("ctx")
     few = peers <= FEW and lax.axis_size("head") == 2 and key_absorb.shape[2] == LANES
 
@@ -313,16 +348,22 @@
     bias, rope_rows = prepare(lengths, block_ids[0], query_rope[0], tokens)
     cache = latent_cache[0].T
     if few:
-        pieces = [q_piece] + [swap(q_piece, "ctx", step) for step in range(1, peers)]
-        blocks = attend(pieces, rope_rows, cache, bias, scale)
-        blocks = [blocks[0]] + [swap(blocks[step], "ctx", step) for step in range(1, peers)]
+        steps = tuple(range(peers))
+        pieces = [q_piece] + [swap(q_piece, "ctx", step) for step in steps[1:]]
+        early, late = (0, 1), (2, 3)
+        begun = begin([pieces[step] for step in early], early, rope_rows, cache, bias)
+        blocks = attend(
+            [pieces[step] for step in late], late, begun, cache, latent, steps, scale
+        )
+        blocks = [keep(blocks[0])] + [swap(blocks[step], "ctx", step) for step in (2, 3, 1)]
         partial = values_of(blocks, value_absorb, drafts)
-        partials = [partial] + [swap(partial, "ctx", step) for step in range(1, peers)]
+        partials = [partial] + [swap(partial, "ctx", step) for step in (2, 3, 1)]
         theirs, flat = theirs_of(partials, output_weight, drafts)
         summed = mine_of(flat, output_weight) + swap(theirs, "head", 1)
     else:
         queries = lax.all_gather(q_piece, "ctx", axis=1, tiled=True)
-        block = attend([queries], rope_rows, cache, bias, scale)[0]
+        begun = begin([queries], (), rope_rows, cache, bias)
+        block = attend([], (), begun, cache, latent, (), scale)[0]
         o_latent = combine_many(block, rows)
         head_values = jnp.einsum(
             "htc,hcv->thv",

time: 41.1 us -> 39.2 us (0.954)
  starting transfers between devices: 16.2 us -> 14.3 us
    ppermute x10, starting transfers between devices: 16.2 us -> 14.3 us  [swap(): return lax.ppermute(value, axis, [(i, i ^ step) for i in range(count)])]
    pallas_call x1 -> x3, Pallas kernels: 3.69 us -> 3.93 us  [the longest x1 2.69 us: attend(): pl.pallas_call(functools.partial(attend_kernel, steps=steps, outs_of=outs...]
    unnamed x22 -> x24, local copies, waits for them, and re-layouts: 1.56 us -> 1.5 us
  transfers between devices with their start and end apart: 10 -> 10, of which waited for: 7 -> 7; matrix products, arithmetic and copies ran while one was open for 0% -> 0% of each run, Pallas kernels for 7% -> 10%
where the time goes in v4:
time: 39.2 us; the launch traced here: 39 us
  starting transfers between devices  14.3 us (36%)
  Pallas kernels  11.1 us (28%)
  waiting for transfers between devices  10.7 us (27%)
  local copies, waits for them, and re-layouts  1.5 us (4%)
  between operations  0.83 us (2%)
  other arithmetic  0.6 us (2%)
    ppermute x10, starting transfers between devices, swap(): return lax.ppermute(value, axis, [(i, i ^ step) for i in range(count)])  14.3 us
    ppermute x10, waiting for transfers between devices, swap(): return lax.ppermute(value, axis, [(i, i ^ step) for i in range(count)])  10.7 us
    pallas_call x1, Pallas kernels, attend(): pl.pallas_call(functools.partial(attend_kernel, steps=steps, outs_of=outs...  2.69 us
    pallas_call x1, Pallas kernels, theirs_of(): pl.pallas_call(functools.partial(theirs_kernel, drafts=drafts), out_shape...  2.04 us
    pallas_call x1, Pallas kernels, mine_of(): pl.pallas_call(mine_kernel, out_shape=jax.ShapeDtypeStruct((flat.shape[0]...  2 us
    pallas_call x1, Pallas kernels, queries_of(): pl.pallas_call(queries_kernel, out_shape=pltpu.VMEM((rows, width), jnp.bf...  1.92 us
    unnamed x24, local copies, waits for them, and re-layouts  1.5 us
    pallas_call x1, Pallas kernels, begin(): pl.pallas_call(functools.partial(begin_kernel, steps=steps), out_shape=ja...  1.23 us
  transfers between devices with their start and end apart: 10, of which 7 were waited for; matrix products, arithmetic and copies ran while one was open for 0% of the time, Pallas kernels for 10%

profile of v4, /device:TPU:0, one launch (start us, length us, event | category | flops | bytes accessed | tf_op | source)
XLA Modules:
  0.0 39.0 jit_solution(17674055281415977743)
XLA Ops:
  0.0 0.0 copy-start.1
  0.0 0.0 copy-start.2
  0.0 0.0 slice-start.7
  0.0 1.9 %queries.1.refs_0_ = bf16[256,128]{1,0:T(8,128)(2,1)S(1)} custom-call(bf16[4,64,128]{2,1,0:T(8,128)(2,1)} %bitcast.16, bf16[64,128,128]{2,1,0:T(8,128)(2,1)} %key_absorb.1), custom_call_target="tpu_custom_call" | custom-call | flops 5000000000 | tf_op jit(solution)/shard_map/queries/pallas_call | solution.py:75
  1.9 3.1 %collective-permute-start.2 = (bf16[256,128]{1,0:T(8,128)(2,1)S(1)}, bf16[256,128]{1,0:T(8,128)(2,1)S(1)}, u32[]{:S(2)}, u32[]{:S(2)}) collective-permute-start(bf16[256,128]{1,0:T(8,128)(2,1)S(1)} %queries.1.refs_0_), channel_id=1, source_target_pairs={{0,4},{4,0},{8,12},{12,8},{1,5},{5,1},{9,13},{13,9},{2,6},{6,2},{1... | collective-permute-start | bytes 196616 | tf_op jit(solution)/shard_map/ppermute | solution.py:27
  5.0 2.6 %collective-permute-start = (bf16[256,128]{1,0:T(8,128)(2,1)S(1)}, bf16[256,128]{1,0:T(8,128)(2,1)S(1)}, u32[]{:S(2)}, u32[]{:S(2)}) collective-permute-start(bf16[256,128]{1,0:T(8,128)(2,1)S(1)} %queries.1.refs_0_), channel_id=1, source_target_pairs={{0,8},{4,12},{8,0},{12,4},{1,9},{5,13},{9,1},{13,5},{2,10},{6,14},... | collective-permute-start | bytes 196616 | tf_op jit(solution)/shard_map/ppermute | solution.py:27
  7.6 0.0 collective-permute-start.1
  8.3 0.0 copy-done.1
  8.3 0.0 copy-done.2
  8.3 0.0 slice-start.8
  8.3 0.7 %prepare.1 = (f32[8,4096]{1,0:T(8,128)S(1)}, bf16[256,64]{1,0:T(8,128)(2,1)S(1)}) custom-call(s32[1]{0:T(128)S(6)} %copy.9.lengths, s32[4,32]{1,0:T(4,128)S(1)} %bitcast.15, bf16[4,64,64]{2,1,0:T(8,128)(2,1)S(1)} %bitcast.14), custom_call_target="tpu_custom_call" | custom-call | flops 12000000000 | tf_op jit(solution)/shard_map/prepare/pallas_call | solution.py:112
  9.0 0.0 collective-permute-done.2.refs_1_
  9.0 0.0 slice-done.7
  9.0 1.5 %slice-done.8 = s8[4194304]{0:T(1024)(128)(4,1)S(1)} async-done(((s8[4718592]{0:T(1024)(128)(4,1)}), s8[4194304]{0:T(1024)(128)(4,1)S(1)}, s32[]{:S(2)}) %slice-start.8) | async-done | bytes 4194328
  10.5 1.2 %begin.1.refs_2_ = f32[256,4096]{1,0:T(8,128)S(1)} custom-call(bf16[256,128]{1,0:T(8,128)(2,1)S(1)} %queries.1.refs_0_, bf16[256,128]{1,0:T(8,128)(2,1)S(1)} %collective-permute-done.2.refs_1_, bf16[256,64]{1,0:T(8,128)(2,1)S(1)} %get-tuple-element.13.refs_2_, bf16[576,4096]{1,0:T(8,128)(2,1)S(1)} %bitcast.12, f32[8,4096]{1,0:T(8,128)S(1)} %get-tuple-element.14.refs_4_), custom_call_target="tpu_custom_call" | custom-call | tf_op jit(solution)/shard_map/begin/pallas_call | solution.py:153
  11.7 0.6 %collective-permute-done.refs_0_ = bf16[256,128]{1,0:T(8,128)(2,1)S(1)} collective-permute-done((bf16[256,128]{1,0:T(8,128)(2,1)S(1)}, bf16[256,128]{1,0:T(8,128)(2,1)S(1)}, u32[]{:S(2)}, u32[]{:S(2)}) %collective-permute-start) | collective-permute-done | bytes 65568 | tf_op jit(solution)/shard_map/ppermute | solution.py:27
  12.3 1.4 %collective-permute-done.1.refs_1_ = bf16[256,128]{1,0:T(8,128)(2,1)S(1)} collective-permute-done((bf16[256,128]{1,0:T(8,128)(2,1)S(1)}, bf16[256,128]{1,0:T(8,128)(2,1)S(1)}, u32[]{:S(2)}, u32[]{:S(2)}) %collective-permute-start.1) | collective-permute-done | bytes 65568 | tf_op jit(solution)/shard_map/ppermute | solution.py:27
  13.7 2.7 %attend.1 = (bf16[272,128]{1,0:T(8,128)(2,1)S(1)}, bf16[272,128]{1,0:T(8,128)(2,1)S(1)}, bf16[272,128]{1,0:T(8,128)(2,1)S(1)}, bf16[272,128]{1,0:T(8,128)(2,1)S(1)}) custom-call(bf16[256,128]{1,0:T(8,128)(2,1)S(1)} %collective-permute-done.refs_0_, bf16[256,128]{1,0:T(8,128)(2,1)S(1)} %collective-permute-done.1.refs_1_, f32[256,4096]{1,0:T(8,128)S(1)} %begin.1.refs_2_, ...), custom_call_target="tpu_custom_call" | custom-call | tf_op jit(solution)/shard_map/attend/pallas_call | solution.py:200
  16.4 1.7 %collective-permute-start.3 = (bf16[272,128]{1,0:T(8,128)(2,1)S(1)}, bf16[272,128]{1,0:T(8,128)(2,1)S(1)}, u32[]{:S(2)}, u32[]{:S(2)}) collective-permute-start(bf16[272,128]{1,0:T(8,128)(2,1)S(1)} %get-tuple-element.16), channel_id=1, source_target_pairs={{0,8},{4,12},{8,0},{12,4},{1,9},{5,13},{9,1},{13,5},{2,10},{6,14},... | collective-permute-start | bytes 208904 | tf_op jit(solution)/shard_map/ppermute | solution.py:27
  18.0 0.7 %collective-permute-start.4 = (bf16[272,128]{1,0:T(8,128)(2,1)S(1)}, bf16[272,128]{1,0:T(8,128)(2,1)S(1)}, u32[]{:S(2)}, u32[]{:S(2)}) collective-permute-start(bf16[272,128]{1,0:T(8,128)(2,1)S(1)} %get-tuple-element.17), channel_id=1, source_target_pairs={{0,12},{4,8},{8,4},{12,0},{1,13},{5,9},{9,5},{13,1},{2,14},{6,10},... | collective-permute-start | bytes 208904 | tf_op jit(solution)/shard_map/ppermute | solution.py:27
  18.7 1.2 %collective-permute-start.5 = (bf16[272,128]{1,0:T(8,128)(2,1)S(1)}, bf16[272,128]{1,0:T(8,128)(2,1)S(1)}, u32[]{:S(2)}, u32[]{:S(2)}) collective-permute-start(bf16[272,128]{1,0:T(8,128)(2,1)S(1)} %get-tuple-element.18), channel_id=1, source_target_pairs={{0,4},{4,0},{8,12},{12,8},{1,5},{5,1},{9,13},{13,9},{2,6},{6,2},{1... | collective-permute-start | bytes 208904 | tf_op jit(solution)/shard_map/ppermute | solution.py:27
  20.0 0.0 slice-start.3
  20.0 0.0 slice-start.4
  20.0 0.0 slice-start.5
  20.0 0.0 slice-start.6
  20.0 2.7 %collective-permute-done.3.refs_1_ = bf16[272,128]{1,0:T(8,128)(2,1)S(1)} collective-permute-done((bf16[272,128]{1,0:T(8,128)(2,1)S(1)}, bf16[272,128]{1,0:T(8,128)(2,1)S(1)}, u32[]{:S(2)}, u32[]{:S(2)}) %collective-permute-start.3) | collective-permute-done | bytes 69664 | tf_op jit(solution)/shard_map/ppermute | solution.py:27
  22.7 1.5 %collective-permute-done.4.refs_2_ = bf16[272,128]{1,0:T(8,128)(2,1)S(1)} collective-permute-done((bf16[272,128]{1,0:T(8,128)(2,1)S(1)}, bf16[272,128]{1,0:T(8,128)(2,1)S(1)}, u32[]{:S(2)}, u32[]{:S(2)}) %collective-permute-start.4) | collective-permute-done | bytes 69664 | tf_op jit(solution)/shard_map/ppermute | solution.py:27
  24.2 0.0 collective-permute-done.5.refs_3_
  24.2 0.0 copy-done
  24.2 0.5 %values.1.refs_0_ = bf16[256,128]{1,0:T(8,128)(2,1)S(1)} custom-call(bf16[272,128]{1,0:T(8,128)(2,1)S(1)} %keep.1.refs_0_, bf16[272,128]{1,0:T(8,128)(2,1)S(1)} %collective-permute-done.3.refs_1_, bf16[272,128]{1,0:T(8,128)(2,1)S(1)} %collective-permute-done.4.refs_2_, bf16[272,128]{1,0:T(8,128)(2,1)S(1)} %collective-permute-done.5.refs_3_, ...), custom_call_target="tpu_custom_call" | custom-call | tf_op jit(solution)/shard_map/values/pallas_call | solution.py:258
  24.7 1.8 %collective-permute-start.6 = (bf16[256,128]{1,0:T(8,128)(2,1)S(1)}, bf16[256,128]{1,0:T(8,128)(2,1)S(1)}, u32[]{:S(2)}, u32[]{:S(2)}) collective-permute-start(bf16[256,128]{1,0:T(8,128)(2,1)S(1)} %values.1.refs_0_), channel_id=1, source_target_pairs={{0,8},{4,12},{8,0},{12,4},{1,9},{5,13},{9,1},{13,5},{2,10},{6,14},... | collective-permute-start | bytes 196616 | tf_op jit(solution)/shard_map/ppermute | solution.py:27
  26.5 0.7 %collective-permute-start.7 = (bf16[256,128]{1,0:T(8,128)(2,1)S(1)}, bf16[256,128]{1,0:T(8,128)(2,1)S(1)}, u32[]{:S(2)}, u32[]{:S(2)}) collective-permute-start(bf16[256,128]{1,0:T(8,128)(2,1)S(1)} %values.1.refs_0_), channel_id=1, source_target_pairs={{0,12},{4,8},{8,4},{12,0},{1,13},{5,9},{9,5},{13,1},{2,14},{6,10},... | collective-permute-start | bytes 196616 | tf_op jit(solution)/shard_map/ppermute | solution.py:27
  27.2 1.0 %collective-permute-start.8 = (bf16[256,128]{1,0:T(8,128)(2,1)S(1)}, bf16[256,128]{1,0:T(8,128)(2,1)S(1)}, u32[]{:S(2)}, u32[]{:S(2)}) collective-permute-start(bf16[256,128]{1,0:T(8,128)(2,1)S(1)} %values.1.refs_0_), channel_id=1, source_target_pairs={{0,4},{4,0},{8,12},{12,8},{1,5},{5,1},{9,13},{13,9},{2,6},{6,2},{1... | collective-permute-start | bytes 196616 | tf_op jit(solution)/shard_map/ppermute | solution.py:27
  28.2 3.0 %collective-permute-done.6.refs_1_ = bf16[256,128]{1,0:T(8,128)(2,1)S(1)} collective-permute-done((bf16[256,128]{1,0:T(8,128)(2,1)S(1)}, bf16[256,128]{1,0:T(8,128)(2,1)S(1)}, u32[]{:S(2)}, u32[]{:S(2)}) %collective-permute-start.6) | collective-permute-done | bytes 65568 | tf_op jit(solution)/shard_map/ppermute | solution.py:27
  31.2 1.4 %collective-permute-done.7.refs_2_ = bf16[256,128]{1,0:T(8,128)(2,1)S(1)} collective-permute-done((bf16[256,128]{1,0:T(8,128)(2,1)S(1)}, bf16[256,128]{1,0:T(8,128)(2,1)S(1)}, u32[]{:S(2)}, u32[]{:S(2)}) %collective-permute-start.7) | collective-permute-done | bytes 65568 | tf_op jit(solution)/shard_map/ppermute | solution.py:27
  32.6 0.0 collective-permute-done.8.refs_3_
  32.6 0.0 slice-done
  32.6 0.0 slice-done.1
  32.6 0.0 slice-done.2
  32.6 0.0 slice-done.3
  32.6 0.0 slice-done.4
  32.6 0.0 slice-done.5
  32.6 0.0 slice-done.6
  32.6 2.0 %theirs.1 = (f32[4,896]{1,0:T(4,128)S(1)}, bf16[4,8192]{1,0:T(4,128)(2,1)S(1)}) custom-call(bf16[256,128]{1,0:T(8,128)(2,1)S(1)} %values.1.refs_0_, bf16[256,128]{1,0:T(8,128)(2,1)S(1)} %collective-permute-done.6.refs_1_, bf16[256,128]{1,0:T(8,128)(2,1)S(1)} %collective-permute-done.7.refs_2_, bf16[256,128]{1,0:T(8,128)(2,1)S(1)} %collective-permute-done.8.refs_3_, ...), custom_call_target="tpu_custom_call" | custom-call | tf_op jit(solution)/shard_map/theirs/pallas_call | solution.py:289
  34.7 1.5 %collective-permute-start.9 = (f32[4,896]{1,0:T(4,128)S(1)}, f32[4,896]{1,0:T(4,128)S(1)}, u32[]{:S(2)}, u32[]{:S(2)}) collective-permute-start(f32[4,896]{1,0:T(4,128)S(1)} %get-tuple-element.20), channel_id=1, source_target_pairs={{0,2},{2,0},{1,3},{3,1},{4,6},{6,4},{5,7},{7,5},{8,10},{10,8},{9,1... | collective-permute-start | bytes 43016 | tf_op jit(solution)/shard_map/ppermute | solution.py:27
  36.2 2.0 %mine.1 = f32[4,896]{1,0:T(4,128)S(1)} custom-call(bf16[4,8192]{1,0:T(4,128)(2,1)S(1)} %get-tuple-element.19.flat, bf16[8192,1792]{1,0:T(8,128)(2,1)S(1)} %bitcast.9), custom_call_target="tpu_custom_call" | custom-call | flops 2000000000 | tf_op jit(solution)/shard_map/mine/pallas_call | solution.py:308
  38.2 0.2 collective-permute-done.9
  38.4 0.6 %fusion = bf16[1,4,896]{2,1,0:T(4,128)(2,1)} fusion(f32[4,896]{1,0:T(4,128)S(1)} %mine.1, f32[4,896]{1,0:T(4,128)S(1)} %collective-permute-done.9), kind=kLoop, calls=%fused_computation.1 | loop fusion | flops 7168 | bytes 35840 | tf_op jit(solution)/shard_map/broadcast_in_dim | solution.py:379
  (7 shorter events, 0.0 us)
Async XLA Ops:
  0.0 8.3 %copy-start.1 = (bf16[1,4,64,64]{3,2,1,0:T(8,128)(2,1)S(1)}, bf16[1,4,64,64]{3,2,1,0:T(8,128)(2,1)}, u32[]{:S(2)}) copy-start(bf16[1,4,64,64]{3,2,1,0:T(8,128)(2,1)} %param.9) | copy-start | bytes 98308
  0.0 8.3 %copy-start.2 = (s32[1,4,32]{2,1,0:T(4,128)S(1)}, s32[1,4,32]{2,1,0:T(4,128)}, u32[]{:S(2)}) copy-start(s32[1,4,32]{2,1,0:T(4,128)} %param.12) | copy-start | bytes 1540
  0.0 9.0 %slice-start.7 = ((s8[4718592]{0:T(1024)(128)(4,1)}), s8[524288]{0:T(1024)(128)(4,1)S(1)}, s32[]{:S(2)}) async-start(s8[4718592]{0:T(1024)(128)(4,1)} %bitcast.10), calls=%async_computation.7 | async-start | bytes 1048576
  1.9 7.1 %collective-permute-start.2 = (bf16[256,128]{1,0:T(8,128)(2,1)S(1)}, bf16[256,128]{1,0:T(8,128)(2,1)S(1)}, u32[]{:S(2)}, u32[]{:S(2)}) collective-permute-start(bf16[256,128]{1,0:T(8,128)(2,1)S(1)} %queries.1.refs_0_), channel_id=1, source_target_pairs={{0,4},{4,0},{8,12},{12,8},{1,5},{5,1},{9,13},{13,9},{2,6},{6,2},{1... | collective-permute-start | bytes 196616 | tf_op jit(solution)/shard_map/ppermute | solution.py:27
  5.0 7.3 %collective-permute-start = (bf16[256,128]{1,0:T(8,128)(2,1)S(1)}, bf16[256,128]{1,0:T(8,128)(2,1)S(1)}, u32[]{:S(2)}, u32[]{:S(2)}) collective-permute-start(bf16[256,128]{1,0:T(8,128)(2,1)S(1)} %queries.1.refs_0_), channel_id=1, source_target_pairs={{0,8},{4,12},{8,0},{12,4},{1,9},{5,13},{9,1},{13,5},{2,10},{6,14},... | collective-permute-start | bytes 196616 | tf_op jit(solution)/shard_map/ppermute | solution.py:27
  7.6 6.1 %collective-permute-start.1 = (bf16[256,128]{1,0:T(8,128)(2,1)S(1)}, bf16[256,128]{1,0:T(8,128)(2,1)S(1)}, u32[]{:S(2)}, u32[]{:S(2)}) collective-permute-start(bf16[256,128]{1,0:T(8,128)(2,1)S(1)} %queries.1.refs_0_), channel_id=1, source_target_pairs={{0,12},{4,8},{8,4},{12,0},{1,13},{5,9},{9,5},{13,1},{2,14},{6,10},... | collective-permute-start | bytes 196616 | tf_op jit(solution)/shard_map/ppermute | solution.py:27
  8.3 2.2 %slice-start.8 = ((s8[4718592]{0:T(1024)(128)(4,1)}), s8[4194304]{0:T(1024)(128)(4,1)S(1)}, s32[]{:S(2)}) async-start(s8[4718592]{0:T(1024)(128)(4,1)} %bitcast.10), calls=%async_computation.8 | async-start | bytes 8388608
  16.4 6.3 %collective-permute-start.3 = (bf16[272,128]{1,0:T(8,128)(2,1)S(1)}, bf16[272,128]{1,0:T(8,128)(2,1)S(1)}, u32[]{:S(2)}, u32[]{:S(2)}) collective-permute-start(bf16[272,128]{1,0:T(8,128)(2,1)S(1)} %get-tuple-element.16), channel_id=1, source_target_pairs={{0,8},{4,12},{8,0},{12,4},{1,9},{5,13},{9,1},{13,5},{2,10},{6,14},... | collective-permute-start | bytes 208904 | tf_op jit(solution)/shard_map/ppermute | solution.py:27
  18.0 6.1 %collective-permute-start.4 = (bf16[272,128]{1,0:T(8,128)(2,1)S(1)}, bf16[272,128]{1,0:T(8,128)(2,1)S(1)}, u32[]{:S(2)}, u32[]{:S(2)}) collective-permute-start(bf16[272,128]{1,0:T(8,128)(2,1)S(1)} %get-tuple-element.17), channel_id=1, source_target_pairs={{0,12},{4,8},{8,4},{12,0},{1,13},{5,9},{9,5},{13,1},{2,14},{6,10},... | collective-permute-start | bytes 208904 | tf_op jit(solution)/shard_map/ppermute | solution.py:27
  18.7 5.5 %collective-permute-start.5 = (bf16[272,128]{1,0:T(8,128)(2,1)S(1)}, bf16[272,128]{1,0:T(8,128)(2,1)S(1)}, u32[]{:S(2)}, u32[]{:S(2)}) collective-permute-start(bf16[272,128]{1,0:T(8,128)(2,1)S(1)} %get-tuple-element.18), channel_id=1, source_target_pairs={{0,4},{4,0},{8,12},{12,8},{1,5},{5,1},{9,13},{13,9},{2,6},{6,2},{1... | collective-permute-start | bytes 208904 | tf_op jit(solution)/shard_map/ppermute | solution.py:27
  19.9 12.6 %slice-start = ((s8[29360128]{0:T(1024)(128)(4,1)}), s8[4194304]{0:T(1024)(128)(4,1)S(1)}, s32[]{:S(2)}) async-start(s8[29360128]{0:T(1024)(128)(4,1)} %bitcast.8), calls=%async_computation | async-start | bytes 8388608
  19.9 4.2 %copy-start = (bf16[64,128,128]{2,1,0:T(8,128)(2,1)S(1)}, bf16[64,128,128]{2,1,0:T(8,128)(2,1)}, u32[]{:S(2)}) copy-start(bf16[64,128,128]{2,1,0:T(8,128)(2,1)} %refs_4_.2) | copy-start | bytes 6291460
  20.0 12.6 %slice-start.1 = ((s8[29360128]{0:T(1024)(128)(4,1)}), s8[4194304]{0:T(1024)(128)(4,1)S(1)}, s32[]{:S(2)}) async-start(s8[29360128]{0:T(1024)(128)(4,1)} %bitcast.8), calls=%async_computation.1 | async-start | bytes 8388608
  20.0 12.6 %slice-start.2 = ((s8[29360128]{0:T(1024)(128)(4,1)}), s8[4194304]{0:T(1024)(128)(4,1)S(1)}, s32[]{:S(2)}) async-start(s8[29360128]{0:T(1024)(128)(4,1)} %bitcast.8), calls=%async_computation.2 | async-start | bytes 8388608
  20.0 12.6 %slice-start.3 = ((s8[29360128]{0:T(1024)(128)(4,1)}), s8[4194304]{0:T(1024)(128)(4,1)S(1)}, s32[]{:S(2)}) async-start(s8[29360128]{0:T(1024)(128)(4,1)} %bitcast.8), calls=%async_computation.3 | async-start | bytes 8388608
  20.0 12.6 %slice-start.4 = ((s8[29360128]{0:T(1024)(128)(4,1)}), s8[4194304]{0:T(1024)(128)(4,1)S(1)}, s32[]{:S(2)}) async-start(s8[29360128]{0:T(1024)(128)(4,1)} %bitcast.8), calls=%async_computation.4 | async-start | bytes 8388608
  20.0 12.6 %slice-start.5 = ((s8[29360128]{0:T(1024)(128)(4,1)}), s8[4194304]{0:T(1024)(128)(4,1)S(1)}, s32[]{:S(2)}) async-start(s8[29360128]{0:T(1024)(128)(4,1)} %bitcast.8), calls=%async_computation.5 | async-start | bytes 8388608
  20.0 12.6 %slice-start.6 = ((s8[29360128]{0:T(1024)(128)(4,1)}), s8[4194304]{0:T(1024)(128)(4,1)S(1)}, s32[]{:S(2)}) async-start(s8[29360128]{0:T(1024)(128)(4,1)} %bitcast.8), calls=%async_computation.6 | async-start | bytes 8388608
  24.7 6.5 %collective-permute-start.6 = (bf16[256,128]{1,0:T(8,128)(2,1)S(1)}, bf16[256,128]{1,0:T(8,128)(2,1)S(1)}, u32[]{:S(2)}, u32[]{:S(2)}) collective-permute-start(bf16[256,128]{1,0:T(8,128)(2,1)S(1)} %values.1.refs_0_), channel_id=1, source_target_pairs={{0,8},{4,12},{8,0},{12,4},{1,9},{5,13},{9,1},{13,5},{2,10},{6,14},... | collective-permute-start | bytes 196616 | tf_op jit(solution)/shard_map/ppermute | solution.py:27
  26.5 6.1 %collective-permute-start.7 = (bf16[256,128]{1,0:T(8,128)(2,1)S(1)}, bf16[256,128]{1,0:T(8,128)(2,1)S(1)}, u32[]{:S(2)}, u32[]{:S(2)}) collective-permute-start(bf16[256,128]{1,0:T(8,128)(2,1)S(1)} %values.1.refs_0_), channel_id=1, source_target_pairs={{0,12},{4,8},{8,4},{12,0},{1,13},{5,9},{9,5},{13,1},{2,14},{6,10},... | collective-permute-start | bytes 196616 | tf_op jit(solution)/shard_map/ppermute | solution.py:27
  27.2 5.4 %collective-permute-start.8 = (bf16[256,128]{1,0:T(8,128)(2,1)S(1)}, bf16[256,128]{1,0:T(8,128)(2,1)S(1)}, u32[]{:S(2)}, u32[]{:S(2)}) collective-permute-start(bf16[256,128]{1,0:T(8,128)(2,1)S(1)} %values.1.refs_0_), channel_id=1, source_target_pairs={{0,4},{4,0},{8,12},{12,8},{1,5},{5,1},{9,13},{13,9},{2,6},{6,2},{1... | collective-permute-start | bytes 196616 | tf_op jit(solution)/shard_map/ppermute | solution.py:27
  34.7 3.8 %collective-permute-start.9 = (f32[4,896]{1,0:T(4,128)S(1)}, f32[4,896]{1,0:T(4,128)S(1)}, u32[]{:S(2)}, u32[]{:S(2)}) collective-permute-start(f32[4,896]{1,0:T(4,128)S(1)} %get-tuple-element.20), channel_id=1, source_target_pairs={{0,2},{2,0},{1,3},{3,1},{4,6},{6,4},{5,7},{7,5},{8,10},{10,8},{9,1... | collective-permute-start | bytes 43016 | tf_op jit(solution)/shard_map/ppermute | solution.py:27

commit v5 on v4

--- a/solution.py
+++ b/solution.py
@@ -47,11 +47,13 @@
     for head in range(first, last, 2):
         both = jnp.concatenate([heads[head], heads[head + 1]], axis=1)
         at = slice(head * drafts, head * drafts + pair)
-        found = jnp.dot(left[at], both, preferred_element_type=jnp.float32)
-        store[at, :] = jnp.where(upper, found[:, :width], found[:, width:]).astype(store.dtype)
-
-
-def queries_kernel(query, key_absorb, out, query_here, held, rows_ref, arrived):
+        found = jnp.dot(
+            left[at].astype(jnp.bfloat16), both, preferred_element_type=jnp.float32
+        )
+        store[at, :] = jnp.where(upper, found[:, :width], found[:, width:])
+
+
+def queries_kernel(query, key_absorb, out, query_here, held, rows_ref, found, arrived):
     drafts, heads, _ = query.shape
     parts = arrived.shape[0] - 1
     each = heads // parts
@@ -63,10 +65,11 @@
         copy.start()
     copies[0].wait()
     by_head(query_here[...], rows_ref)
-    left = rows_ref[...].astype(jnp.bfloat16)
+    left = rows_ref[...]
     for i in range(parts):
         copies[1 + i].wait()
-        pair_products(left, held, i * each, (i + 1) * each, drafts, out)
+        pair_products(left, held, i * each, (i + 1) * each, drafts, found)
+    out[...] = found[...].astype(out.dtype)
 
 
 def queries_of(query, key_absorb):
@@ -81,6 +84,7 @@
             pltpu.VMEM(query.shape, query.dtype),
             pltpu.VMEM(key_absorb.shape, key_absorb.dtype),
             pltpu.VMEM((rows, nope), jnp.float32),
+            pltpu.VMEM((rows, width), jnp.float32),
             pltpu.SemaphoreType.DMA((min(4, heads // 2) + 1,)),
         ],
         compiler_params=pltpu.CompilerParams(vmem_limit_bytes=60 * MIB),
@@ -238,7 +242,7 @@
 
 
 def values_kernel(*refs, drafts):
-    blocks, value_absorb, out = refs[:-2], refs[-2], refs[-1]
+    blocks, (value_absorb, out, found) = refs[:-3], refs[-3:]
     rows = out.shape[0]
     heads, width, value_width = value_absorb.shape
     numbers = [numbers_of(block[rows:, :], rows) for block in blocks]
@@ -249,8 +253,8 @@
     for block, factor in zip(blocks, factors):
         column = jnp.broadcast_to(factor / total, (width, rows)).T
         latent += block[:rows, :].astype(jnp.float32) * column
-    latent = latent.astype(jnp.bfloat16)
-    pair_products(latent, value_absorb, 0, heads, drafts, out)
+    pair_products(latent, value_absorb, 0, heads, drafts, found)
+    out[...] = found[...].astype(out.dtype)
 
 
 def values_of(blocks, value_absorb, drafts):
@@ -260,6 +264,7 @@
         out_shape=jax.ShapeDtypeStruct((rows, value_absorb.shape[2]), jnp.bfloat16),
         in_specs=[VMEM] * (len(blocks) + 1),
         out_specs=VMEM,
+        scratch_shapes=[pltpu.VMEM((rows, value_absorb.shape[2]), jnp.float32)],
         compiler_params=pltpu.CompilerParams(vmem_limit_bytes=8 * MIB),
         name="values",
     )(*blocks, value_absorb)

time: 39.2 us -> 39.2 us (level)
  no operation moved by 1% of the time
where the time goes in v5:
time: 39.2 us; the launch traced here: 39 us
  starting transfers between devices  14.3 us (36%)
  Pallas kernels  11.1 us (28%)
  waiting for transfers between devices  10.7 us (27%)
  local copies, waits for them, and re-layouts  1.5 us (4%)
  between operations  0.84 us (2%)
  other arithmetic  0.6 us (2%)
    ppermute x10, starting transfers between devices, swap(): return lax.ppermute(value, axis, [(i, i ^ step) for i in range(count)])  14.3 us
    ppermute x10, waiting for transfers between devices, swap(): return lax.ppermute(value, axis, [(i, i ^ step) for i in range(count)])  10.7 us
    pallas_call x1, Pallas kernels, attend(): pl.pallas_call(functools.partial(attend_kernel, steps=steps, outs_of=outs...  2.69 us
    pallas_call x1, Pallas kernels, theirs_of(): pl.pallas_call(functools.partial(theirs_kernel, drafts=drafts), out_shape...  2.04 us
    pallas_call x1, Pallas kernels, mine_of(): pl.pallas_call(mine_kernel, out_shape=jax.ShapeDtypeStruct((flat.shape[0]...  2 us
    pallas_call x1, Pallas kernels, queries_of(): pl.pallas_call(queries_kernel, out_shape=pltpu.VMEM((rows, width), jnp.bf...  1.92 us
    unnamed x24, local copies, waits for them, and re-layouts  1.5 us
    pallas_call x1, Pallas kernels, begin(): pl.pallas_call(functools.partial(begin_kernel, steps=steps), out_shape=ja...  1.24 us
  transfers between devices with their start and end apart: 10, of which 7 were waited for; matrix products, arithmetic and copies ran while one was open for 0% of the time, Pallas kernels for 10%

profile of v5, /device:TPU:0, one launch (start us, length us, event | category | flops | bytes accessed | tf_op | source)
XLA Modules:
  0.0 39.0 jit_solution(9854233366210878875)
XLA Ops:
  0.0 0.0 copy-start.1
  0.0 0.0 copy-start.2
  0.0 0.0 slice-start.7
  0.0 1.9 %queries.1.refs_0_ = bf16[256,128]{1,0:T(8,128)(2,1)S(1)} custom-call(bf16[4,64,128]{2,1,0:T(8,128)(2,1)} %bitcast.16, bf16[64,128,128]{2,1,0:T(8,128)(2,1)} %key_absorb.1), custom_call_target="tpu_custom_call" | custom-call | flops 5000000000 | tf_op jit(solution)/shard_map/queries/pallas_call | solution.py:78
  1.9 3.1 %collective-permute-start.2 = (bf16[256,128]{1,0:T(8,128)(2,1)S(1)}, bf16[256,128]{1,0:T(8,128)(2,1)S(1)}, u32[]{:S(2)}, u32[]{:S(2)}) collective-permute-start(bf16[256,128]{1,0:T(8,128)(2,1)S(1)} %queries.1.refs_0_), channel_id=1, source_target_pairs={{0,4},{4,0},{8,12},{12,8},{1,5},{5,1},{9,13},{13,9},{2,6},{6,2},{1... | collective-permute-start | bytes 196616 | tf_op jit(solution)/shard_map/ppermute | solution.py:27
  5.0 2.6 %collective-permute-start = (bf16[256,128]{1,0:T(8,128)(2,1)S(1)}, bf16[256,128]{1,0:T(8,128)(2,1)S(1)}, u32[]{:S(2)}, u32[]{:S(2)}) collective-permute-start(bf16[256,128]{1,0:T(8,128)(2,1)S(1)} %queries.1.refs_0_), channel_id=1, source_target_pairs={{0,8},{4,12},{8,0},{12,4},{1,9},{5,13},{9,1},{13,5},{2,10},{6,14},... | collective-permute-start | bytes 196616 | tf_op jit(solution)/shard_map/ppermute | solution.py:27
  7.6 0.0 collective-permute-start.1
  8.3 0.0 copy-done.1
  8.3 0.0 copy-done.2
  8.3 0.0 slice-start.8
  8.3 0.7 %prepare.1 = (f32[8,4096]{1,0:T(8,128)S(1)}, bf16[256,64]{1,0:T(8,128)(2,1)S(1)}) custom-call(s32[1]{0:T(128)S(6)} %copy.9.lengths, s32[4,32]{1,0:T(4,128)S(1)} %bitcast.15, bf16[4,64,64]{2,1,0:T(8,128)(2,1)S(1)} %bitcast.14), custom_call_target="tpu_custom_call" | custom-call | flops 12000000000 | tf_op jit(solution)/shard_map/prepare/pallas_call | solution.py:116
  9.0 0.0 collective-permute-done.2.refs_1_
  9.0 0.0 slice-done.7
  9.0 1.5 %slice-done.8 = s8[4194304]{0:T(1024)(128)(4,1)S(1)} async-done(((s8[4718592]{0:T(1024)(128)(4,1)}), s8[4194304]{0:T(1024)(128)(4,1)S(1)}, s32[]{:S(2)}) %slice-start.8) | async-done | bytes 4194328
  10.5 1.2 %begin.1.refs_2_ = f32[256,4096]{1,0:T(8,128)S(1)} custom-call(bf16[256,128]{1,0:T(8,128)(2,1)S(1)} %queries.1.refs_0_, bf16[256,128]{1,0:T(8,128)(2,1)S(1)} %collective-permute-done.2.refs_1_, bf16[256,64]{1,0:T(8,128)(2,1)S(1)} %get-tuple-element.13.refs_2_, bf16[576,4096]{1,0:T(8,128)(2,1)S(1)} %bitcast.12, f32[8,4096]{1,0:T(8,128)S(1)} %get-tuple-element.14.refs_4_), custom_call_target="tpu_custom_call" | custom-call | tf_op jit(solution)/shard_map/begin/pallas_call | solution.py:157
  11.7 0.6 %collective-permute-done.refs_0_ = bf16[256,128]{1,0:T(8,128)(2,1)S(1)} collective-permute-done((bf16[256,128]{1,0:T(8,128)(2,1)S(1)}, bf16[256,128]{1,0:T(8,128)(2,1)S(1)}, u32[]{:S(2)}, u32[]{:S(2)}) %collective-permute-start) | collective-permute-done | bytes 65568 | tf_op jit(solution)/shard_map/ppermute | solution.py:27
  12.3 1.4 %collective-permute-done.1.refs_1_ = bf16[256,128]{1,0:T(8,128)(2,1)S(1)} collective-permute-done((bf16[256,128]{1,0:T(8,128)(2,1)S(1)}, bf16[256,128]{1,0:T(8,128)(2,1)S(1)}, u32[]{:S(2)}, u32[]{:S(2)}) %collective-permute-start.1) | collective-permute-done | bytes 65568 | tf_op jit(solution)/shard_map/ppermute | solution.py:27
  13.7 2.7 %attend.1 = (bf16[272,128]{1,0:T(8,128)(2,1)S(1)}, bf16[272,128]{1,0:T(8,128)(2,1)S(1)}, bf16[272,128]{1,0:T(8,128)(2,1)S(1)}, bf16[272,128]{1,0:T(8,128)(2,1)S(1)}) custom-call(bf16[256,128]{1,0:T(8,128)(2,1)S(1)} %collective-permute-done.refs_0_, bf16[256,128]{1,0:T(8,128)(2,1)S(1)} %collective-permute-done.1.refs_1_, f32[256,4096]{1,0:T(8,128)S(1)} %begin.1.refs_2_, ...), custom_call_target="tpu_custom_call" | custom-call | tf_op jit(solution)/shard_map/attend/pallas_call | solution.py:204
  16.4 1.7 %collective-permute-start.3 = (bf16[272,128]{1,0:T(8,128)(2,1)S(1)}, bf16[272,128]{1,0:T(8,128)(2,1)S(1)}, u32[]{:S(2)}, u32[]{:S(2)}) collective-permute-start(bf16[272,128]{1,0:T(8,128)(2,1)S(1)} %get-tuple-element.16), channel_id=1, source_target_pairs={{0,8},{4,12},{8,0},{12,4},{1,9},{5,13},{9,1},{13,5},{2,10},{6,14},... | collective-permute-start | bytes 208904 | tf_op jit(solution)/shard_map/ppermute | solution.py:27
  18.0 0.7 %collective-permute-start.4 = (bf16[272,128]{1,0:T(8,128)(2,1)S(1)}, bf16[272,128]{1,0:T(8,128)(2,1)S(1)}, u32[]{:S(2)}, u32[]{:S(2)}) collective-permute-start(bf16[272,128]{1,0:T(8,128)(2,1)S(1)} %get-tuple-element.17), channel_id=1, source_target_pairs={{0,12},{4,8},{8,4},{12,0},{1,13},{5,9},{9,5},{13,1},{2,14},{6,10},... | collective-permute-start | bytes 208904 | tf_op jit(solution)/shard_map/ppermute | solution.py:27
  18.7 1.2 %collective-permute-start.5 = (bf16[272,128]{1,0:T(8,128)(2,1)S(1)}, bf16[272,128]{1,0:T(8,128)(2,1)S(1)}, u32[]{:S(2)}, u32[]{:S(2)}) collective-permute-start(bf16[272,128]{1,0:T(8,128)(2,1)S(1)} %get-tuple-element.18), channel_id=1, source_target_pairs={{0,4},{4,0},{8,12},{12,8},{1,5},{5,1},{9,13},{13,9},{2,6},{6,2},{1... | collective-permute-start | bytes 208904 | tf_op jit(solution)/shard_map/ppermute | solution.py:27
  20.0 0.0 slice-start.3
  20.0 0.0 slice-start.4
  20.0 0.0 slice-start.5
  20.0 0.0 slice-start.6
  20.0 2.7 %collective-permute-done.3.refs_1_ = bf16[272,128]{1,0:T(8,128)(2,1)S(1)} collective-permute-done((bf16[272,128]{1,0:T(8,128)(2,1)S(1)}, bf16[272,128]{1,0:T(8,128)(2,1)S(1)}, u32[]{:S(2)}, u32[]{:S(2)}) %collective-permute-start.3) | collective-permute-done | bytes 69664 | tf_op jit(solution)/shard_map/ppermute | solution.py:27
  22.7 1.5 %collective-permute-done.4.refs_2_ = bf16[272,128]{1,0:T(8,128)(2,1)S(1)} collective-permute-done((bf16[272,128]{1,0:T(8,128)(2,1)S(1)}, bf16[272,128]{1,0:T(8,128)(2,1)S(1)}, u32[]{:S(2)}, u32[]{:S(2)}) %collective-permute-start.4) | collective-permute-done | bytes 69664 | tf_op jit(solution)/shard_map/ppermute | solution.py:27
  24.2 0.0 collective-permute-done.5.refs_3_
  24.2 0.0 copy-done
  24.2 0.5 %values.1.refs_0_ = bf16[256,128]{1,0:T(8,128)(2,1)S(1)} custom-call(bf16[272,128]{1,0:T(8,128)(2,1)S(1)} %keep.1.refs_0_, bf16[272,128]{1,0:T(8,128)(2,1)S(1)} %collective-permute-done.3.refs_1_, bf16[272,128]{1,0:T(8,128)(2,1)S(1)} %collective-permute-done.4.refs_2_, bf16[272,128]{1,0:T(8,128)(2,1)S(1)} %collective-permute-done.5.refs_3_, ...), custom_call_target="tpu_custom_call" | custom-call | tf_op jit(solution)/shard_map/values/pallas_call | solution.py:262
  24.7 1.8 %collective-permute-start.6 = (bf16[256,128]{1,0:T(8,128)(2,1)S(1)}, bf16[256,128]{1,0:T(8,128)(2,1)S(1)}, u32[]{:S(2)}, u32[]{:S(2)}) collective-permute-start(bf16[256,128]{1,0:T(8,128)(2,1)S(1)} %values.1.refs_0_), channel_id=1, source_target_pairs={{0,8},{4,12},{8,0},{12,4},{1,9},{5,13},{9,1},{13,5},{2,10},{6,14},... | collective-permute-start | bytes 196616 | tf_op jit(solution)/shard_map/ppermute | solution.py:27
  26.5 0.7 %collective-permute-start.7 = (bf16[256,128]{1,0:T(8,128)(2,1)S(1)}, bf16[256,128]{1,0:T(8,128)(2,1)S(1)}, u32[]{:S(2)}, u32[]{:S(2)}) collective-permute-start(bf16[256,128]{1,0:T(8,128)(2,1)S(1)} %values.1.refs_0_), channel_id=1, source_target_pairs={{0,12},{4,8},{8,4},{12,0},{1,13},{5,9},{9,5},{13,1},{2,14},{6,10},... | collective-permute-start | bytes 196616 | tf_op jit(solution)/shard_map/ppermute | solution.py:27
  27.2 1.0 %collective-permute-start.8 = (bf16[256,128]{1,0:T(8,128)(2,1)S(1)}, bf16[256,128]{1,0:T(8,128)(2,1)S(1)}, u32[]{:S(2)}, u32[]{:S(2)}) collective-permute-start(bf16[256,128]{1,0:T(8,128)(2,1)S(1)} %values.1.refs_0_), channel_id=1, source_target_pairs={{0,4},{4,0},{8,12},{12,8},{1,5},{5,1},{9,13},{13,9},{2,6},{6,2},{1... | collective-permute-start | bytes 196616 | tf_op jit(solution)/shard_map/ppermute | solution.py:27
  28.2 2.9 %collective-permute-done.6.refs_1_ = bf16[256,128]{1,0:T(8,128)(2,1)S(1)} collective-permute-done((bf16[256,128]{1,0:T(8,128)(2,1)S(1)}, bf16[256,128]{1,0:T(8,128)(2,1)S(1)}, u32[]{:S(2)}, u32[]{:S(2)}) %collective-permute-start.6) | collective-permute-done | bytes 65568 | tf_op jit(solution)/shard_map/ppermute | solution.py:27
  31.2 1.4 %collective-permute-done.7.refs_2_ = bf16[256,128]{1,0:T(8,128)(2,1)S(1)} collective-permute-done((bf16[256,128]{1,0:T(8,128)(2,1)S(1)}, bf16[256,128]{1,0:T(8,128)(2,1)S(1)}, u32[]{:S(2)}, u32[]{:S(2)}) %collective-permute-start.7) | collective-permute-done | bytes 65568 | tf_op jit(solution)/shard_map/ppermute | solution.py:27
  32.5 0.0 collective-permute-done.8.refs_3_
  32.6 0.0 slice-done
  32.6 0.0 slice-done.1
  32.6 0.0 slice-done.2
  32.6 0.0 slice-done.3
  32.6 0.0 slice-done.4
  32.6 0.0 slice-done.5
  32.6 0.0 slice-done.6
  32.6 2.0 %theirs.1 = (f32[4,896]{1,0:T(4,128)S(1)}, bf16[4,8192]{1,0:T(4,128)(2,1)S(1)}) custom-call(bf16[256,128]{1,0:T(8,128)(2,1)S(1)} %values.1.refs_0_, bf16[256,128]{1,0:T(8,128)(2,1)S(1)} %collective-permute-done.6.refs_1_, bf16[256,128]{1,0:T(8,128)(2,1)S(1)} %collective-permute-done.7.refs_2_, bf16[256,128]{1,0:T(8,128)(2,1)S(1)} %collective-permute-done.8.refs_3_, ...), custom_call_target="tpu_custom_call" | custom-call | tf_op jit(solution)/shard_map/theirs/pallas_call | solution.py:294
  34.7 1.5 %collective-permute-start.9 = (f32[4,896]{1,0:T(4,128)S(1)}, f32[4,896]{1,0:T(4,128)S(1)}, u32[]{:S(2)}, u32[]{:S(2)}) collective-permute-start(f32[4,896]{1,0:T(4,128)S(1)} %get-tuple-element.20), channel_id=1, source_target_pairs={{0,2},{2,0},{1,3},{3,1},{4,6},{6,4},{5,7},{7,5},{8,10},{10,8},{9,1... | collective-permute-start | bytes 43016 | tf_op jit(solution)/shard_map/ppermute | solution.py:27
  36.2 2.0 %mine.1 = f32[4,896]{1,0:T(4,128)S(1)} custom-call(bf16[4,8192]{1,0:T(4,128)(2,1)S(1)} %get-tuple-element.19.flat, bf16[8192,1792]{1,0:T(8,128)(2,1)S(1)} %bitcast.9), custom_call_target="tpu_custom_call" | custom-call | flops 2000000000 | tf_op jit(solution)/shard_map/mine/pallas_call | solution.py:313
  38.2 0.2 collective-permute-done.9
  38.4 0.6 %fusion = bf16[1,4,896]{2,1,0:T(4,128)(2,1)} fusion(f32[4,896]{1,0:T(4,128)S(1)} %mine.1, f32[4,896]{1,0:T(4,128)S(1)} %collective-permute-done.9), kind=kLoop, calls=%fused_computation.1 | loop fusion | flops 7168 | bytes 35840 | tf_op jit(solution)/shard_map/broadcast_in_dim | solution.py:384
  (7 shorter events, 0.0 us)
Async XLA Ops:
  0.0 8.3 %copy-start.1 = (bf16[1,4,64,64]{3,2,1,0:T(8,128)(2,1)S(1)}, bf16[1,4,64,64]{3,2,1,0:T(8,128)(2,1)}, u32[]{:S(2)}) copy-start(bf16[1,4,64,64]{3,2,1,0:T(8,128)(2,1)} %param.9) | copy-start | bytes 98308
  0.0 8.3 %copy-start.2 = (s32[1,4,32]{2,1,0:T(4,128)S(1)}, s32[1,4,32]{2,1,0:T(4,128)}, u32[]{:S(2)}) copy-start(s32[1,4,32]{2,1,0:T(4,128)} %param.12) | copy-start | bytes 1540
  0.0 9.0 %slice-start.7 = ((s8[4718592]{0:T(1024)(128)(4,1)}), s8[524288]{0:T(1024)(128)(4,1)S(1)}, s32[]{:S(2)}) async-start(s8[4718592]{0:T(1024)(128)(4,1)} %bitcast.10), calls=%async_computation.7 | async-start | bytes 1048576
  1.9 7.1 %collective-permute-start.2 = (bf16[256,128]{1,0:T(8,128)(2,1)S(1)}, bf16[256,128]{1,0:T(8,128)(2,1)S(1)}, u32[]{:S(2)}, u32[]{:S(2)}) collective-permute-start(bf16[256,128]{1,0:T(8,128)(2,1)S(1)} %queries.1.refs_0_), channel_id=1, source_target_pairs={{0,4},{4,0},{8,12},{12,8},{1,5},{5,1},{9,13},{13,9},{2,6},{6,2},{1... | collective-permute-start | bytes 196616 | tf_op jit(solution)/shard_map/ppermute | solution.py:27
  5.0 7.3 %collective-permute-start = (bf16[256,128]{1,0:T(8,128)(2,1)S(1)}, bf16[256,128]{1,0:T(8,128)(2,1)S(1)}, u32[]{:S(2)}, u32[]{:S(2)}) collective-permute-start(bf16[256,128]{1,0:T(8,128)(2,1)S(1)} %queries.1.refs_0_), channel_id=1, source_target_pairs={{0,8},{4,12},{8,0},{12,4},{1,9},{5,13},{9,1},{13,5},{2,10},{6,14},... | collective-permute-start | bytes 196616 | tf_op jit(solution)/shard_map/ppermute | solution.py:27
  7.6 6.1 %collective-permute-start.1 = (bf16[256,128]{1,0:T(8,128)(2,1)S(1)}, bf16[256,128]{1,0:T(8,128)(2,1)S(1)}, u32[]{:S(2)}, u32[]{:S(2)}) collective-permute-start(bf16[256,128]{1,0:T(8,128)(2,1)S(1)} %queries.1.refs_0_), channel_id=1, source_target_pairs={{0,12},{4,8},{8,4},{12,0},{1,13},{5,9},{9,5},{13,1},{2,14},{6,10},... | collective-permute-start | bytes 196616 | tf_op jit(solution)/shard_map/ppermute | solution.py:27
  8.3 2.2 %slice-start.8 = ((s8[4718592]{0:T(1024)(128)(4,1)}), s8[4194304]{0:T(1024)(128)(4,1)S(1)}, s32[]{:S(2)}) async-start(s8[4718592]{0:T(1024)(128)(4,1)} %bitcast.10), calls=%async_computation.8 | async-start | bytes 8388608
  16.4 6.3 %collective-permute-start.3 = (bf16[272,128]{1,0:T(8,128)(2,1)S(1)}, bf16[272,128]{1,0:T(8,128)(2,1)S(1)}, u32[]{:S(2)}, u32[]{:S(2)}) collective-permute-start(bf16[272,128]{1,0:T(8,128)(2,1)S(1)} %get-tuple-element.16), channel_id=1, source_target_pairs={{0,8},{4,12},{8,0},{12,4},{1,9},{5,13},{9,1},{13,5},{2,10},{6,14},... | collective-permute-start | bytes 208904 | tf_op jit(solution)/shard_map/ppermute | solution.py:27
  18.0 6.1 %collective-permute-start.4 = (bf16[272,128]{1,0:T(8,128)(2,1)S(1)}, bf16[272,128]{1,0:T(8,128)(2,1)S(1)}, u32[]{:S(2)}, u32[]{:S(2)}) collective-permute-start(bf16[272,128]{1,0:T(8,128)(2,1)S(1)} %get-tuple-element.17), channel_id=1, source_target_pairs={{0,12},{4,8},{8,4},{12,0},{1,13},{5,9},{9,5},{13,1},{2,14},{6,10},... | collective-permute-start | bytes 208904 | tf_op jit(solution)/shard_map/ppermute | solution.py:27
  18.7 5.5 %collective-permute-start.5 = (bf16[272,128]{1,0:T(8,128)(2,1)S(1)}, bf16[272,128]{1,0:T(8,128)(2,1)S(1)}, u32[]{:S(2)}, u32[]{:S(2)}) collective-permute-start(bf16[272,128]{1,0:T(8,128)(2,1)S(1)} %get-tuple-element.18), channel_id=1, source_target_pairs={{0,4},{4,0},{8,12},{12,8},{1,5},{5,1},{9,13},{13,9},{2,6},{6,2},{1... | collective-permute-start | bytes 208904 | tf_op jit(solution)/shard_map/ppermute | solution.py:27
  19.9 12.6 %slice-start = ((s8[29360128]{0:T(1024)(128)(4,1)}), s8[4194304]{0:T(1024)(128)(4,1)S(1)}, s32[]{:S(2)}) async-start(s8[29360128]{0:T(1024)(128)(4,1)} %bitcast.8), calls=%async_computation | async-start | bytes 8388608
  19.9 4.2 %copy-start = (bf16[64,128,128]{2,1,0:T(8,128)(2,1)S(1)}, bf16[64,128,128]{2,1,0:T(8,128)(2,1)}, u32[]{:S(2)}) copy-start(bf16[64,128,128]{2,1,0:T(8,128)(2,1)} %refs_4_.2) | copy-start | bytes 6291460
  20.0 12.6 %slice-start.1 = ((s8[29360128]{0:T(1024)(128)(4,1)}), s8[4194304]{0:T(1024)(128)(4,1)S(1)}, s32[]{:S(2)}) async-start(s8[29360128]{0:T(1024)(128)(4,1)} %bitcast.8), calls=%async_computation.1 | async-start | bytes 8388608
  20.0 12.6 %slice-start.2 = ((s8[29360128]{0:T(1024)(128)(4,1)}), s8[4194304]{0:T(1024)(128)(4,1)S(1)}, s32[]{:S(2)}) async-start(s8[29360128]{0:T(1024)(128)(4,1)} %bitcast.8), calls=%async_computation.2 | async-start | bytes 8388608
  20.0 12.6 %slice-start.3 = ((s8[29360128]{0:T(1024)(128)(4,1)}), s8[4194304]{0:T(1024)(128)(4,1)S(1)}, s32[]{:S(2)}) async-start(s8[29360128]{0:T(1024)(128)(4,1)} %bitcast.8), calls=%async_computation.3 | async-start | bytes 8388608
  20.0 12.6 %slice-start.4 = ((s8[29360128]{0:T(1024)(128)(4,1)}), s8[4194304]{0:T(1024)(128)(4,1)S(1)}, s32[]{:S(2)}) async-start(s8[29360128]{0:T(1024)(128)(4,1)} %bitcast.8), calls=%async_computation.4 | async-start | bytes 8388608
  20.0 12.6 %slice-start.5 = ((s8[29360128]{0:T(1024)(128)(4,1)}), s8[4194304]{0:T(1024)(128)(4,1)S(1)}, s32[]{:S(2)}) async-start(s8[29360128]{0:T(1024)(128)(4,1)} %bitcast.8), calls=%async_computation.5 | async-start | bytes 8388608
  20.0 12.6 %slice-start.6 = ((s8[29360128]{0:T(1024)(128)(4,1)}), s8[4194304]{0:T(1024)(128)(4,1)S(1)}, s32[]{:S(2)}) async-start(s8[29360128]{0:T(1024)(128)(4,1)} %bitcast.8), calls=%async_computation.6 | async-start | bytes 8388608
  24.7 6.5 %collective-permute-start.6 = (bf16[256,128]{1,0:T(8,128)(2,1)S(1)}, bf16[256,128]{1,0:T(8,128)(2,1)S(1)}, u32[]{:S(2)}, u32[]{:S(2)}) collective-permute-start(bf16[256,128]{1,0:T(8,128)(2,1)S(1)} %values.1.refs_0_), channel_id=1, source_target_pairs={{0,8},{4,12},{8,0},{12,4},{1,9},{5,13},{9,1},{13,5},{2,10},{6,14},... | collective-permute-start | bytes 196616 | tf_op jit(solution)/shard_map/ppermute | solution.py:27
  26.5 6.1 %collective-permute-start.7 = (bf16[256,128]{1,0:T(8,128)(2,1)S(1)}, bf16[256,128]{1,0:T(8,128)(2,1)S(1)}, u32[]{:S(2)}, u32[]{:S(2)}) collective-permute-start(bf16[256,128]{1,0:T(8,128)(2,1)S(1)} %values.1.refs_0_), channel_id=1, source_target_pairs={{0,12},{4,8},{8,4},{12,0},{1,13},{5,9},{9,5},{13,1},{2,14},{6,10},... | collective-permute-start | bytes 196616 | tf_op jit(solution)/shard_map/ppermute | solution.py:27
  27.2 5.4 %collective-permute-start.8 = (bf16[256,128]{1,0:T(8,128)(2,1)S(1)}, bf16[256,128]{1,0:T(8,128)(2,1)S(1)}, u32[]{:S(2)}, u32[]{:S(2)}) collective-permute-start(bf16[256,128]{1,0:T(8,128)(2,1)S(1)} %values.1.refs_0_), channel_id=1, source_target_pairs={{0,4},{4,0},{8,12},{12,8},{1,5},{5,1},{9,13},{13,9},{2,6},{6,2},{1... | collective-permute-start | bytes 196616 | tf_op jit(solution)/shard_map/ppermute | solution.py:27
  34.7 3.8 %collective-permute-start.9 = (f32[4,896]{1,0:T(4,128)S(1)}, f32[4,896]{1,0:T(4,128)S(1)}, u32[]{:S(2)}, u32[]{:S(2)}) collective-permute-start(f32[4,896]{1,0:T(4,128)S(1)} %get-tuple-element.20), channel_id=1, source_target_pairs={{0,2},{2,0},{1,3},{3,1},{4,6},{6,4},{5,7},{7,5},{8,10},{10,8},{9,1... | collective-permute-start | bytes 43016 | tf_op jit(solution)/shard_map/ppermute | solution.py:27

commit v6 on v5

--- a/solution.py
+++ b/solution.py
@@ -8,8 +8,9 @@
 from jax.sharding import PartitionSpec as P
 
 BLK = 64
-FEW = 4
+PEERS = 4
 LANES = 128
+CHUNK = 512
 TAIL = 16
 LOG2E = 1.4426950408889634
 HIDDEN = -1e30
@@ -25,6 +26,11 @@
 def swap(value, axis, step):
     count = lax.axis_size(axis)
     return lax.ppermute(value, axis, [(i, i ^ step) for i in range(count)])
+
+
+def turn(value, axis, step):
+    order = (0, 1, 3, 2)
+    return lax.ppermute(value, axis, [(order[i], order[(i + step) % 4]) for i in range(4)])
 
 
 def thirds(value):
@@ -177,14 +183,20 @@
             preferred_element_type=jnp.float32,
         )
     top = jnp.max(scores, axis=1, keepdims=True)
-    weights = jnp.exp2((scores - top) * (scale * LOG2E))
-    total = jnp.sum(weights, axis=1, keepdims=True)
-    total_sums[...] = lax.dot_general(
-        weights.astype(jnp.bfloat16),
-        cache[:latent, :],
-        (((1,), (1,)), ((), ())),
-        preferred_element_type=jnp.float32,
-    )
+    tokens = scores.shape[1]
+    total = jnp.zeros((rows, 1), jnp.float32)
+    sums = jnp.zeros((rows, latent), jnp.float32)
+    for first in range(0, tokens, CHUNK):
+        at = slice(first, first + CHUNK)
+        weights = jnp.exp2((scores[:, at] - top) * (scale * LOG2E))
+        total += jnp.sum(weights, axis=1, keepdims=True)
+        sums += lax.dot_general(
+            weights.astype(jnp.bfloat16),
+            cache[:latent, at],
+            (((1,), (1,)), ((), ())),
+            preferred_element_type=jnp.float32,
+        )
+    total_sums[...] = sums
 
     lines = []
     for value in (top * scale, total):
@@ -347,7 +359,7 @@
     scale = (nope + rope) ** (-0.5)
     rows, latent = drafts * heads, latent_cache.shape[2] - rope
     peers = lax.axis_size("ctx")
-    few = peers <= FEW and lax.axis_size("head") == 2 and key_absorb.shape[2] == LANES
+    few = peers == PEERS and lax.axis_size("head") == 2 and key_absorb.shape[2] == LANES
 
     q_piece = queries_of(query_nope[0], key_absorb)
     bias, rope_rows = prepare(lengths, block_ids[0], query_rope[0], tokens)
@@ -362,7 +374,7 @@
         )
         blocks = [keep(blocks[0])] + [swap(blocks[step], "ctx", step) for step in (2, 3, 1)]
         partial = values_of(blocks, value_absorb, drafts)
-        partials = [partial] + [swap(partial, "ctx", step) for step in (2, 3, 1)]
+        partials = [partial] + [turn(partial, "ctx", step) for step in (2, 1, 3)]
         theirs, flat = theirs_of(partials, output_weight, drafts)
         summed = mine_of(flat, output_weight) + swap(theirs, "head", 1)
     else:

time: 39.2 us -> 38.8 us (0.990)
  waiting for transfers between devices: 10.7 us -> 8.66 us
  starting transfers between devices: 14.3 us -> 16 us
    ppermute x0 -> x3, starting transfers between devices: none -> 5.23 us  [turn(): lax.ppermute(value, axis, [(order[i], order[(i + step) % 4]) for i in ran...]
    ppermute x10 -> x7, waiting for transfers between devices: 10.7 us -> 6.33 us  [swap(): return lax.ppermute(value, axis, [(i, i ^ step) for i in range(count)])]
    ppermute x10 -> x7, starting transfers between devices: 14.3 us -> 10.8 us  [swap(): return lax.ppermute(value, axis, [(i, i ^ step) for i in range(count)])]
    ppermute x0 -> x3, waiting for transfers between devices: none -> 2.33 us  [turn(): lax.ppermute(value, axis, [(order[i], order[(i + step) % 4]) for i in ran...]
where the time goes in v6:
time: 38.8 us; the launch traced here: 38.6 us
  starting transfers between devices  16 us (41%)
  Pallas kernels  11 us (28%)
  waiting for transfers between devices  8.66 us (22%)
  local copies, waits for them, and re-layouts  1.5 us (4%)
  between operations  0.84 us (2%)
  other arithmetic  0.6 us (2%)
    ppermute x7, starting transfers between devices, swap(): return lax.ppermute(value, axis, [(i, i ^ step) for i in range(count)])  10.8 us
    ppermute x7, waiting for transfers between devices, swap(): return lax.ppermute(value, axis, [(i, i ^ step) for i in range(count)])  6.33 us
    ppermute x3, starting transfers between devices, turn(): lax.ppermute(value, axis, [(order[i], order[(i + step) % 4]) for i in ran...  5.23 us
    pallas_call x1, Pallas kernels, attend(): pl.pallas_call(functools.partial(attend_kernel, steps=steps, outs_of=outs...  2.57 us
    ppermute x3, waiting for transfers between devices, turn(): lax.ppermute(value, axis, [(order[i], order[(i + step) % 4]) for i in ran...  2.33 us
    pallas_call x1, Pallas kernels, theirs_of(): pl.pallas_call(functools.partial(theirs_kernel, drafts=drafts), out_shape...  2.04 us
    pallas_call x1, Pallas kernels, mine_of(): pl.pallas_call(mine_kernel, out_shape=jax.ShapeDtypeStruct((flat.shape[0]...  2 us
    pallas_call x1, Pallas kernels, queries_of(): pl.pallas_call(queries_kernel, out_shape=pltpu.VMEM((rows, width), jnp.bf...  1.92 us
  transfers between devices with their start and end apart: 10, of which 7 were waited for; matrix products, arithmetic and copies ran while one was open for 0% of the time, Pallas kernels for 10%

profile of v6, /device:TPU:0, one launch (start us, length us, event | category | flops | bytes accessed | tf_op | source)
XLA Modules:
  0.0 38.6 jit_solution(4862195459702751698)
XLA Ops:
  0.0 0.0 copy-start.1
  0.0 0.0 copy-start.2
  0.0 0.0 slice-start.7
  0.0 1.9 %queries.1.refs_0_ = bf16[256,128]{1,0:T(8,128)(2,1)S(1)} custom-call(bf16[4,64,128]{2,1,0:T(8,128)(2,1)} %bitcast.16, bf16[64,128,128]{2,1,0:T(8,128)(2,1)} %key_absorb.1), custom_call_target="tpu_custom_call" | custom-call | flops 5000000000 | tf_op jit(solution)/shard_map/queries/pallas_call | solution.py:84
  1.9 3.1 %collective-permute-start.2 = (bf16[256,128]{1,0:T(8,128)(2,1)S(1)}, bf16[256,128]{1,0:T(8,128)(2,1)S(1)}, u32[]{:S(2)}, u32[]{:S(2)}) collective-permute-start(bf16[256,128]{1,0:T(8,128)(2,1)S(1)} %queries.1.refs_0_), channel_id=1, source_target_pairs={{0,4},{4,0},{8,12},{12,8},{1,5},{5,1},{9,13},{13,9},{2,6},{6,2},{1... | collective-permute-start | bytes 196616 | tf_op jit(solution)/shard_map/ppermute | solution.py:28
  5.0 2.6 %collective-permute-start = (bf16[256,128]{1,0:T(8,128)(2,1)S(1)}, bf16[256,128]{1,0:T(8,128)(2,1)S(1)}, u32[]{:S(2)}, u32[]{:S(2)}) collective-permute-start(bf16[256,128]{1,0:T(8,128)(2,1)S(1)} %queries.1.refs_0_), channel_id=1, source_target_pairs={{0,8},{4,12},{8,0},{12,4},{1,9},{5,13},{9,1},{13,5},{2,10},{6,14},... | collective-permute-start | bytes 196616 | tf_op jit(solution)/shard_map/ppermute | solution.py:28
  7.6 0.0 collective-permute-start.1
  8.3 0.0 copy-done.1
  8.3 0.0 copy-done.2
  8.3 0.0 slice-start.8
  8.3 0.7 %prepare.1 = (f32[8,4096]{1,0:T(8,128)S(1)}, bf16[256,64]{1,0:T(8,128)(2,1)S(1)}) custom-call(s32[1]{0:T(128)S(6)} %copy.9.lengths, s32[4,32]{1,0:T(4,128)S(1)} %bitcast.15, bf16[4,64,64]{2,1,0:T(8,128)(2,1)S(1)} %bitcast.14), custom_call_target="tpu_custom_call" | custom-call | flops 12000000000 | tf_op jit(solution)/shard_map/prepare/pallas_call | solution.py:122
  9.0 0.0 collective-permute-done.2.refs_1_
  9.0 0.0 slice-done.7
  9.0 1.5 %slice-done.8 = s8[4194304]{0:T(1024)(128)(4,1)S(1)} async-done(((s8[4718592]{0:T(1024)(128)(4,1)}), s8[4194304]{0:T(1024)(128)(4,1)S(1)}, s32[]{:S(2)}) %slice-start.8) | async-done | bytes 4194328
  10.5 1.2 %begin.1.refs_2_ = f32[256,4096]{1,0:T(8,128)S(1)} custom-call(bf16[256,128]{1,0:T(8,128)(2,1)S(1)} %queries.1.refs_0_, bf16[256,128]{1,0:T(8,128)(2,1)S(1)} %collective-permute-done.2.refs_1_, bf16[256,64]{1,0:T(8,128)(2,1)S(1)} %get-tuple-element.13.refs_2_, bf16[576,4096]{1,0:T(8,128)(2,1)S(1)} %bitcast.12, f32[8,4096]{1,0:T(8,128)S(1)} %get-tuple-element.14.refs_4_), custom_call_target="tpu_custom_call" | custom-call | tf_op jit(solution)/shard_map/begin/pallas_call | solution.py:163
  11.7 0.6 %collective-permute-done.refs_0_ = bf16[256,128]{1,0:T(8,128)(2,1)S(1)} collective-permute-done((bf16[256,128]{1,0:T(8,128)(2,1)S(1)}, bf16[256,128]{1,0:T(8,128)(2,1)S(1)}, u32[]{:S(2)}, u32[]{:S(2)}) %collective-permute-start) | collective-permute-done | bytes 65568 | tf_op jit(solution)/shard_map/ppermute | solution.py:28
  12.3 1.4 %collective-permute-done.1.refs_1_ = bf16[256,128]{1,0:T(8,128)(2,1)S(1)} collective-permute-done((bf16[256,128]{1,0:T(8,128)(2,1)S(1)}, bf16[256,128]{1,0:T(8,128)(2,1)S(1)}, u32[]{:S(2)}, u32[]{:S(2)}) %collective-permute-start.1) | collective-permute-done | bytes 65568 | tf_op jit(solution)/shard_map/ppermute | solution.py:28
  13.7 2.6 %attend.1 = (bf16[272,128]{1,0:T(8,128)(2,1)S(1)}, bf16[272,128]{1,0:T(8,128)(2,1)S(1)}, bf16[272,128]{1,0:T(8,128)(2,1)S(1)}, bf16[272,128]{1,0:T(8,128)(2,1)S(1)}) custom-call(bf16[256,128]{1,0:T(8,128)(2,1)S(1)} %collective-permute-done.refs_0_, bf16[256,128]{1,0:T(8,128)(2,1)S(1)} %collective-permute-done.1.refs_1_, f32[256,4096]{1,0:T(8,128)S(1)} %begin.1.refs_2_, ...), custom_call_target="tpu_custom_call" | custom-call | tf_op jit(solution)/shard_map/attend/pallas_call | solution.py:216
  16.3 1.7 %collective-permute-start.3 = (bf16[272,128]{1,0:T(8,128)(2,1)S(1)}, bf16[272,128]{1,0:T(8,128)(2,1)S(1)}, u32[]{:S(2)}, u32[]{:S(2)}) collective-permute-start(bf16[272,128]{1,0:T(8,128)(2,1)S(1)} %get-tuple-element.16), channel_id=1, source_target_pairs={{0,8},{4,12},{8,0},{12,4},{1,9},{5,13},{9,1},{13,5},{2,10},{6,14},... | collective-permute-start | bytes 208904 | tf_op jit(solution)/shard_map/ppermute | solution.py:28
  17.9 0.7 %collective-permute-start.4 = (bf16[272,128]{1,0:T(8,128)(2,1)S(1)}, bf16[272,128]{1,0:T(8,128)(2,1)S(1)}, u32[]{:S(2)}, u32[]{:S(2)}) collective-permute-start(bf16[272,128]{1,0:T(8,128)(2,1)S(1)} %get-tuple-element.17), channel_id=1, source_target_pairs={{0,12},{4,8},{8,4},{12,0},{1,13},{5,9},{9,5},{13,1},{2,14},{6,10},... | collective-permute-start | bytes 208904 | tf_op jit(solution)/shard_map/ppermute | solution.py:28
  18.6 1.2 %collective-permute-start.5 = (bf16[272,128]{1,0:T(8,128)(2,1)S(1)}, bf16[272,128]{1,0:T(8,128)(2,1)S(1)}, u32[]{:S(2)}, u32[]{:S(2)}) collective-permute-start(bf16[272,128]{1,0:T(8,128)(2,1)S(1)} %get-tuple-element.18), channel_id=1, source_target_pairs={{0,4},{4,0},{8,12},{12,8},{1,5},{5,1},{9,13},{13,9},{2,6},{6,2},{1... | collective-permute-start | bytes 208904 | tf_op jit(solution)/shard_map/ppermute | solution.py:28
  19.8 0.0 slice-start.3
  19.8 0.0 slice-start.4
  19.9 0.0 slice-start.5
  19.9 0.0 slice-start.6
  19.9 2.7 %collective-permute-done.3.refs_1_ = bf16[272,128]{1,0:T(8,128)(2,1)S(1)} collective-permute-done((bf16[272,128]{1,0:T(8,128)(2,1)S(1)}, bf16[272,128]{1,0:T(8,128)(2,1)S(1)}, u32[]{:S(2)}, u32[]{:S(2)}) %collective-permute-start.3) | collective-permute-done | bytes 69664 | tf_op jit(solution)/shard_map/ppermute | solution.py:28
  22.6 1.5 %collective-permute-done.4.refs_2_ = bf16[272,128]{1,0:T(8,128)(2,1)S(1)} collective-permute-done((bf16[272,128]{1,0:T(8,128)(2,1)S(1)}, bf16[272,128]{1,0:T(8,128)(2,1)S(1)}, u32[]{:S(2)}, u32[]{:S(2)}) %collective-permute-start.4) | collective-permute-done | bytes 69664 | tf_op jit(solution)/shard_map/ppermute | solution.py:28
  24.0 0.0 collective-permute-done.5.refs_3_
  24.0 0.0 copy-done
  24.0 0.5 %values.1.refs_0_ = bf16[256,128]{1,0:T(8,128)(2,1)S(1)} custom-call(bf16[272,128]{1,0:T(8,128)(2,1)S(1)} %keep.1.refs_0_, bf16[272,128]{1,0:T(8,128)(2,1)S(1)} %collective-permute-done.3.refs_1_, bf16[272,128]{1,0:T(8,128)(2,1)S(1)} %collective-permute-done.4.refs_2_, bf16[272,128]{1,0:T(8,128)(2,1)S(1)} %collective-permute-done.5.refs_3_, ...), custom_call_target="tpu_custom_call" | custom-call | tf_op jit(solution)/shard_map/values/pallas_call | solution.py:274
  24.5 2.3 %collective-permute-start.6 = (bf16[256,128]{1,0:T(8,128)(2,1)S(1)}, bf16[256,128]{1,0:T(8,128)(2,1)S(1)}, u32[]{:S(2)}, u32[]{:S(2)}) collective-permute-start(bf16[256,128]{1,0:T(8,128)(2,1)S(1)} %values.1.refs_0_), channel_id=1, source_target_pairs={{0,12},{4,8},{12,0},{8,4},{1,13},{5,9},{13,1},{9,5},{2,14},{6,10},... | collective-permute-start | bytes 196616 | tf_op jit(solution)/shard_map/ppermute | solution.py:33
  26.8 0.1 collective-permute-start.7
  26.9 2.8 %collective-permute-start.8 = (bf16[256,128]{1,0:T(8,128)(2,1)S(1)}, bf16[256,128]{1,0:T(8,128)(2,1)S(1)}, u32[]{:S(2)}, u32[]{:S(2)}) collective-permute-start(bf16[256,128]{1,0:T(8,128)(2,1)S(1)} %values.1.refs_0_), channel_id=1, source_target_pairs={{0,8},{4,0},{12,4},{8,12},{1,9},{5,1},{13,5},{9,13},{2,10},{6,2},{... | collective-permute-start | bytes 196616 | tf_op jit(solution)/shard_map/ppermute | solution.py:33
  29.8 0.9 %collective-permute-done.6.refs_1_ = bf16[256,128]{1,0:T(8,128)(2,1)S(1)} collective-permute-done((bf16[256,128]{1,0:T(8,128)(2,1)S(1)}, bf16[256,128]{1,0:T(8,128)(2,1)S(1)}, u32[]{:S(2)}, u32[]{:S(2)}) %collective-permute-start.6) | collective-permute-done | bytes 65568 | tf_op jit(solution)/shard_map/ppermute | solution.py:33
  30.7 1.4 %collective-permute-done.7.refs_2_ = bf16[256,128]{1,0:T(8,128)(2,1)S(1)} collective-permute-done((bf16[256,128]{1,0:T(8,128)(2,1)S(1)}, bf16[256,128]{1,0:T(8,128)(2,1)S(1)}, u32[]{:S(2)}, u32[]{:S(2)}) %collective-permute-start.7) | collective-permute-done | bytes 65568 | tf_op jit(solution)/shard_map/ppermute | solution.py:33
  32.1 0.0 collective-permute-done.8.refs_3_
  32.1 0.0 slice-done
  32.1 0.0 slice-done.1
  32.1 0.0 slice-done.2
  32.1 0.0 slice-done.3
  32.1 0.0 slice-done.4
  32.1 0.0 slice-done.5
  32.2 0.0 slice-done.6
  32.2 2.0 %theirs.1 = (f32[4,896]{1,0:T(4,128)S(1)}, bf16[4,8192]{1,0:T(4,128)(2,1)S(1)}) custom-call(bf16[256,128]{1,0:T(8,128)(2,1)S(1)} %values.1.refs_0_, bf16[256,128]{1,0:T(8,128)(2,1)S(1)} %collective-permute-done.6.refs_1_, bf16[256,128]{1,0:T(8,128)(2,1)S(1)} %collective-permute-done.7.refs_2_, bf16[256,128]{1,0:T(8,128)(2,1)S(1)} %collective-permute-done.8.refs_3_, ...), custom_call_target="tpu_custom_call" | custom-call | tf_op jit(solution)/shard_map/theirs/pallas_call | solution.py:306
  34.2 1.5 %collective-permute-start.9 = (f32[4,896]{1,0:T(4,128)S(1)}, f32[4,896]{1,0:T(4,128)S(1)}, u32[]{:S(2)}, u32[]{:S(2)}) collective-permute-start(f32[4,896]{1,0:T(4,128)S(1)} %get-tuple-element.20), channel_id=1, source_target_pairs={{0,2},{2,0},{1,3},{3,1},{4,6},{6,4},{5,7},{7,5},{8,10},{10,8},{9,1... | collective-permute-start | bytes 43016 | tf_op jit(solution)/shard_map/ppermute | solution.py:28
  35.7 2.0 %mine.1 = f32[4,896]{1,0:T(4,128)S(1)} custom-call(bf16[4,8192]{1,0:T(4,128)(2,1)S(1)} %get-tuple-element.19.flat, bf16[8192,1792]{1,0:T(8,128)(2,1)S(1)} %bitcast.9), custom_call_target="tpu_custom_call" | custom-call | flops 2000000000 | tf_op jit(solution)/shard_map/mine/pallas_call | solution.py:325
  37.7 0.2 collective-permute-done.9
  38.0 0.6 %fusion = bf16[1,4,896]{2,1,0:T(4,128)(2,1)} fusion(f32[4,896]{1,0:T(4,128)S(1)} %mine.1, f32[4,896]{1,0:T(4,128)S(1)} %collective-permute-done.9), kind=kLoop, calls=%fused_computation.1 | loop fusion | flops 7168 | bytes 35840 | tf_op jit(solution)/shard_map/broadcast_in_dim | solution.py:396
  (7 shorter events, 0.0 us)
Async XLA Ops:
  0.0 8.3 %copy-start.1 = (bf16[1,4,64,64]{3,2,1,0:T(8,128)(2,1)S(1)}, bf16[1,4,64,64]{3,2,1,0:T(8,128)(2,1)}, u32[]{:S(2)}) copy-start(bf16[1,4,64,64]{3,2,1,0:T(8,128)(2,1)} %param.9) | copy-start | bytes 98308
  0.0 8.3 %copy-start.2 = (s32[1,4,32]{2,1,0:T(4,128)S(1)}, s32[1,4,32]{2,1,0:T(4,128)}, u32[]{:S(2)}) copy-start(s32[1,4,32]{2,1,0:T(4,128)} %param.12) | copy-start | bytes 1540
  0.0 9.0 %slice-start.7 = ((s8[4718592]{0:T(1024)(128)(4,1)}), s8[524288]{0:T(1024)(128)(4,1)S(1)}, s32[]{:S(2)}) async-start(s8[4718592]{0:T(1024)(128)(4,1)} %bitcast.10), calls=%async_computation.7 | async-start | bytes 1048576
  1.9 7.1 %collective-permute-start.2 = (bf16[256,128]{1,0:T(8,128)(2,1)S(1)}, bf16[256,128]{1,0:T(8,128)(2,1)S(1)}, u32[]{:S(2)}, u32[]{:S(2)}) collective-permute-start(bf16[256,128]{1,0:T(8,128)(2,1)S(1)} %queries.1.refs_0_), channel_id=1, source_target_pairs={{0,4},{4,0},{8,12},{12,8},{1,5},{5,1},{9,13},{13,9},{2,6},{6,2},{1... | collective-permute-start | bytes 196616 | tf_op jit(solution)/shard_map/ppermute | solution.py:28
  5.0 7.3 %collective-permute-start = (bf16[256,128]{1,0:T(8,128)(2,1)S(1)}, bf16[256,128]{1,0:T(8,128)(2,1)S(1)}, u32[]{:S(2)}, u32[]{:S(2)}) collective-permute-start(bf16[256,128]{1,0:T(8,128)(2,1)S(1)} %queries.1.refs_0_), channel_id=1, source_target_pairs={{0,8},{4,12},{8,0},{12,4},{1,9},{5,13},{9,1},{13,5},{2,10},{6,14},... | collective-permute-start | bytes 196616 | tf_op jit(solution)/shard_map/ppermute | solution.py:28
  7.6 6.1 %collective-permute-start.1 = (bf16[256,128]{1,0:T(8,128)(2,1)S(1)}, bf16[256,128]{1,0:T(8,128)(2,1)S(1)}, u32[]{:S(2)}, u32[]{:S(2)}) collective-permute-start(bf16[256,128]{1,0:T(8,128)(2,1)S(1)} %queries.1.refs_0_), channel_id=1, source_target_pairs={{0,12},{4,8},{8,4},{12,0},{1,13},{5,9},{9,5},{13,1},{2,14},{6,10},... | collective-permute-start | bytes 196616 | tf_op jit(solution)/shard_map/ppermute | solution.py:28
  8.3 2.2 %slice-start.8 = ((s8[4718592]{0:T(1024)(128)(4,1)}), s8[4194304]{0:T(1024)(128)(4,1)S(1)}, s32[]{:S(2)}) async-start(s8[4718592]{0:T(1024)(128)(4,1)} %bitcast.10), calls=%async_computation.8 | async-start | bytes 8388608
  16.3 6.3 %collective-permute-start.3 = (bf16[272,128]{1,0:T(8,128)(2,1)S(1)}, bf16[272,128]{1,0:T(8,128)(2,1)S(1)}, u32[]{:S(2)}, u32[]{:S(2)}) collective-permute-start(bf16[272,128]{1,0:T(8,128)(2,1)S(1)} %get-tuple-element.16), channel_id=1, source_target_pairs={{0,8},{4,12},{8,0},{12,4},{1,9},{5,13},{9,1},{13,5},{2,10},{6,14},... | collective-permute-start | bytes 208904 | tf_op jit(solution)/shard_map/ppermute | solution.py:28
  17.9 6.1 %collective-permute-start.4 = (bf16[272,128]{1,0:T(8,128)(2,1)S(1)}, bf16[272,128]{1,0:T(8,128)(2,1)S(1)}, u32[]{:S(2)}, u32[]{:S(2)}) collective-permute-start(bf16[272,128]{1,0:T(8,128)(2,1)S(1)} %get-tuple-element.17), channel_id=1, source_target_pairs={{0,12},{4,8},{8,4},{12,0},{1,13},{5,9},{9,5},{13,1},{2,14},{6,10},... | collective-permute-start | bytes 208904 | tf_op jit(solution)/shard_map/ppermute | solution.py:28
  18.6 5.5 %collective-permute-start.5 = (bf16[272,128]{1,0:T(8,128)(2,1)S(1)}, bf16[272,128]{1,0:T(8,128)(2,1)S(1)}, u32[]{:S(2)}, u32[]{:S(2)}) collective-permute-start(bf16[272,128]{1,0:T(8,128)(2,1)S(1)} %get-tuple-element.18), channel_id=1, source_target_pairs={{0,4},{4,0},{8,12},{12,8},{1,5},{5,1},{9,13},{13,9},{2,6},{6,2},{1... | collective-permute-start | bytes 208904 | tf_op jit(solution)/shard_map/ppermute | solution.py:28
  19.8 12.3 %slice-start = ((s8[29360128]{0:T(1024)(128)(4,1)}), s8[4194304]{0:T(1024)(128)(4,1)S(1)}, s32[]{:S(2)}) async-start(s8[29360128]{0:T(1024)(128)(4,1)} %bitcast.8), calls=%async_computation | async-start | bytes 8388608
  19.8 4.2 %copy-start = (bf16[64,128,128]{2,1,0:T(8,128)(2,1)S(1)}, bf16[64,128,128]{2,1,0:T(8,128)(2,1)}, u32[]{:S(2)}) copy-start(bf16[64,128,128]{2,1,0:T(8,128)(2,1)} %refs_4_.2) | copy-start | bytes 6291460
  19.8 12.3 %slice-start.1 = ((s8[29360128]{0:T(1024)(128)(4,1)}), s8[4194304]{0:T(1024)(128)(4,1)S(1)}, s32[]{:S(2)}) async-start(s8[29360128]{0:T(1024)(128)(4,1)} %bitcast.8), calls=%async_computation.1 | async-start | bytes 8388608
  19.8 12.3 %slice-start.2 = ((s8[29360128]{0:T(1024)(128)(4,1)}), s8[4194304]{0:T(1024)(128)(4,1)S(1)}, s32[]{:S(2)}) async-start(s8[29360128]{0:T(1024)(128)(4,1)} %bitcast.8), calls=%async_computation.2 | async-start | bytes 8388608
  19.8 12.3 %slice-start.3 = ((s8[29360128]{0:T(1024)(128)(4,1)}), s8[4194304]{0:T(1024)(128)(4,1)S(1)}, s32[]{:S(2)}) async-start(s8[29360128]{0:T(1024)(128)(4,1)} %bitcast.8), calls=%async_computation.3 | async-start | bytes 8388608
  19.8 12.3 %slice-start.4 = ((s8[29360128]{0:T(1024)(128)(4,1)}), s8[4194304]{0:T(1024)(128)(4,1)S(1)}, s32[]{:S(2)}) async-start(s8[29360128]{0:T(1024)(128)(4,1)} %bitcast.8), calls=%async_computation.4 | async-start | bytes 8388608
  19.9 12.3 %slice-start.5 = ((s8[29360128]{0:T(1024)(128)(4,1)}), s8[4194304]{0:T(1024)(128)(4,1)S(1)}, s32[]{:S(2)}) async-start(s8[29360128]{0:T(1024)(128)(4,1)} %bitcast.8), calls=%async_computation.5 | async-start | bytes 8388608
  19.9 12.3 %slice-start.6 = ((s8[29360128]{0:T(1024)(128)(4,1)}), s8[4194304]{0:T(1024)(128)(4,1)S(1)}, s32[]{:S(2)}) async-start(s8[29360128]{0:T(1024)(128)(4,1)} %bitcast.8), calls=%async_computation.6 | async-start | bytes 8388608
  24.5 6.1 %collective-permute-start.6 = (bf16[256,128]{1,0:T(8,128)(2,1)S(1)}, bf16[256,128]{1,0:T(8,128)(2,1)S(1)}, u32[]{:S(2)}, u32[]{:S(2)}) collective-permute-start(bf16[256,128]{1,0:T(8,128)(2,1)S(1)} %values.1.refs_0_), channel_id=1, source_target_pairs={{0,12},{4,8},{12,0},{8,4},{1,13},{5,9},{13,1},{9,5},{2,14},{6,10},... | collective-permute-start | bytes 196616 | tf_op jit(solution)/shard_map/ppermute | solution.py:33
  26.8 5.3 %collective-permute-start.7 = (bf16[256,128]{1,0:T(8,128)(2,1)S(1)}, bf16[256,128]{1,0:T(8,128)(2,1)S(1)}, u32[]{:S(2)}, u32[]{:S(2)}) collective-permute-start(bf16[256,128]{1,0:T(8,128)(2,1)S(1)} %values.1.refs_0_), channel_id=1, source_target_pairs={{0,4},{4,12},{12,8},{8,0},{1,5},{5,13},{13,9},{9,1},{2,6},{6,14},{... | collective-permute-start | bytes 196616 | tf_op jit(solution)/shard_map/ppermute | solution.py:33
  26.9 5.2 %collective-permute-start.8 = (bf16[256,128]{1,0:T(8,128)(2,1)S(1)}, bf16[256,128]{1,0:T(8,128)(2,1)S(1)}, u32[]{:S(2)}, u32[]{:S(2)}) collective-permute-start(bf16[256,128]{1,0:T(8,128)(2,1)S(1)} %values.1.refs_0_), channel_id=1, source_target_pairs={{0,8},{4,0},{12,4},{8,12},{1,9},{5,1},{13,5},{9,13},{2,10},{6,2},{... | collective-permute-start | bytes 196616 | tf_op jit(solution)/shard_map/ppermute | solution.py:33
  34.2 3.8 %collective-permute-start.9 = (f32[4,896]{1,0:T(4,128)S(1)}, f32[4,896]{1,0:T(4,128)S(1)}, u32[]{:S(2)}, u32[]{:S(2)}) collective-permute-start(f32[4,896]{1,0:T(4,128)S(1)} %get-tuple-element.20), channel_id=1, source_target_pairs={{0,2},{2,0},{1,3},{3,1},{4,6},{6,4},{5,7},{7,5},{8,10},{10,8},{9,1... | collective-permute-start | bytes 43016 | tf_op jit(solution)/shard_map/ppermute | solution.py:28

commit v7 on v6

--- a/solution.py
+++ b/solution.py
@@ -10,7 +10,7 @@
 BLK = 64
 PEERS = 4
 LANES = 128
-CHUNK = 512
+CHUNK = 256
 TAIL = 16
 LOG2E = 1.4426950408889634
 HIDDEN = -1e30
@@ -143,6 +143,15 @@
     return [lax.axis_index("ctx") ^ step for step in steps] if steps else [0]
 
 
+def on_ring(steps):
+    if not steps:
+        return [0]
+    me = lax.axis_index("ctx")
+    spot = me ^ (me >> 1)
+    spots = [(spot + step) & 3 for step in steps]
+    return [there ^ (there >> 1) for there in spots]
+
+
 def begin_kernel(*refs, steps):
     pieces, (rope, cache, bias, scores) = refs[:-4], refs[-4:]
     rows, width = pieces[0].shape
@@ -205,7 +214,7 @@
             lines += [part[:, at : at + LANES] for at in range(0, rows, LANES)]
     lines.append(jnp.zeros((TAIL - len(lines), LANES), jnp.float32))
     tail = jnp.concatenate(lines, axis=0).astype(jnp.bfloat16)
-    for out, place in zip(outs, slices_of(outs_of)):
+    for out, place in zip(outs, on_ring(outs_of)):
         at = pl.multiple_of(place * width, width)
         out[:rows, :] = total_sums[:, pl.ds(at, width)].astype(jnp.bfloat16)
         out[rows:, :LANES] = tail
@@ -372,7 +381,7 @@
         blocks = attend(
             [pieces[step] for step in late], late, begun, cache, latent, steps, scale
         )
-        blocks = [keep(blocks[0])] + [swap(blocks[step], "ctx", step) for step in (2, 3, 1)]
+        blocks = [keep(blocks[0])] + [turn(blocks[step], "ctx", step) for step in (1, 2, 3)]
         partial = values_of(blocks, value_absorb, drafts)
         partials = [partial] + [turn(partial, "ctx", step) for step in (2, 1, 3)]
         theirs, flat = theirs_of(partials, output_weight, drafts)

time: 38.8 us -> 38.5 us (level)
    ppermute x7 -> x4, waiting for transfers between devices: 6.33 us -> 2.18 us  [swap(): return lax.ppermute(value, axis, [(i, i ^ step) for i in range(count)])]
    ppermute x3 -> x6, starting transfers between devices: 5.23 us -> 9.09 us  [turn(): lax.ppermute(value, axis, [(order[i], order[(i + step) % 4]) for i in ran...]
    ppermute x3 -> x6, waiting for transfers between devices: 2.33 us -> 6.09 us  [turn(): lax.ppermute(value, axis, [(order[i], order[(i + step) % 4]) for i in ran...]
    ppermute x7 -> x4, starting transfers between devices: 10.8 us -> 7.22 us  [swap(): return lax.ppermute(value, axis, [(i, i ^ step) for i in range(count)])]
  transfers between devices with their start and end apart: 10 -> 10, of which waited for: 7 -> 8; matrix products, arithmetic and copies ran while one was open for 0% -> 0% of each run, Pallas kernels for 10% -> 10%
where the time goes in v7:
time: 38.5 us; the launch traced here: 38.3 us
  starting transfers between devices  16.3 us (42%)
  Pallas kernels  10.8 us (28%)
  waiting for transfers between devices  8.28 us (22%)
  local copies, waits for them, and re-layouts  1.5 us (4%)
  between operations  0.84 us (2%)
  other arithmetic  0.6 us (2%)
    ppermute x6, starting transfers between devices, turn(): lax.ppermute(value, axis, [(order[i], order[(i + step) % 4]) for i in ran...  9.09 us
    ppermute x4, starting transfers between devices, swap(): return lax.ppermute(value, axis, [(i, i ^ step) for i in range(count)])  7.22 us
    ppermute x6, waiting for transfers between devices, turn(): lax.ppermute(value, axis, [(order[i], order[(i + step) % 4]) for i in ran...  6.09 us
    pallas_call x1, Pallas kernels, attend(): pl.pallas_call(functools.partial(attend_kernel, steps=steps, outs_of=outs...  2.36 us
    ppermute x4, waiting for transfers between devices, swap(): return lax.ppermute(value, axis, [(i, i ^ step) for i in range(count)])  2.18 us
    pallas_call x1, Pallas kernels, theirs_of(): pl.pallas_call(functools.partial(theirs_kernel, drafts=drafts), out_shape...  2.04 us
    pallas_call x1, Pallas kernels, mine_of(): pl.pallas_call(mine_kernel, out_shape=jax.ShapeDtypeStruct((flat.shape[0]...  2 us
    pallas_call x1, Pallas kernels, queries_of(): pl.pallas_call(queries_kernel, out_shape=pltpu.VMEM((rows, width), jnp.bf...  1.92 us
  transfers between devices with their start and end apart: 10, of which 8 were waited for; matrix products, arithmetic and copies ran while one was open for 0% of the time, Pallas kernels for 10%

profile of v7, /device:TPU:0, one launch (start us, length us, event | category | flops | bytes accessed | tf_op | source)
XLA Modules:
  0.0 38.3 jit_solution(1624673543015833893)
XLA Ops:
  0.0 0.0 copy-start.1
  0.0 0.0 copy-start.2
  0.0 0.0 slice-start.7
  0.0 1.9 %queries.1.refs_0_ = bf16[256,128]{1,0:T(8,128)(2,1)S(1)} custom-call(bf16[4,64,128]{2,1,0:T(8,128)(2,1)} %bitcast.16, bf16[64,128,128]{2,1,0:T(8,128)(2,1)} %key_absorb.1), custom_call_target="tpu_custom_call" | custom-call | flops 5000000000 | tf_op jit(solution)/shard_map/queries/pallas_call | solution.py:84
  1.9 3.1 %collective-permute-start.2 = (bf16[256,128]{1,0:T(8,128)(2,1)S(1)}, bf16[256,128]{1,0:T(8,128)(2,1)S(1)}, u32[]{:S(2)}, u32[]{:S(2)}) collective-permute-start(bf16[256,128]{1,0:T(8,128)(2,1)S(1)} %queries.1.refs_0_), channel_id=1, source_target_pairs={{0,4},{4,0},{8,12},{12,8},{1,5},{5,1},{9,13},{13,9},{2,6},{6,2},{1... | collective-permute-start | bytes 196616 | tf_op jit(solution)/shard_map/ppermute | solution.py:28
  5.0 2.6 %collective-permute-start = (bf16[256,128]{1,0:T(8,128)(2,1)S(1)}, bf16[256,128]{1,0:T(8,128)(2,1)S(1)}, u32[]{:S(2)}, u32[]{:S(2)}) collective-permute-start(bf16[256,128]{1,0:T(8,128)(2,1)S(1)} %queries.1.refs_0_), channel_id=1, source_target_pairs={{0,8},{4,12},{8,0},{12,4},{1,9},{5,13},{9,1},{13,5},{2,10},{6,14},... | collective-permute-start | bytes 196616 | tf_op jit(solution)/shard_map/ppermute | solution.py:28
  7.6 0.0 collective-permute-start.1
  8.3 0.0 copy-done.1
  8.3 0.0 copy-done.2
  8.3 0.0 slice-start.8
  8.3 0.7 %prepare.1 = (f32[8,4096]{1,0:T(8,128)S(1)}, bf16[256,64]{1,0:T(8,128)(2,1)S(1)}) custom-call(s32[1]{0:T(128)S(6)} %copy.9.lengths, s32[4,32]{1,0:T(4,128)S(1)} %bitcast.15, bf16[4,64,64]{2,1,0:T(8,128)(2,1)S(1)} %bitcast.14), custom_call_target="tpu_custom_call" | custom-call | flops 12000000000 | tf_op jit(solution)/shard_map/prepare/pallas_call | solution.py:122
  9.0 0.0 collective-permute-done.2.refs_1_
  9.0 0.0 slice-done.7
  9.0 1.5 %slice-done.8 = s8[4194304]{0:T(1024)(128)(4,1)S(1)} async-done(((s8[4718592]{0:T(1024)(128)(4,1)}), s8[4194304]{0:T(1024)(128)(4,1)S(1)}, s32[]{:S(2)}) %slice-start.8) | async-done | bytes 4194328
  10.5 1.2 %begin.1.refs_2_ = f32[256,4096]{1,0:T(8,128)S(1)} custom-call(bf16[256,128]{1,0:T(8,128)(2,1)S(1)} %queries.1.refs_0_, bf16[256,128]{1,0:T(8,128)(2,1)S(1)} %collective-permute-done.2.refs_1_, bf16[256,64]{1,0:T(8,128)(2,1)S(1)} %get-tuple-element.13.refs_2_, bf16[576,4096]{1,0:T(8,128)(2,1)S(1)} %bitcast.12, f32[8,4096]{1,0:T(8,128)S(1)} %get-tuple-element.14.refs_4_), custom_call_target="tpu_custom_call" | custom-call | tf_op jit(solution)/shard_map/begin/pallas_call | solution.py:172
  11.7 0.6 %collective-permute-done.refs_0_ = bf16[256,128]{1,0:T(8,128)(2,1)S(1)} collective-permute-done((bf16[256,128]{1,0:T(8,128)(2,1)S(1)}, bf16[256,128]{1,0:T(8,128)(2,1)S(1)}, u32[]{:S(2)}, u32[]{:S(2)}) %collective-permute-start) | collective-permute-done | bytes 65568 | tf_op jit(solution)/shard_map/ppermute | solution.py:28
  12.3 1.4 %collective-permute-done.1.refs_1_ = bf16[256,128]{1,0:T(8,128)(2,1)S(1)} collective-permute-done((bf16[256,128]{1,0:T(8,128)(2,1)S(1)}, bf16[256,128]{1,0:T(8,128)(2,1)S(1)}, u32[]{:S(2)}, u32[]{:S(2)}) %collective-permute-start.1) | collective-permute-done | bytes 65568 | tf_op jit(solution)/shard_map/ppermute | solution.py:28
  13.7 2.4 %attend.1 = (bf16[272,128]{1,0:T(8,128)(2,1)S(1)}, bf16[272,128]{1,0:T(8,128)(2,1)S(1)}, bf16[272,128]{1,0:T(8,128)(2,1)S(1)}, bf16[272,128]{1,0:T(8,128)(2,1)S(1)}) custom-call(bf16[256,128]{1,0:T(8,128)(2,1)S(1)} %collective-permute-done.refs_0_, bf16[256,128]{1,0:T(8,128)(2,1)S(1)} %collective-permute-done.1.refs_1_, f32[256,4096]{1,0:T(8,128)S(1)} %begin.1.refs_2_, ...), custom_call_target="tpu_custom_call" | custom-call | tf_op jit(solution)/shard_map/attend/pallas_call | solution.py:225
  16.1 0.1 collective-permute-start.3
  16.1 3.0 %collective-permute-start.4 = (bf16[272,128]{1,0:T(8,128)(2,1)S(1)}, bf16[272,128]{1,0:T(8,128)(2,1)S(1)}, u32[]{:S(2)}, u32[]{:S(2)}) collective-permute-start(bf16[272,128]{1,0:T(8,128)(2,1)S(1)} %get-tuple-element.17), channel_id=1, source_target_pairs={{0,12},{4,8},{12,0},{8,4},{1,13},{5,9},{13,1},{9,5},{2,14},{6,10},... | collective-permute-start | bytes 208904 | tf_op jit(solution)/shard_map/ppermute | solution.py:33
  19.2 0.9 %collective-permute-start.5 = (bf16[272,128]{1,0:T(8,128)(2,1)S(1)}, bf16[272,128]{1,0:T(8,128)(2,1)S(1)}, u32[]{:S(2)}, u32[]{:S(2)}) collective-permute-start(bf16[272,128]{1,0:T(8,128)(2,1)S(1)} %get-tuple-element.18), channel_id=1, source_target_pairs={{0,8},{4,0},{12,4},{8,12},{1,9},{5,1},{13,5},{9,13},{2,10},{6,2},{... | collective-permute-start | bytes 208904 | tf_op jit(solution)/shard_map/ppermute | solution.py:33
  20.0 0.0 slice-start.3
  20.1 0.0 slice-start.4
  20.1 0.0 slice-start.5
  20.1 0.0 slice-start.6
  20.1 2.8 %collective-permute-done.3.refs_1_ = bf16[272,128]{1,0:T(8,128)(2,1)S(1)} collective-permute-done((bf16[272,128]{1,0:T(8,128)(2,1)S(1)}, bf16[272,128]{1,0:T(8,128)(2,1)S(1)}, u32[]{:S(2)}, u32[]{:S(2)}) %collective-permute-start.3) | collective-permute-done | bytes 69664 | tf_op jit(solution)/shard_map/ppermute | solution.py:33
  22.9 0.0 collective-permute-done.4.refs_2_
  22.9 0.7 %collective-permute-done.5.refs_3_ = bf16[272,128]{1,0:T(8,128)(2,1)S(1)} collective-permute-done((bf16[272,128]{1,0:T(8,128)(2,1)S(1)}, bf16[272,128]{1,0:T(8,128)(2,1)S(1)}, u32[]{:S(2)}, u32[]{:S(2)}) %collective-permute-start.5) | collective-permute-done | bytes 69664 | tf_op jit(solution)/shard_map/ppermute | solution.py:33
  23.6 0.0 copy-done
  23.6 0.5 %values.1.refs_0_ = bf16[256,128]{1,0:T(8,128)(2,1)S(1)} custom-call(bf16[272,128]{1,0:T(8,128)(2,1)S(1)} %keep.1.refs_0_, bf16[272,128]{1,0:T(8,128)(2,1)S(1)} %collective-permute-done.3.refs_1_, bf16[272,128]{1,0:T(8,128)(2,1)S(1)} %collective-permute-done.4.refs_2_, bf16[272,128]{1,0:T(8,128)(2,1)S(1)} %collective-permute-done.5.refs_3_, ...), custom_call_target="tpu_custom_call" | custom-call | tf_op jit(solution)/shard_map/values/pallas_call | solution.py:283
  24.1 2.2 %collective-permute-start.6 = (bf16[256,128]{1,0:T(8,128)(2,1)S(1)}, bf16[256,128]{1,0:T(8,128)(2,1)S(1)}, u32[]{:S(2)}, u32[]{:S(2)}) collective-permute-start(bf16[256,128]{1,0:T(8,128)(2,1)S(1)} %values.1.refs_0_), channel_id=1, source_target_pairs={{0,12},{4,8},{12,0},{8,4},{1,13},{5,9},{13,1},{9,5},{2,14},{6,10},... | collective-permute-start | bytes 196616 | tf_op jit(solution)/shard_map/ppermute | solution.py:33
  26.3 0.6 %collective-permute-start.7 = (bf16[256,128]{1,0:T(8,128)(2,1)S(1)}, bf16[256,128]{1,0:T(8,128)(2,1)S(1)}, u32[]{:S(2)}, u32[]{:S(2)}) collective-permute-start(bf16[256,128]{1,0:T(8,128)(2,1)S(1)} %values.1.refs_0_), channel_id=1, source_target_pairs={{0,4},{4,12},{12,8},{8,0},{1,5},{5,13},{13,9},{9,1},{2,6},{6,14},{... | collective-permute-start | bytes 196616 | tf_op jit(solution)/shard_map/ppermute | solution.py:33
  26.9 2.4 %collective-permute-start.8 = (bf16[256,128]{1,0:T(8,128)(2,1)S(1)}, bf16[256,128]{1,0:T(8,128)(2,1)S(1)}, u32[]{:S(2)}, u32[]{:S(2)}) collective-permute-start(bf16[256,128]{1,0:T(8,128)(2,1)S(1)} %values.1.refs_0_), channel_id=1, source_target_pairs={{0,8},{4,0},{12,4},{8,12},{1,9},{5,1},{13,5},{9,13},{2,10},{6,2},{... | collective-permute-start | bytes 196616 | tf_op jit(solution)/shard_map/ppermute | solution.py:33
  29.2 1.0 %collective-permute-done.6.refs_1_ = bf16[256,128]{1,0:T(8,128)(2,1)S(1)} collective-permute-done((bf16[256,128]{1,0:T(8,128)(2,1)S(1)}, bf16[256,128]{1,0:T(8,128)(2,1)S(1)}, u32[]{:S(2)}, u32[]{:S(2)}) %collective-permute-start.6) | collective-permute-done | bytes 65568 | tf_op jit(solution)/shard_map/ppermute | solution.py:33
  30.2 1.4 %collective-permute-done.7.refs_2_ = bf16[256,128]{1,0:T(8,128)(2,1)S(1)} collective-permute-done((bf16[256,128]{1,0:T(8,128)(2,1)S(1)}, bf16[256,128]{1,0:T(8,128)(2,1)S(1)}, u32[]{:S(2)}, u32[]{:S(2)}) %collective-permute-start.7) | collective-permute-done | bytes 65568 | tf_op jit(solution)/shard_map/ppermute | solution.py:33
  31.6 0.3 collective-permute-done.8.refs_3_
  31.8 0.0 slice-done
  31.8 0.0 slice-done.1
  31.8 0.0 slice-done.2
  31.8 0.0 slice-done.3
  31.8 0.0 slice-done.4
  31.9 0.0 slice-done.5
  31.9 0.0 slice-done.6
  31.9 2.0 %theirs.1 = (f32[4,896]{1,0:T(4,128)S(1)}, bf16[4,8192]{1,0:T(4,128)(2,1)S(1)}) custom-call(bf16[256,128]{1,0:T(8,128)(2,1)S(1)} %values.1.refs_0_, bf16[256,128]{1,0:T(8,128)(2,1)S(1)} %collective-permute-done.6.refs_1_, bf16[256,128]{1,0:T(8,128)(2,1)S(1)} %collective-permute-done.7.refs_2_, bf16[256,128]{1,0:T(8,128)(2,1)S(1)} %collective-permute-done.8.refs_3_, ...), custom_call_target="tpu_custom_call" | custom-call | tf_op jit(solution)/shard_map/theirs/pallas_call | solution.py:315
  33.9 1.5 %collective-permute-start.9 = (f32[4,896]{1,0:T(4,128)S(1)}, f32[4,896]{1,0:T(4,128)S(1)}, u32[]{:S(2)}, u32[]{:S(2)}) collective-permute-start(f32[4,896]{1,0:T(4,128)S(1)} %get-tuple-element.20), channel_id=1, source_target_pairs={{0,2},{2,0},{1,3},{3,1},{4,6},{6,4},{5,7},{7,5},{8,10},{10,8},{9,1... | collective-permute-start | bytes 43016 | tf_op jit(solution)/shard_map/ppermute | solution.py:28
  35.5 2.0 %mine.1 = f32[4,896]{1,0:T(4,128)S(1)} custom-call(bf16[4,8192]{1,0:T(4,128)(2,1)S(1)} %get-tuple-element.19.flat, bf16[8192,1792]{1,0:T(8,128)(2,1)S(1)} %bitcast.9), custom_call_target="tpu_custom_call" | custom-call | flops 2000000000 | tf_op jit(solution)/shard_map/mine/pallas_call | solution.py:334
  37.5 0.2 collective-permute-done.9
  37.7 0.6 %fusion = bf16[1,4,896]{2,1,0:T(4,128)(2,1)} fusion(f32[4,896]{1,0:T(4,128)S(1)} %mine.1, f32[4,896]{1,0:T(4,128)S(1)} %collective-permute-done.9), kind=kLoop, calls=%fused_computation.1 | loop fusion | flops 7168 | bytes 35840 | tf_op jit(solution)/shard_map/broadcast_in_dim | solution.py:405
  (7 shorter events, 0.0 us)
Async XLA Ops:
  0.0 8.3 %copy-start.1 = (bf16[1,4,64,64]{3,2,1,0:T(8,128)(2,1)S(1)}, bf16[1,4,64,64]{3,2,1,0:T(8,128)(2,1)}, u32[]{:S(2)}) copy-start(bf16[1,4,64,64]{3,2,1,0:T(8,128)(2,1)} %param.9) | copy-start | bytes 98308
  0.0 8.3 %copy-start.2 = (s32[1,4,32]{2,1,0:T(4,128)S(1)}, s32[1,4,32]{2,1,0:T(4,128)}, u32[]{:S(2)}) copy-start(s32[1,4,32]{2,1,0:T(4,128)} %param.12) | copy-start | bytes 1540
  0.0 9.0 %slice-start.7 = ((s8[4718592]{0:T(1024)(128)(4,1)}), s8[524288]{0:T(1024)(128)(4,1)S(1)}, s32[]{:S(2)}) async-start(s8[4718592]{0:T(1024)(128)(4,1)} %bitcast.10), calls=%async_computation.7 | async-start | bytes 1048576
  1.9 7.1 %collective-permute-start.2 = (bf16[256,128]{1,0:T(8,128)(2,1)S(1)}, bf16[256,128]{1,0:T(8,128)(2,1)S(1)}, u32[]{:S(2)}, u32[]{:S(2)}) collective-permute-start(bf16[256,128]{1,0:T(8,128)(2,1)S(1)} %queries.1.refs_0_), channel_id=1, source_target_pairs={{0,4},{4,0},{8,12},{12,8},{1,5},{5,1},{9,13},{13,9},{2,6},{6,2},{1... | collective-permute-start | bytes 196616 | tf_op jit(solution)/shard_map/ppermute | solution.py:28
  5.0 7.3 %collective-permute-start = (bf16[256,128]{1,0:T(8,128)(2,1)S(1)}, bf16[256,128]{1,0:T(8,128)(2,1)S(1)}, u32[]{:S(2)}, u32[]{:S(2)}) collective-permute-start(bf16[256,128]{1,0:T(8,128)(2,1)S(1)} %queries.1.refs_0_), channel_id=1, source_target_pairs={{0,8},{4,12},{8,0},{12,4},{1,9},{5,13},{9,1},{13,5},{2,10},{6,14},... | collective-permute-start | bytes 196616 | tf_op jit(solution)/shard_map/ppermute | solution.py:28
  7.6 6.1 %collective-permute-start.1 = (bf16[256,128]{1,0:T(8,128)(2,1)S(1)}, bf16[256,128]{1,0:T(8,128)(2,1)S(1)}, u32[]{:S(2)}, u32[]{:S(2)}) collective-permute-start(bf16[256,128]{1,0:T(8,128)(2,1)S(1)} %queries.1.refs_0_), channel_id=1, source_target_pairs={{0,12},{4,8},{8,4},{12,0},{1,13},{5,9},{9,5},{13,1},{2,14},{6,10},... | collective-permute-start | bytes 196616 | tf_op jit(solution)/shard_map/ppermute | solution.py:28
  8.3 2.2 %slice-start.8 = ((s8[4718592]{0:T(1024)(128)(4,1)}), s8[4194304]{0:T(1024)(128)(4,1)S(1)}, s32[]{:S(2)}) async-start(s8[4718592]{0:T(1024)(128)(4,1)} %bitcast.10), calls=%async_computation.8 | async-start | bytes 8388608
  16.1 6.8 %collective-permute-start.3 = (bf16[272,128]{1,0:T(8,128)(2,1)S(1)}, bf16[272,128]{1,0:T(8,128)(2,1)S(1)}, u32[]{:S(2)}, u32[]{:S(2)}) collective-permute-start(bf16[272,128]{1,0:T(8,128)(2,1)S(1)} %get-tuple-element.16), channel_id=1, source_target_pairs={{0,4},{4,12},{12,8},{8,0},{1,5},{5,13},{13,9},{9,1},{2,6},{6,14},{... | collective-permute-start | bytes 208904 | tf_op jit(solution)/shard_map/ppermute | solution.py:33
  16.1 6.7 %collective-permute-start.4 = (bf16[272,128]{1,0:T(8,128)(2,1)S(1)}, bf16[272,128]{1,0:T(8,128)(2,1)S(1)}, u32[]{:S(2)}, u32[]{:S(2)}) collective-permute-start(bf16[272,128]{1,0:T(8,128)(2,1)S(1)} %get-tuple-element.17), channel_id=1, source_target_pairs={{0,12},{4,8},{12,0},{8,4},{1,13},{5,9},{13,1},{9,5},{2,14},{6,10},... | collective-permute-start | bytes 208904 | tf_op jit(solution)/shard_map/ppermute | solution.py:33
  19.2 4.4 %collective-permute-start.5 = (bf16[272,128]{1,0:T(8,128)(2,1)S(1)}, bf16[272,128]{1,0:T(8,128)(2,1)S(1)}, u32[]{:S(2)}, u32[]{:S(2)}) collective-permute-start(bf16[272,128]{1,0:T(8,128)(2,1)S(1)} %get-tuple-element.18), channel_id=1, source_target_pairs={{0,8},{4,0},{12,4},{8,12},{1,9},{5,1},{13,5},{9,13},{2,10},{6,2},{... | collective-permute-start | bytes 208904 | tf_op jit(solution)/shard_map/ppermute | solution.py:33
  20.0 11.8 %slice-start = ((s8[29360128]{0:T(1024)(128)(4,1)}), s8[4194304]{0:T(1024)(128)(4,1)S(1)}, s32[]{:S(2)}) async-start(s8[29360128]{0:T(1024)(128)(4,1)} %bitcast.8), calls=%async_computation | async-start | bytes 8388608
  20.0 3.6 %copy-start = (bf16[64,128,128]{2,1,0:T(8,128)(2,1)S(1)}, bf16[64,128,128]{2,1,0:T(8,128)(2,1)}, u32[]{:S(2)}) copy-start(bf16[64,128,128]{2,1,0:T(8,128)(2,1)} %refs_4_.2) | copy-start | bytes 6291460
  20.0 11.8 %slice-start.1 = ((s8[29360128]{0:T(1024)(128)(4,1)}), s8[4194304]{0:T(1024)(128)(4,1)S(1)}, s32[]{:S(2)}) async-start(s8[29360128]{0:T(1024)(128)(4,1)} %bitcast.8), calls=%async_computation.1 | async-start | bytes 8388608
  20.0 11.8 %slice-start.2 = ((s8[29360128]{0:T(1024)(128)(4,1)}), s8[4194304]{0:T(1024)(128)(4,1)S(1)}, s32[]{:S(2)}) async-start(s8[29360128]{0:T(1024)(128)(4,1)} %bitcast.8), calls=%async_computation.2 | async-start | bytes 8388608
  20.0 11.8 %slice-start.3 = ((s8[29360128]{0:T(1024)(128)(4,1)}), s8[4194304]{0:T(1024)(128)(4,1)S(1)}, s32[]{:S(2)}) async-start(s8[29360128]{0:T(1024)(128)(4,1)} %bitcast.8), calls=%async_computation.3 | async-start | bytes 8388608
  20.1 11.8 %slice-start.4 = ((s8[29360128]{0:T(1024)(128)(4,1)}), s8[4194304]{0:T(1024)(128)(4,1)S(1)}, s32[]{:S(2)}) async-start(s8[29360128]{0:T(1024)(128)(4,1)} %bitcast.8), calls=%async_computation.4 | async-start | bytes 8388608
  20.1 11.8 %slice-start.5 = ((s8[29360128]{0:T(1024)(128)(4,1)}), s8[4194304]{0:T(1024)(128)(4,1)S(1)}, s32[]{:S(2)}) async-start(s8[29360128]{0:T(1024)(128)(4,1)} %bitcast.8), calls=%async_computation.5 | async-start | bytes 8388608
  20.1 11.8 %slice-start.6 = ((s8[29360128]{0:T(1024)(128)(4,1)}), s8[4194304]{0:T(1024)(128)(4,1)S(1)}, s32[]{:S(2)}) async-start(s8[29360128]{0:T(1024)(128)(4,1)} %bitcast.8), calls=%async_computation.6 | async-start | bytes 8388608
  24.1 6.1 %collective-permute-start.6 = (bf16[256,128]{1,0:T(8,128)(2,1)S(1)}, bf16[256,128]{1,0:T(8,128)(2,1)S(1)}, u32[]{:S(2)}, u32[]{:S(2)}) collective-permute-start(bf16[256,128]{1,0:T(8,128)(2,1)S(1)} %values.1.refs_0_), channel_id=1, source_target_pairs={{0,12},{4,8},{12,0},{8,4},{1,13},{5,9},{13,1},{9,5},{2,14},{6,10},... | collective-permute-start | bytes 196616 | tf_op jit(solution)/shard_map/ppermute | solution.py:33
  26.3 5.3 %collective-permute-start.7 = (bf16[256,128]{1,0:T(8,128)(2,1)S(1)}, bf16[256,128]{1,0:T(8,128)(2,1)S(1)}, u32[]{:S(2)}, u32[]{:S(2)}) collective-permute-start(bf16[256,128]{1,0:T(8,128)(2,1)S(1)} %values.1.refs_0_), channel_id=1, source_target_pairs={{0,4},{4,12},{12,8},{8,0},{1,5},{5,13},{13,9},{9,1},{2,6},{6,14},{... | collective-permute-start | bytes 196616 | tf_op jit(solution)/shard_map/ppermute | solution.py:33
  26.9 5.0 %collective-permute-start.8 = (bf16[256,128]{1,0:T(8,128)(2,1)S(1)}, bf16[256,128]{1,0:T(8,128)(2,1)S(1)}, u32[]{:S(2)}, u32[]{:S(2)}) collective-permute-start(bf16[256,128]{1,0:T(8,128)(2,1)S(1)} %values.1.refs_0_), channel_id=1, source_target_pairs={{0,8},{4,0},{12,4},{8,12},{1,9},{5,1},{13,5},{9,13},{2,10},{6,2},{... | collective-permute-start | bytes 196616 | tf_op jit(solution)/shard_map/ppermute | solution.py:33
  33.9 3.8 %collective-permute-start.9 = (f32[4,896]{1,0:T(4,128)S(1)}, f32[4,896]{1,0:T(4,128)S(1)}, u32[]{:S(2)}, u32[]{:S(2)}) collective-permute-start(f32[4,896]{1,0:T(4,128)S(1)} %get-tuple-element.20), channel_id=1, source_target_pairs={{0,2},{2,0},{1,3},{3,1},{4,6},{6,4},{5,7},{7,5},{8,10},{10,8},{9,1... | collective-permute-start | bytes 43016 | tf_op jit(solution)/shard_map/ppermute | solution.py:28

commit v8 on v7

--- a/solution.py
+++ b/solution.py
@@ -184,13 +184,17 @@
     outs, total_sums = refs[len(steps) + 2 : -1], refs[-1]
     rows, latent = total_sums.shape
     width = latent // len(outs)
-    scores = begun[...]
-    if steps:
-        scores += jnp.dot(
-            jnp.concatenate([piece[...] for piece in pieces], axis=1),
-            rows_at(cache, slices_of(steps), width),
-            preferred_element_type=jnp.float32,
-        )
+    left = jnp.concatenate([piece[...] for piece in pieces], axis=1) if steps else None
+    right = rows_at(cache, slices_of(steps), width) if steps else None
+    found = []
+    for first in range(0, begun.shape[1], 1024):
+        part = begun[:, first : first + 1024]
+        if steps:
+            part += jnp.dot(
+                left, right[:, first : first + 1024], preferred_element_type=jnp.float32
+            )
+        found.append(part)
+    scores = jnp.concatenate(found, axis=1)
     top = jnp.max(scores, axis=1, keepdims=True)
     tokens = scores.shape[1]
     total = jnp.zeros((rows, 1), jnp.float32)

time: 38.5 us -> 38.5 us (level)
  no operation moved by 1% of the time
where the time goes in v8:
time: 38.5 us; the launch traced here: 38.3 us
  starting transfers between devices  16.3 us (42%)
  Pallas kernels  10.8 us (28%)
  waiting for transfers between devices  8.28 us (22%)
  local copies, waits for them, and re-layouts  1.5 us (4%)
  between operations  0.84 us (2%)
  other arithmetic  0.6 us (2%)
    ppermute x6, starting transfers between devices, turn(): lax.ppermute(value, axis, [(order[i], order[(i + step) % 4]) for i in ran...  9.09 us
    ppermute x4, starting transfers between devices, swap(): return lax.ppermute(value, axis, [(i, i ^ step) for i in range(count)])  7.22 us
    ppermute x6, waiting for transfers between devices, turn(): lax.ppermute(value, axis, [(order[i], order[(i + step) % 4]) for i in ran...  6.09 us
    pallas_call x1, Pallas kernels, attend(): pl.pallas_call(functools.partial(attend_kernel, steps=steps, outs_of=outs...  2.36 us
    ppermute x4, waiting for transfers between devices, swap(): return lax.ppermute(value, axis, [(i, i ^ step) for i in range(count)])  2.18 us
    pallas_call x1, Pallas kernels, theirs_of(): pl.pallas_call(functools.partial(theirs_kernel, drafts=drafts), out_shape...  2.04 us
    pallas_call x1, Pallas kernels, mine_of(): pl.pallas_call(mine_kernel, out_shape=jax.ShapeDtypeStruct((flat.shape[0]...  2 us
    pallas_call x1, Pallas kernels, queries_of(): pl.pallas_call(queries_kernel, out_shape=pltpu.VMEM((rows, width), jnp.bf...  1.92 us
  transfers between devices with their start and end apart: 10, of which 8 were waited for; matrix products, arithmetic and copies ran while one was open for 0% of the time, Pallas kernels for 10%

profile of v8, /device:TPU:0, one launch (start us, length us, event | category | flops | bytes accessed | tf_op | source)
XLA Modules:
  0.0 38.3 jit_solution(1624673543015833893)
XLA Ops:
  0.0 0.0 copy-start.1
  0.0 0.0 copy-start.2
  0.0 0.0 slice-start.7
  0.0 1.9 %queries.1.refs_0_ = bf16[256,128]{1,0:T(8,128)(2,1)S(1)} custom-call(bf16[4,64,128]{2,1,0:T(8,128)(2,1)} %bitcast.16, bf16[64,128,128]{2,1,0:T(8,128)(2,1)} %key_absorb.1), custom_call_target="tpu_custom_call" | custom-call | flops 5000000000 | tf_op jit(solution)/shard_map/queries/pallas_call | solution.py:84
  1.9 3.1 %collective-permute-start.2 = (bf16[256,128]{1,0:T(8,128)(2,1)S(1)}, bf16[256,128]{1,0:T(8,128)(2,1)S(1)}, u32[]{:S(2)}, u32[]{:S(2)}) collective-permute-start(bf16[256,128]{1,0:T(8,128)(2,1)S(1)} %queries.1.refs_0_), channel_id=1, source_target_pairs={{0,4},{4,0},{8,12},{12,8},{1,5},{5,1},{9,13},{13,9},{2,6},{6,2},{1... | collective-permute-start | bytes 196616 | tf_op jit(solution)/shard_map/ppermute | solution.py:28
  5.0 2.6 %collective-permute-start = (bf16[256,128]{1,0:T(8,128)(2,1)S(1)}, bf16[256,128]{1,0:T(8,128)(2,1)S(1)}, u32[]{:S(2)}, u32[]{:S(2)}) collective-permute-start(bf16[256,128]{1,0:T(8,128)(2,1)S(1)} %queries.1.refs_0_), channel_id=1, source_target_pairs={{0,8},{4,12},{8,0},{12,4},{1,9},{5,13},{9,1},{13,5},{2,10},{6,14},... | collective-permute-start | bytes 196616 | tf_op jit(solution)/shard_map/ppermute | solution.py:28
  7.6 0.0 collective-permute-start.1
  8.3 0.0 copy-done.1
  8.3 0.0 copy-done.2
  8.3 0.0 slice-start.8
  8.3 0.7 %prepare.1 = (f32[8,4096]{1,0:T(8,128)S(1)}, bf16[256,64]{1,0:T(8,128)(2,1)S(1)}) custom-call(s32[1]{0:T(128)S(6)} %copy.9.lengths, s32[4,32]{1,0:T(4,128)S(1)} %bitcast.15, bf16[4,64,64]{2,1,0:T(8,128)(2,1)S(1)} %bitcast.14), custom_call_target="tpu_custom_call" | custom-call | flops 12000000000 | tf_op jit(solution)/shard_map/prepare/pallas_call | solution.py:122
  9.0 0.0 collective-permute-done.2.refs_1_
  9.0 0.0 slice-done.7
  9.0 1.5 %slice-done.8 = s8[4194304]{0:T(1024)(128)(4,1)S(1)} async-done(((s8[4718592]{0:T(1024)(128)(4,1)}), s8[4194304]{0:T(1024)(128)(4,1)S(1)}, s32[]{:S(2)}) %slice-start.8) | async-done | bytes 4194328
  10.5 1.2 %begin.1.refs_2_ = f32[256,4096]{1,0:T(8,128)S(1)} custom-call(bf16[256,128]{1,0:T(8,128)(2,1)S(1)} %queries.1.refs_0_, bf16[256,128]{1,0:T(8,128)(2,1)S(1)} %collective-permute-done.2.refs_1_, bf16[256,64]{1,0:T(8,128)(2,1)S(1)} %get-tuple-element.13.refs_2_, bf16[576,4096]{1,0:T(8,128)(2,1)S(1)} %bitcast.12, f32[8,4096]{1,0:T(8,128)S(1)} %get-tuple-element.14.refs_4_), custom_call_target="tpu_custom_call" | custom-call | tf_op jit(solution)/shard_map/begin/pallas_call | solution.py:172
  11.7 0.6 %collective-permute-done.refs_0_ = bf16[256,128]{1,0:T(8,128)(2,1)S(1)} collective-permute-done((bf16[256,128]{1,0:T(8,128)(2,1)S(1)}, bf16[256,128]{1,0:T(8,128)(2,1)S(1)}, u32[]{:S(2)}, u32[]{:S(2)}) %collective-permute-start) | collective-permute-done | bytes 65568 | tf_op jit(solution)/shard_map/ppermute | solution.py:28
  12.3 1.4 %collective-permute-done.1.refs_1_ = bf16[256,128]{1,0:T(8,128)(2,1)S(1)} collective-permute-done((bf16[256,128]{1,0:T(8,128)(2,1)S(1)}, bf16[256,128]{1,0:T(8,128)(2,1)S(1)}, u32[]{:S(2)}, u32[]{:S(2)}) %collective-permute-start.1) | collective-permute-done | bytes 65568 | tf_op jit(solution)/shard_map/ppermute | solution.py:28
  13.7 2.4 %attend.1 = (bf16[272,128]{1,0:T(8,128)(2,1)S(1)}, bf16[272,128]{1,0:T(8,128)(2,1)S(1)}, bf16[272,128]{1,0:T(8,128)(2,1)S(1)}, bf16[272,128]{1,0:T(8,128)(2,1)S(1)}) custom-call(bf16[256,128]{1,0:T(8,128)(2,1)S(1)} %collective-permute-done.refs_0_, bf16[256,128]{1,0:T(8,128)(2,1)S(1)} %collective-permute-done.1.refs_1_, f32[256,4096]{1,0:T(8,128)S(1)} %begin.1.refs_2_, ...), custom_call_target="tpu_custom_call" | custom-call | tf_op jit(solution)/shard_map/attend/pallas_call | solution.py:229
  16.1 0.1 collective-permute-start.3
  16.1 3.0 %collective-permute-start.4 = (bf16[272,128]{1,0:T(8,128)(2,1)S(1)}, bf16[272,128]{1,0:T(8,128)(2,1)S(1)}, u32[]{:S(2)}, u32[]{:S(2)}) collective-permute-start(bf16[272,128]{1,0:T(8,128)(2,1)S(1)} %get-tuple-element.17), channel_id=1, source_target_pairs={{0,12},{4,8},{12,0},{8,4},{1,13},{5,9},{13,1},{9,5},{2,14},{6,10},... | collective-permute-start | bytes 208904 | tf_op jit(solution)/shard_map/ppermute | solution.py:33
  19.2 0.9 %collective-permute-start.5 = (bf16[272,128]{1,0:T(8,128)(2,1)S(1)}, bf16[272,128]{1,0:T(8,128)(2,1)S(1)}, u32[]{:S(2)}, u32[]{:S(2)}) collective-permute-start(bf16[272,128]{1,0:T(8,128)(2,1)S(1)} %get-tuple-element.18), channel_id=1, source_target_pairs={{0,8},{4,0},{12,4},{8,12},{1,9},{5,1},{13,5},{9,13},{2,10},{6,2},{... | collective-permute-start | bytes 208904 | tf_op jit(solution)/shard_map/ppermute | solution.py:33
  20.0 0.0 slice-start.3
  20.1 0.0 slice-start.4
  20.1 0.0 slice-start.5
  20.1 0.0 slice-start.6
  20.1 2.8 %collective-permute-done.3.refs_1_ = bf16[272,128]{1,0:T(8,128)(2,1)S(1)} collective-permute-done((bf16[272,128]{1,0:T(8,128)(2,1)S(1)}, bf16[272,128]{1,0:T(8,128)(2,1)S(1)}, u32[]{:S(2)}, u32[]{:S(2)}) %collective-permute-start.3) | collective-permute-done | bytes 69664 | tf_op jit(solution)/shard_map/ppermute | solution.py:33
  22.9 0.0 collective-permute-done.4.refs_2_
  22.9 0.7 %collective-permute-done.5.refs_3_ = bf16[272,128]{1,0:T(8,128)(2,1)S(1)} collective-permute-done((bf16[272,128]{1,0:T(8,128)(2,1)S(1)}, bf16[272,128]{1,0:T(8,128)(2,1)S(1)}, u32[]{:S(2)}, u32[]{:S(2)}) %collective-permute-start.5) | collective-permute-done | bytes 69664 | tf_op jit(solution)/shard_map/ppermute | solution.py:33
  23.6 0.0 copy-done
  23.6 0.5 %values.1.refs_0_ = bf16[256,128]{1,0:T(8,128)(2,1)S(1)} custom-call(bf16[272,128]{1,0:T(8,128)(2,1)S(1)} %keep.1.refs_0_, bf16[272,128]{1,0:T(8,128)(2,1)S(1)} %collective-permute-done.3.refs_1_, bf16[272,128]{1,0:T(8,128)(2,1)S(1)} %collective-permute-done.4.refs_2_, bf16[272,128]{1,0:T(8,128)(2,1)S(1)} %collective-permute-done.5.refs_3_, ...), custom_call_target="tpu_custom_call" | custom-call | tf_op jit(solution)/shard_map/values/pallas_call | solution.py:287
  24.1 2.2 %collective-permute-start.6 = (bf16[256,128]{1,0:T(8,128)(2,1)S(1)}, bf16[256,128]{1,0:T(8,128)(2,1)S(1)}, u32[]{:S(2)}, u32[]{:S(2)}) collective-permute-start(bf16[256,128]{1,0:T(8,128)(2,1)S(1)} %values.1.refs_0_), channel_id=1, source_target_pairs={{0,12},{4,8},{12,0},{8,4},{1,13},{5,9},{13,1},{9,5},{2,14},{6,10},... | collective-permute-start | bytes 196616 | tf_op jit(solution)/shard_map/ppermute | solution.py:33
  26.3 0.6 %collective-permute-start.7 = (bf16[256,128]{1,0:T(8,128)(2,1)S(1)}, bf16[256,128]{1,0:T(8,128)(2,1)S(1)}, u32[]{:S(2)}, u32[]{:S(2)}) collective-permute-start(bf16[256,128]{1,0:T(8,128)(2,1)S(1)} %values.1.refs_0_), channel_id=1, source_target_pairs={{0,4},{4,12},{12,8},{8,0},{1,5},{5,13},{13,9},{9,1},{2,6},{6,14},{... | collective-permute-start | bytes 196616 | tf_op jit(solution)/shard_map/ppermute | solution.py:33
  26.9 2.4 %collective-permute-start.8 = (bf16[256,128]{1,0:T(8,128)(2,1)S(1)}, bf16[256,128]{1,0:T(8,128)(2,1)S(1)}, u32[]{:S(2)}, u32[]{:S(2)}) collective-permute-start(bf16[256,128]{1,0:T(8,128)(2,1)S(1)} %values.1.refs_0_), channel_id=1, source_target_pairs={{0,8},{4,0},{12,4},{8,12},{1,9},{5,1},{13,5},{9,13},{2,10},{6,2},{... | collective-permute-start | bytes 196616 | tf_op jit(solution)/shard_map/ppermute | solution.py:33
  29.2 1.0 %collective-permute-done.6.refs_1_ = bf16[256,128]{1,0:T(8,128)(2,1)S(1)} collective-permute-done((bf16[256,128]{1,0:T(8,128)(2,1)S(1)}, bf16[256,128]{1,0:T(8,128)(2,1)S(1)}, u32[]{:S(2)}, u32[]{:S(2)}) %collective-permute-start.6) | collective-permute-done | bytes 65568 | tf_op jit(solution)/shard_map/ppermute | solution.py:33
  30.2 1.4 %collective-permute-done.7.refs_2_ = bf16[256,128]{1,0:T(8,128)(2,1)S(1)} collective-permute-done((bf16[256,128]{1,0:T(8,128)(2,1)S(1)}, bf16[256,128]{1,0:T(8,128)(2,1)S(1)}, u32[]{:S(2)}, u32[]{:S(2)}) %collective-permute-start.7) | collective-permute-done | bytes 65568 | tf_op jit(solution)/shard_map/ppermute | solution.py:33
  31.6 0.3 collective-permute-done.8.refs_3_
  31.8 0.0 slice-done
  31.8 0.0 slice-done.1
  31.8 0.0 slice-done.2
  31.8 0.0 slice-done.3
  31.8 0.0 slice-done.4
  31.9 0.0 slice-done.5
  31.9 0.0 slice-done.6
  31.9 2.0 %theirs.1 = (f32[4,896]{1,0:T(4,128)S(1)}, bf16[4,8192]{1,0:T(4,128)(2,1)S(1)}) custom-call(bf16[256,128]{1,0:T(8,128)(2,1)S(1)} %values.1.refs_0_, bf16[256,128]{1,0:T(8,128)(2,1)S(1)} %collective-permute-done.6.refs_1_, bf16[256,128]{1,0:T(8,128)(2,1)S(1)} %collective-permute-done.7.refs_2_, bf16[256,128]{1,0:T(8,128)(2,1)S(1)} %collective-permute-done.8.refs_3_, ...), custom_call_target="tpu_custom_call" | custom-call | tf_op jit(solution)/shard_map/theirs/pallas_call | solution.py:319
  33.9 1.5 %collective-permute-start.9 = (f32[4,896]{1,0:T(4,128)S(1)}, f32[4,896]{1,0:T(4,128)S(1)}, u32[]{:S(2)}, u32[]{:S(2)}) collective-permute-start(f32[4,896]{1,0:T(4,128)S(1)} %get-tuple-element.20), channel_id=1, source_target_pairs={{0,2},{2,0},{1,3},{3,1},{4,6},{6,4},{5,7},{7,5},{8,10},{10,8},{9,1... | collective-permute-start | bytes 43016 | tf_op jit(solution)/shard_map/ppermute | solution.py:28
  35.5 2.0 %mine.1 = f32[4,896]{1,0:T(4,128)S(1)} custom-call(bf16[4,8192]{1,0:T(4,128)(2,1)S(1)} %get-tuple-element.19.flat, bf16[8192,1792]{1,0:T(8,128)(2,1)S(1)} %bitcast.9), custom_call_target="tpu_custom_call" | custom-call | flops 2000000000 | tf_op jit(solution)/shard_map/mine/pallas_call | solution.py:338
  37.5 0.2 collective-permute-done.9
  37.7 0.6 %fusion = bf16[1,4,896]{2,1,0:T(4,128)(2,1)} fusion(f32[4,896]{1,0:T(4,128)S(1)} %mine.1, f32[4,896]{1,0:T(4,128)S(1)} %collective-permute-done.9), kind=kLoop, calls=%fused_computation.1 | loop fusion | flops 7168 | bytes 35840 | tf_op jit(solution)/shard_map/broadcast_in_dim | solution.py:409
  (7 shorter events, 0.0 us)
Async XLA Ops:
  0.0 8.3 %copy-start.1 = (bf16[1,4,64,64]{3,2,1,0:T(8,128)(2,1)S(1)}, bf16[1,4,64,64]{3,2,1,0:T(8,128)(2,1)}, u32[]{:S(2)}) copy-start(bf16[1,4,64,64]{3,2,1,0:T(8,128)(2,1)} %param.9) | copy-start | bytes 98308
  0.0 8.3 %copy-start.2 = (s32[1,4,32]{2,1,0:T(4,128)S(1)}, s32[1,4,32]{2,1,0:T(4,128)}, u32[]{:S(2)}) copy-start(s32[1,4,32]{2,1,0:T(4,128)} %param.12) | copy-start | bytes 1540
  0.0 9.0 %slice-start.7 = ((s8[4718592]{0:T(1024)(128)(4,1)}), s8[524288]{0:T(1024)(128)(4,1)S(1)}, s32[]{:S(2)}) async-start(s8[4718592]{0:T(1024)(128)(4,1)} %bitcast.10), calls=%async_computation.7 | async-start | bytes 1048576
  1.9 7.1 %collective-permute-start.2 = (bf16[256,128]{1,0:T(8,128)(2,1)S(1)}, bf16[256,128]{1,0:T(8,128)(2,1)S(1)}, u32[]{:S(2)}, u32[]{:S(2)}) collective-permute-start(bf16[256,128]{1,0:T(8,128)(2,1)S(1)} %queries.1.refs_0_), channel_id=1, source_target_pairs={{0,4},{4,0},{8,12},{12,8},{1,5},{5,1},{9,13},{13,9},{2,6},{6,2},{1... | collective-permute-start | bytes 196616 | tf_op jit(solution)/shard_map/ppermute | solution.py:28
  5.0 7.3 %collective-permute-start = (bf16[256,128]{1,0:T(8,128)(2,1)S(1)}, bf16[256,128]{1,0:T(8,128)(2,1)S(1)}, u32[]{:S(2)}, u32[]{:S(2)}) collective-permute-start(bf16[256,128]{1,0:T(8,128)(2,1)S(1)} %queries.1.refs_0_), channel_id=1, source_target_pairs={{0,8},{4,12},{8,0},{12,4},{1,9},{5,13},{9,1},{13,5},{2,10},{6,14},... | collective-permute-start | bytes 196616 | tf_op jit(solution)/shard_map/ppermute | solution.py:28
  7.6 6.1 %collective-permute-start.1 = (bf16[256,128]{1,0:T(8,128)(2,1)S(1)}, bf16[256,128]{1,0:T(8,128)(2,1)S(1)}, u32[]{:S(2)}, u32[]{:S(2)}) collective-permute-start(bf16[256,128]{1,0:T(8,128)(2,1)S(1)} %queries.1.refs_0_), channel_id=1, source_target_pairs={{0,12},{4,8},{8,4},{12,0},{1,13},{5,9},{9,5},{13,1},{2,14},{6,10},... | collective-permute-start | bytes 196616 | tf_op jit(solution)/shard_map/ppermute | solution.py:28
  8.3 2.2 %slice-start.8 = ((s8[4718592]{0:T(1024)(128)(4,1)}), s8[4194304]{0:T(1024)(128)(4,1)S(1)}, s32[]{:S(2)}) async-start(s8[4718592]{0:T(1024)(128)(4,1)} %bitcast.10), calls=%async_computation.8 | async-start | bytes 8388608
  16.1 6.8 %collective-permute-start.3 = (bf16[272,128]{1,0:T(8,128)(2,1)S(1)}, bf16[272,128]{1,0:T(8,128)(2,1)S(1)}, u32[]{:S(2)}, u32[]{:S(2)}) collective-permute-start(bf16[272,128]{1,0:T(8,128)(2,1)S(1)} %get-tuple-element.16), channel_id=1, source_target_pairs={{0,4},{4,12},{12,8},{8,0},{1,5},{5,13},{13,9},{9,1},{2,6},{6,14},{... | collective-permute-start | bytes 208904 | tf_op jit(solution)/shard_map/ppermute | solution.py:33
  16.1 6.7 %collective-permute-start.4 = (bf16[272,128]{1,0:T(8,128)(2,1)S(1)}, bf16[272,128]{1,0:T(8,128)(2,1)S(1)}, u32[]{:S(2)}, u32[]{:S(2)}) collective-permute-start(bf16[272,128]{1,0:T(8,128)(2,1)S(1)} %get-tuple-element.17), channel_id=1, source_target_pairs={{0,12},{4,8},{12,0},{8,4},{1,13},{5,9},{13,1},{9,5},{2,14},{6,10},... | collective-permute-start | bytes 208904 | tf_op jit(solution)/shard_map/ppermute | solution.py:33
  19.2 4.4 %collective-permute-start.5 = (bf16[272,128]{1,0:T(8,128)(2,1)S(1)}, bf16[272,128]{1,0:T(8,128)(2,1)S(1)}, u32[]{:S(2)}, u32[]{:S(2)}) collective-permute-start(bf16[272,128]{1,0:T(8,128)(2,1)S(1)} %get-tuple-element.18), channel_id=1, source_target_pairs={{0,8},{4,0},{12,4},{8,12},{1,9},{5,1},{13,5},{9,13},{2,10},{6,2},{... | collective-permute-start | bytes 208904 | tf_op jit(solution)/shard_map/ppermute | solution.py:33
  20.0 11.8 %slice-start = ((s8[29360128]{0:T(1024)(128)(4,1)}), s8[4194304]{0:T(1024)(128)(4,1)S(1)}, s32[]{:S(2)}) async-start(s8[29360128]{0:T(1024)(128)(4,1)} %bitcast.8), calls=%async_computation | async-start | bytes 8388608
  20.0 3.6 %copy-start = (bf16[64,128,128]{2,1,0:T(8,128)(2,1)S(1)}, bf16[64,128,128]{2,1,0:T(8,128)(2,1)}, u32[]{:S(2)}) copy-start(bf16[64,128,128]{2,1,0:T(8,128)(2,1)} %refs_4_.2) | copy-start | bytes 6291460
  20.0 11.8 %slice-start.1 = ((s8[29360128]{0:T(1024)(128)(4,1)}), s8[4194304]{0:T(1024)(128)(4,1)S(1)}, s32[]{:S(2)}) async-start(s8[29360128]{0:T(1024)(128)(4,1)} %bitcast.8), calls=%async_computation.1 | async-start | bytes 8388608
  20.0 11.8 %slice-start.2 = ((s8[29360128]{0:T(1024)(128)(4,1)}), s8[4194304]{0:T(1024)(128)(4,1)S(1)}, s32[]{:S(2)}) async-start(s8[29360128]{0:T(1024)(128)(4,1)} %bitcast.8), calls=%async_computation.2 | async-start | bytes 8388608
  20.0 11.8 %slice-start.3 = ((s8[29360128]{0:T(1024)(128)(4,1)}), s8[4194304]{0:T(1024)(128)(4,1)S(1)}, s32[]{:S(2)}) async-start(s8[29360128]{0:T(1024)(128)(4,1)} %bitcast.8), calls=%async_computation.3 | async-start | bytes 8388608
  20.1 11.8 %slice-start.4 = ((s8[29360128]{0:T(1024)(128)(4,1)}), s8[4194304]{0:T(1024)(128)(4,1)S(1)}, s32[]{:S(2)}) async-start(s8[29360128]{0:T(1024)(128)(4,1)} %bitcast.8), calls=%async_computation.4 | async-start | bytes 8388608
  20.1 11.8 %slice-start.5 = ((s8[29360128]{0:T(1024)(128)(4,1)}), s8[4194304]{0:T(1024)(128)(4,1)S(1)}, s32[]{:S(2)}) async-start(s8[29360128]{0:T(1024)(128)(4,1)} %bitcast.8), calls=%async_computation.5 | async-start | bytes 8388608
  20.1 11.8 %slice-start.6 = ((s8[29360128]{0:T(1024)(128)(4,1)}), s8[4194304]{0:T(1024)(128)(4,1)S(1)}, s32[]{:S(2)}) async-start(s8[29360128]{0:T(1024)(128)(4,1)} %bitcast.8), calls=%async_computation.6 | async-start | bytes 8388608
  24.1 6.1 %collective-permute-start.6 = (bf16[256,128]{1,0:T(8,128)(2,1)S(1)}, bf16[256,128]{1,0:T(8,128)(2,1)S(1)}, u32[]{:S(2)}, u32[]{:S(2)}) collective-permute-start(bf16[256,128]{1,0:T(8,128)(2,1)S(1)} %values.1.refs_0_), channel_id=1, source_target_pairs={{0,12},{4,8},{12,0},{8,4},{1,13},{5,9},{13,1},{9,5},{2,14},{6,10},... | collective-permute-start | bytes 196616 | tf_op jit(solution)/shard_map/ppermute | solution.py:33
  26.3 5.3 %collective-permute-start.7 = (bf16[256,128]{1,0:T(8,128)(2,1)S(1)}, bf16[256,128]{1,0:T(8,128)(2,1)S(1)}, u32[]{:S(2)}, u32[]{:S(2)}) collective-permute-start(bf16[256,128]{1,0:T(8,128)(2,1)S(1)} %values.1.refs_0_), channel_id=1, source_target_pairs={{0,4},{4,12},{12,8},{8,0},{1,5},{5,13},{13,9},{9,1},{2,6},{6,14},{... | collective-permute-start | bytes 196616 | tf_op jit(solution)/shard_map/ppermute | solution.py:33
  26.9 5.0 %collective-permute-start.8 = (bf16[256,128]{1,0:T(8,128)(2,1)S(1)}, bf16[256,128]{1,0:T(8,128)(2,1)S(1)}, u32[]{:S(2)}, u32[]{:S(2)}) collective-permute-start(bf16[256,128]{1,0:T(8,128)(2,1)S(1)} %values.1.refs_0_), channel_id=1, source_target_pairs={{0,8},{4,0},{12,4},{8,12},{1,9},{5,1},{13,5},{9,13},{2,10},{6,2},{... | collective-permute-start | bytes 196616 | tf_op jit(solution)/shard_map/ppermute | solution.py:33
  33.9 3.8 %collective-permute-start.9 = (f32[4,896]{1,0:T(4,128)S(1)}, f32[4,896]{1,0:T(4,128)S(1)}, u32[]{:S(2)}, u32[]{:S(2)}) collective-permute-start(f32[4,896]{1,0:T(4,128)S(1)} %get-tuple-element.20), channel_id=1, source_target_pairs={{0,2},{2,0},{1,3},{3,1},{4,6},{6,4},{5,7},{7,5},{8,10},{10,8},{9,1... | collective-permute-start | bytes 43016 | tf_op jit(solution)/shard_map/ppermute | solution.py:28
